TPU v7x, 256 devices: a whole 4x4x8 slice. The times are simulated.
256 devices in a mesh: row: 16 (over x, y_hi, core), col: 16 (over y_lo, z).
Axes of the slice: x: 4, y: 4 (y_hi: 2, y_lo: 2; y = y_hi * 2 + y_lo), z: 8, core: 2. Of those that a mesh axis runs over, the one named last changes fastest.
Arguments:
- embeddings: bfloat16 [196608, 512], P(('row', 'col')), may hold values from -40 to 40
- positives: int32 [196608], P(('row', 'col')), may hold values from 0 to 767, as said below
Outputs:
- gradient: float32 [196608, 512], P(('row', 'col'))
Inputs may be any that keep to these rules, and one draw needn't show every extreme that they name: Within each block of 768 rows the rows are paired off: positives[k] names the position of k's partner in k's block, the partner's partner is k, and no row is its own partner.
All inputs are finite; a program needn't handle non-finite values.
Results may differ from a plain program's by a relative error of at most 0.0051.
Values may be sent and summed in bfloat16 or wider, within the bound.
No kernel may reach another device: no remote copies, remote signals or barrier semaphores. Data moves between devices by JAX's collectives and lax.ppermute only.
A program may use at most 64 MiB of HBM per device.

v0:
```python
import jax
import jax.numpy as jnp
from jax import lax
from jax.sharding import PartitionSpec as P

inverse_temp = 5.0
epsilon = 1e-06


def passed_along(block, axis, distance):
    devices = range(lax.axis_size(axis))
    route = [((i - distance) % len(devices), i) for i in devices]
    return lax.ppermute(block, axis, route)


def exp_tile(mine, theirs):
    scores = lax.dot_general(
        mine, theirs, (((1,), (1,)), ((), ())), preferred_element_type=jnp.float32
    )
    return jnp.exp(scores * inverse_temp)


def on_device(embeddings, positives):
    row_count = embeddings.shape[0]
    wide = embeddings.astype(jnp.float32)
    normed = (wide * lax.rsqrt(jnp.sum(wide * wide, axis=-1, keepdims=True) + epsilon)).astype(
        jnp.bfloat16
    )
    col_count = lax.axis_size("col")
    total = lax.axis_size("row") * col_count
    offsets = [1, col_count, col_count + 1, total // 4]
    diagonal = jnp.arange(row_count)[:, None] == jnp.arange(row_count)[None, :]
    self_tile = jnp.where(diagonal, jnp.float32(0.0), exp_tile(normed, normed))
    denoms = jnp.sum(self_tile, axis=1)
    below_blocks = []
    below_tiles = []
    above_blocks = []
    above_tiles = []
    for offset in offsets:
        below = passed_along(normed, ("row", "col"), offset)
        tile_below = exp_tile(normed, below)
        denoms = denoms + jnp.sum(tile_below, axis=1)
        below_blocks.append(below)
        below_tiles.append(tile_below)
        above = passed_along(normed, ("row", "col"), -offset)
        tile_above = exp_tile(normed, above)
        denoms = denoms + jnp.sum(tile_above, axis=1)
        above_blocks.append(above)
        above_tiles.append(tile_above)
    below_norms = [passed_along(denoms, ("row", "col"), offset) for offset in offsets]
    above_norms = [passed_along(denoms, ("row", "col"), -offset) for offset in offsets]
    recips = 1.0 / denoms

    def weigh_tile(exps, others):
        return (exps * (recips[:, None] + 1.0 / others[None, :])).astype(jnp.bfloat16)

    gradient = jnp.dot(weigh_tile(self_tile, denoms), normed, preferred_element_type=jnp.float32)
    for number, offset in enumerate(offsets):
        weights = weigh_tile(below_tiles[number], below_norms[number])
        gradient = gradient + jnp.dot(
            weights, below_blocks[number], preferred_element_type=jnp.float32
        )
        weights_above = weigh_tile(above_tiles[number], above_norms[number])
        gradient = gradient + jnp.dot(
            weights_above, above_blocks[number], preferred_element_type=jnp.float32
        )
    matched = jnp.take(normed, positives, axis=0).astype(jnp.float32)
    return inverse_temp * gradient - 2.0 * inverse_temp * matched


def solution(mesh):
    placed = (P(("row", "col"), None), P(("row", "col")))
    return jax.shard_map(
        on_device, mesh=mesh, in_specs=placed, out_specs=P(("row", "col"), None), check_vma=False
    )
```

profile of v0, /device:TPU:1, one launch (start us, length us, event | category | flops | bytes accessed | tf_op | source)
XLA Modules:
  0.0 111.3 jit_solution(7365267149590418120)
XLA Ops:
  0.0 0.0 copy-start
  0.0 1.4 %fusion.9 = f32[768]{0:T(1024)S(1)} fusion(bf16[768,512]{1,0:T(8,128)(2,1)} %param.2), kind=kLoop, calls=%fused_computation.31 | loop fusion | flops 1178880 | bytes 789504 | tf_op jit(solution)/shard_map/reduce_sum | solution.py:26
  1.4 1.4 %fusion.10 = bf16[768,512]{1,0:T(8,128)(2,1)S(1)} fusion(bf16[768,512]{1,0:T(8,128)(2,1)} %param.2, f32[768]{0:T(1024)S(1)} %add_rsqrt_fusion), kind=kLoop, calls=%fused_computation.32 | loop fusion | flops 1179648 | bytes 1575936 | tf_op jit(solution)/shard_map/convert_element_type | solution.py:26
  2.8 11.1 %collective-permute-start.5 = (bf16[768,512]{1,0:T(8,128)(2,1)S(1)}, bf16[768,512]{1,0:T(8,128)(2,1)S(1)}, u32[]{:S(2)}, u32[]{:S(2)}) collective-permute-start(bf16[768,512]{1,0:T(8,128)(2,1)S(1)} %fusion.10), channel_id=1, source_target_pairs={{17,0},{18,1},{19,2},{20,3},{21,4},{22,5},{23,6},{24,7},{25,8},{26... | collective-permute-start | bytes 2359304 | tf_op jit(solution)/shard_map/ppermute | solution.py:13
  13.9 0.0 collective-permute-start.4
  13.9 1.0 collective-permute-start.3
  14.8 2.3 %collective-permute-start.2 = (bf16[768,512]{1,0:T(8,128)(2,1)S(1)}, bf16[768,512]{1,0:T(8,128)(2,1)}, u32[]{:S(2)}, u32[]{:S(2)}) collective-permute-start(bf16[768,512]{1,0:T(8,128)(2,1)S(1)} %fusion.10), channel_id=1, source_target_pairs={{240,0},{241,1},{242,2},{243,3},{244,4},{245,5},{246,6},{247,7},{2... | collective-permute-start | bytes 2359304 | tf_op jit(solution)/shard_map/ppermute | solution.py:13
  17.1 4.5 %collective-permute-start.1 = (bf16[768,512]{1,0:T(8,128)(2,1)S(1)}, bf16[768,512]{1,0:T(8,128)(2,1)}, u32[]{:S(2)}, u32[]{:S(2)}) collective-permute-start(bf16[768,512]{1,0:T(8,128)(2,1)S(1)} %fusion.10), channel_id=1, source_target_pairs={{1,0},{2,1},{3,2},{4,3},{5,4},{6,5},{7,6},{8,7},{9,8},{10,9},{11,1... | collective-permute-start | bytes 2359304 | tf_op jit(solution)/shard_map/ppermute | solution.py:13
  21.6 0.0 copy-done
  21.7 2.7 %gather_fusion = bf16[768,512]{1,0:T(8,128)(2,1)S(1)} fusion(bf16[768,512]{1,0:T(8,128)(2,1)S(1)} %fusion.10, s32[1024]{0:T(1024)S(1)} %pad_clamp_fusion), kind=kCustom, calls=%fused_computation | custom fusion | bytes 1575936 | tf_op jit(solution)/shard_map/jit(_take)/gather | solution.py:67
  24.3 0.8 fusion.8
  25.2 13.7 %collective-permute-done.5 = bf16[768,512]{1,0:T(8,128)(2,1)S(1)} collective-permute-done((bf16[768,512]{1,0:T(8,128)(2,1)S(1)}, bf16[768,512]{1,0:T(8,128)(2,1)S(1)}, u32[]{:S(2)}, u32[]{:S(2)}) %collective-permute-start.5) | collective-permute-done | bytes 786464 | tf_op jit(solution)/shard_map/ppermute | solution.py:13
  38.9 0.0 collective-permute-start
  38.9 0.8 fusion.5
  39.8 8.2 %collective-permute-done.4 = bf16[768,512]{1,0:T(8,128)(2,1)S(1)} collective-permute-done((bf16[768,512]{1,0:T(8,128)(2,1)S(1)}, bf16[768,512]{1,0:T(8,128)(2,1)S(1)}, u32[]{:S(2)}, u32[]{:S(2)}) %collective-permute-start.4) | collective-permute-done | bytes 786464 | tf_op jit(solution)/shard_map/ppermute | solution.py:13
  48.0 0.9 collective-permute-start.7
  48.9 0.8 fusion.4
  49.7 19.8 %collective-permute-done.3 = bf16[768,512]{1,0:T(8,128)(2,1)} collective-permute-done((bf16[768,512]{1,0:T(8,128)(2,1)S(1)}, bf16[768,512]{1,0:T(8,128)(2,1)}, u32[]{:S(2)}, u32[]{:S(2)}) %collective-permute-start.3) | collective-permute-done | bytes 786464 | tf_op jit(solution)/shard_map/ppermute | solution.py:13
  69.5 0.0 collective-permute-start.6
  69.5 2.0 %fusion.3 = (f32[768]{0:T(1024)S(1)}, f32[768,768]{0,1:T(8,128)S(1)}) fusion(bf16[768,512]{1,0:T(8,128)(2,1)S(1)} %fusion.10, bf16[768,512]{1,0:T(8,128)(2,1)} %collective-permute-done.3), kind=kOutput, calls=%fused_computation.23 | convolution fusion | flops 605158656 | bytes 3935232 | tf_op jit(solution)/shard_map/dot_general | solution.py:17
  71.5 0.0 collective-permute-done.2
  71.5 2.0 %fusion.2 = (f32[768]{0:T(1024)S(1)}, f32[768,768]{0,1:T(8,128)S(1)}) fusion(bf16[768,512]{1,0:T(8,128)(2,1)S(1)} %fusion.10, bf16[768,512]{1,0:T(8,128)(2,1)} %collective-permute-done.2), kind=kOutput, calls=%fused_computation.22 | convolution fusion | flops 605158656 | bytes 3935232 | tf_op jit(solution)/shard_map/dot_general | solution.py:17
  73.5 0.0 collective-permute-done.1
  73.5 2.0 %fusion.1 = (f32[768]{0:T(1024)S(1)}, f32[768,768]{0,1:T(8,128)S(1)}) fusion(bf16[768,512]{1,0:T(8,128)(2,1)S(1)} %fusion.10, bf16[768,512]{1,0:T(8,128)(2,1)} %collective-permute-done.1), kind=kOutput, calls=%fused_computation.21 | convolution fusion | flops 605158656 | bytes 3935232 | tf_op jit(solution)/shard_map/dot_general | solution.py:17
  75.5 0.0 collective-permute-done
  75.5 0.8 fusion
  76.3 0.0 collective-permute-done.7
  76.3 0.8 fusion.7
  77.1 4.4 %collective-permute-done.6 = bf16[768,512]{1,0:T(8,128)(2,1)S(1)} collective-permute-done((bf16[768,512]{1,0:T(8,128)(2,1)S(1)}, bf16[768,512]{1,0:T(8,128)(2,1)S(1)}, u32[]{:S(2)}, u32[]{:S(2)}) %collective-permute-start.6) | collective-permute-done | bytes 786464 | tf_op jit(solution)/shard_map/ppermute | solution.py:13
  81.6 0.8 fusion.6
  82.4 0.1 collective-permute-start.8
  82.5 3.8 %collective-permute-start.9 = (f32[768]{0:T(1024)S(1)}, f32[768]{0:T(1024)S(1)}, u32[]{:S(2)}, u32[]{:S(2)}) collective-permute-start(f32[768]{0:T(1024)S(1)} %get-tuple-element.6), channel_id=1, source_target_pairs={{1,0},{2,1},{3,2},{4,3},{5,4},{6,5},{7,6},{8,7},{9,8},{10,9},{11,1... | collective-permute-start | bytes 9224 | tf_op jit(solution)/shard_map/ppermute | solution.py:13
  86.4 0.8 collective-permute-start.10
  87.2 0.0 collective-permute-start.11
  87.2 1.0 collective-permute-start.12
  88.1 1.0 fusion.11
  89.1 0.0 collective-permute-done.8
  89.1 6.0 %collective-permute-start.13 = (f32[768]{0:T(1024)S(1)}, f32[768]{0:T(1024)S(1)}, u32[]{:S(2)}, u32[]{:S(2)}) collective-permute-start(f32[768]{0:T(1024)S(1)} %get-tuple-element.6), channel_id=1, source_target_pairs={{17,0},{18,1},{19,2},{20,3},{21,4},{22,5},{23,6},{24,7},{25,8},{26... | collective-permute-start | bytes 9224 | tf_op jit(solution)/shard_map/ppermute | solution.py:13
  95.2 0.0 collective-permute-done.9
  95.2 0.0 collective-permute-start.14
  95.2 0.0 collective-permute-done.10
  95.2 2.7 %collective-permute-start.15 = (f32[768]{0:T(1024)S(1)}, f32[768]{0:T(1024)S(1)}, u32[]{:S(2)}, u32[]{:S(2)}) collective-permute-start(f32[768]{0:T(1024)S(1)} %get-tuple-element.6), channel_id=1, source_target_pairs={{64,0},{65,1},{66,2},{67,3},{68,4},{69,5},{70,6},{71,7},{72,8},{73... | collective-permute-start | bytes 9224 | tf_op jit(solution)/shard_map/ppermute | solution.py:13
  97.9 0.0 collective-permute-done.11
  97.9 0.0 collective-permute-done.12
  97.9 0.0 collective-permute-done.13
  97.9 0.9 collective-permute-done.14
  98.8 0.0 collective-permute-done.15
  98.8 0.9 fusion.12
  99.8 2.1 %fusion.13 = f32[768,512]{1,0:T(8,128)S(1)} fusion(bf16[768,512]{1,0:T(8,128)(2,1)} %collective-permute-done.1, f32[768,768]{0,1:T(8,128)S(1)} %get-tuple-element.20, f32[768]{0:T(1024)S(1)} %broadcast_divide_fusion.6, f32[768]{0:T(1024)S(1)} %get-tuple-element.5), kind=kOutput, calls=%fused_computation.36 | convolution fusion | flops 606339072 | bytes 4724736 | tf_op jit(solution)/shard_map/dot_general | solution.py:64
  101.9 2.0 %fusion.14 = f32[768,512]{1,0:T(8,128)S(1)} fusion(bf16[768,512]{1,0:T(8,128)(2,1)} %collective-permute-done.2, f32[768,768]{0,1:T(8,128)S(1)} %get-tuple-element.18, f32[768]{0:T(1024)S(1)} %broadcast_divide_fusion.5, f32[768]{0:T(1024)S(1)} %get-tuple-element.5), kind=kOutput, calls=%fused_computation.37 | convolution fusion | flops 606339072 | bytes 4724736 | tf_op jit(solution)/shard_map/dot_general | solution.py:60
  103.9 2.0 %fusion.15 = f32[768,512]{1,0:T(8,128)S(1)} fusion(bf16[768,512]{1,0:T(8,128)(2,1)} %collective-permute-done.3, f32[768,768]{0,1:T(8,128)S(1)} %get-tuple-element.16, f32[768]{0:T(1024)S(1)} %broadcast_divide_fusion.4, f32[768]{0:T(1024)S(1)} %get-tuple-element.5), kind=kOutput, calls=%fused_computation.38 | convolution fusion | flops 606339072 | bytes 4724736 | tf_op jit(solution)/shard_map/dot_general | solution.py:64
  106.0 0.9 fusion.16
  106.9 0.9 fusion.17
  107.8 0.9 fusion.18
  108.7 2.6 %multiply_subtract_fusion = f32[768,512]{1,0:T(8,128)} fusion(f32[768,512]{1,0:T(8,128)S(1)} %fusion.18, f32[768,512]{1,0:T(8,128)S(1)} %fusion.17, f32[768,512]{1,0:T(8,128)S(1)} %fusion.16, f32[768,512]{1,0:T(8,128)S(1)} %fusion.15, f32[768,512]{1,0:T(8,128)S(1)} %fusion.14, f32[768,512]{1,0:T(8,128)S(1)} %fusion.13, f32[768,512]{1,0:T(8,128)S(1)} %fusion.11, ...), kind=kOutput, calls=%fused_computation.33 | convolution fusion | flops 611450880 | bytes 18094848 | tf_op jit(solution)/shard_map/dot_general | solution.py:64
  (13 shorter events, 0.1 us)
Async XLA Ops:
  0.0 21.6 %copy-start = (s32[768]{0:T(1024)S(1)}, s32[768]{0:T(1024)}, u32[]{:S(2)}) copy-start(s32[768]{0:T(1024)} %param.3) | copy-start | bytes 9220
  2.8 36.2 %collective-permute-start.5 = (bf16[768,512]{1,0:T(8,128)(2,1)S(1)}, bf16[768,512]{1,0:T(8,128)(2,1)S(1)}, u32[]{:S(2)}, u32[]{:S(2)}) collective-permute-start(bf16[768,512]{1,0:T(8,128)(2,1)S(1)} %fusion.10), channel_id=1, source_target_pairs={{17,0},{18,1},{19,2},{20,3},{21,4},{22,5},{23,6},{24,7},{25,8},{26... | collective-permute-start | bytes 2359304 | tf_op jit(solution)/shard_map/ppermute | solution.py:13
  13.9 34.1 %collective-permute-start.4 = (bf16[768,512]{1,0:T(8,128)(2,1)S(1)}, bf16[768,512]{1,0:T(8,128)(2,1)S(1)}, u32[]{:S(2)}, u32[]{:S(2)}) collective-permute-start(bf16[768,512]{1,0:T(8,128)(2,1)S(1)} %fusion.10), channel_id=1, source_target_pairs={{239,0},{240,1},{241,2},{242,3},{243,4},{244,5},{245,6},{246,7},{2... | collective-permute-start | bytes 2359304 | tf_op jit(solution)/shard_map/ppermute | solution.py:13
  13.9 55.6 %collective-permute-start.3 = (bf16[768,512]{1,0:T(8,128)(2,1)S(1)}, bf16[768,512]{1,0:T(8,128)(2,1)}, u32[]{:S(2)}, u32[]{:S(2)}) collective-permute-start(bf16[768,512]{1,0:T(8,128)(2,1)S(1)} %fusion.10), channel_id=1, source_target_pairs={{16,0},{17,1},{18,2},{19,3},{20,4},{21,5},{22,6},{23,7},{24,8},{25... | collective-permute-start | bytes 2359304 | tf_op jit(solution)/shard_map/ppermute | solution.py:13
  14.8 56.7 %collective-permute-start.2 = (bf16[768,512]{1,0:T(8,128)(2,1)S(1)}, bf16[768,512]{1,0:T(8,128)(2,1)}, u32[]{:S(2)}, u32[]{:S(2)}) collective-permute-start(bf16[768,512]{1,0:T(8,128)(2,1)S(1)} %fusion.10), channel_id=1, source_target_pairs={{240,0},{241,1},{242,2},{243,3},{244,4},{245,5},{246,6},{247,7},{2... | collective-permute-start | bytes 2359304 | tf_op jit(solution)/shard_map/ppermute | solution.py:13
  17.1 56.3 %collective-permute-start.1 = (bf16[768,512]{1,0:T(8,128)(2,1)S(1)}, bf16[768,512]{1,0:T(8,128)(2,1)}, u32[]{:S(2)}, u32[]{:S(2)}) collective-permute-start(bf16[768,512]{1,0:T(8,128)(2,1)S(1)} %fusion.10), channel_id=1, source_target_pairs={{1,0},{2,1},{3,2},{4,3},{5,4},{6,5},{7,6},{8,7},{9,8},{10,9},{11,1... | collective-permute-start | bytes 2359304 | tf_op jit(solution)/shard_map/ppermute | solution.py:13
  38.9 36.5 %collective-permute-start = (bf16[768,512]{1,0:T(8,128)(2,1)S(1)}, bf16[768,512]{1,0:T(8,128)(2,1)S(1)}, u32[]{:S(2)}, u32[]{:S(2)}) collective-permute-start(bf16[768,512]{1,0:T(8,128)(2,1)S(1)} %fusion.10), channel_id=1, source_target_pairs={{255,0},{0,1},{1,2},{2,3},{3,4},{4,5},{5,6},{6,7},{7,8},{8,9},{9,1... | collective-permute-start | bytes 2359304 | tf_op jit(solution)/shard_map/ppermute | solution.py:13
  48.0 28.3 %collective-permute-start.7 = (bf16[768,512]{1,0:T(8,128)(2,1)S(1)}, bf16[768,512]{1,0:T(8,128)(2,1)S(1)}, u32[]{:S(2)}, u32[]{:S(2)}) collective-permute-start(bf16[768,512]{1,0:T(8,128)(2,1)S(1)} %fusion.10), channel_id=1, source_target_pairs={{64,0},{65,1},{66,2},{67,3},{68,4},{69,5},{70,6},{71,7},{72,8},{73... | collective-permute-start | bytes 2359304 | tf_op jit(solution)/shard_map/ppermute | solution.py:13
  69.5 12.1 %collective-permute-start.6 = (bf16[768,512]{1,0:T(8,128)(2,1)S(1)}, bf16[768,512]{1,0:T(8,128)(2,1)S(1)}, u32[]{:S(2)}, u32[]{:S(2)}) collective-permute-start(bf16[768,512]{1,0:T(8,128)(2,1)S(1)} %fusion.10), channel_id=1, source_target_pairs={{192,0},{193,1},{194,2},{195,3},{196,4},{197,5},{198,6},{199,7},{2... | collective-permute-start | bytes 2359304 | tf_op jit(solution)/shard_map/ppermute | solution.py:13
  82.4 6.7 %collective-permute-start.8 = (f32[768]{0:T(1024)S(1)}, f32[768]{0:T(1024)S(1)}, u32[]{:S(2)}, u32[]{:S(2)}) collective-permute-start(f32[768]{0:T(1024)S(1)} %get-tuple-element.6), channel_id=1, source_target_pairs={{255,0},{0,1},{1,2},{2,3},{3,4},{4,5},{5,6},{6,7},{7,8},{8,9},{9,1... | collective-permute-start | bytes 9224 | tf_op jit(solution)/shard_map/ppermute | solution.py:13
  82.5 12.6 %collective-permute-start.9 = (f32[768]{0:T(1024)S(1)}, f32[768]{0:T(1024)S(1)}, u32[]{:S(2)}, u32[]{:S(2)}) collective-permute-start(f32[768]{0:T(1024)S(1)} %get-tuple-element.6), channel_id=1, source_target_pairs={{1,0},{2,1},{3,2},{4,3},{5,4},{6,5},{7,6},{8,7},{9,8},{10,9},{11,1... | collective-permute-start | bytes 9224 | tf_op jit(solution)/shard_map/ppermute | solution.py:13
  86.4 8.8 %collective-permute-start.10 = (f32[768]{0:T(1024)S(1)}, f32[768]{0:T(1024)S(1)}, u32[]{:S(2)}, u32[]{:S(2)}) collective-permute-start(f32[768]{0:T(1024)S(1)} %get-tuple-element.6), channel_id=1, source_target_pairs={{240,0},{241,1},{242,2},{243,3},{244,4},{245,5},{246,6},{247,7},{2... | collective-permute-start | bytes 9224 | tf_op jit(solution)/shard_map/ppermute | solution.py:13
  87.2 10.7 %collective-permute-start.11 = (f32[768]{0:T(1024)S(1)}, f32[768]{0:T(1024)S(1)}, u32[]{:S(2)}, u32[]{:S(2)}) collective-permute-start(f32[768]{0:T(1024)S(1)} %get-tuple-element.6), channel_id=1, source_target_pairs={{16,0},{17,1},{18,2},{19,3},{20,4},{21,5},{22,6},{23,7},{24,8},{25... | collective-permute-start | bytes 9224 | tf_op jit(solution)/shard_map/ppermute | solution.py:13
  87.2 10.7 %collective-permute-start.12 = (f32[768]{0:T(1024)S(1)}, f32[768]{0:T(1024)S(1)}, u32[]{:S(2)}, u32[]{:S(2)}) collective-permute-start(f32[768]{0:T(1024)S(1)} %get-tuple-element.6), channel_id=1, source_target_pairs={{239,0},{240,1},{241,2},{242,3},{243,4},{244,5},{245,6},{246,7},{2... | collective-permute-start | bytes 9224 | tf_op jit(solution)/shard_map/ppermute | solution.py:13
  89.1 8.8 %collective-permute-start.13 = (f32[768]{0:T(1024)S(1)}, f32[768]{0:T(1024)S(1)}, u32[]{:S(2)}, u32[]{:S(2)}) collective-permute-start(f32[768]{0:T(1024)S(1)} %get-tuple-element.6), channel_id=1, source_target_pairs={{17,0},{18,1},{19,2},{20,3},{21,4},{22,5},{23,6},{24,7},{25,8},{26... | collective-permute-start | bytes 9224 | tf_op jit(solution)/shard_map/ppermute | solution.py:13
  95.2 3.7 %collective-permute-start.14 = (f32[768]{0:T(1024)S(1)}, f32[768]{0:T(1024)S(1)}, u32[]{:S(2)}, u32[]{:S(2)}) collective-permute-start(f32[768]{0:T(1024)S(1)} %get-tuple-element.6), channel_id=1, source_target_pairs={{192,0},{193,1},{194,2},{195,3},{196,4},{197,5},{198,6},{199,7},{2... | collective-permute-start | bytes 9224 | tf_op jit(solution)/shard_map/ppermute | solution.py:13
  95.2 3.6 %collective-permute-start.15 = (f32[768]{0:T(1024)S(1)}, f32[768]{0:T(1024)S(1)}, u32[]{:S(2)}, u32[]{:S(2)}) collective-permute-start(f32[768]{0:T(1024)S(1)} %get-tuple-element.6), channel_id=1, source_target_pairs={{64,0},{65,1},{66,2},{67,3},{68,4},{69,5},{70,6},{71,7},{72,8},{73... | collective-permute-start | bytes 9224 | tf_op jit(solution)/shard_map/ppermute | solution.py:13
where the time goes:
time: 112 us; the launch traced here: 111 us
  waiting for transfers between devices  47.1 us (42%)
  starting transfers between devices  34.2 us (31%)
  matrix products  24.2 us (22%)
  other arithmetic  2.79 us (2%)
  local copies, waits for them, and re-layouts  2.69 us (2%)
    ppermute x16, waiting for transfers between devices, passed_along(): return lax.ppermute(block, axis, route)  47.1 us
    ppermute x16, starting transfers between devices, passed_along(): return lax.ppermute(block, axis, route)  34.2 us
    dot_general x9, matrix products, exp_tile(): lax.dot_general(mine, theirs, (((1,), (1,)), ((), ())), preferred_element...  10.9 us
    dot_general x4, matrix products, on_device(): jnp.dot(weights_above, above_blocks[number], preferred_element_type=jnp.f...  7.65 us
    dot_general x4, matrix products, on_device(): jnp.dot(weights, below_blocks[number], preferred_element_type=jnp.float32)  4.77 us
    gather x1, local copies, waits for them, and re-layouts, on_device(): matched = jnp.take(normed, positives, axis=0).astype(jnp.float32)  2.68 us
  transfers between devices with their start and end apart: 16, of which 5 were waited for; matrix products, arithmetic and copies ran while one was open for 12% of the time, Pallas kernels for 0%

commit v1 on v0

v1 whole, which is shorter than its diff:
```python
import jax
import jax.numpy as jnp
from jax import lax
from jax.sharding import PartitionSpec as P

inverse_temp = 5.0
epsilon = 1e-06
both = ("row", "col")


def routes(rows, cols):
    count = rows * cols
    far_step = cols
    x_step = count // 4

    def wrap(value):
        return value % count

    def core(b):
        return (b // cols) % 2

    def half(b):
        return (b // (2 * cols)) % 2

    def far17(b):
        j = b % cols
        if core(b) == 0:
            if j == 0:
                return wrap(b + (2 * cols if half(b) == 0 else -2 * cols) + cols - 1)
            return wrap(b - 2 * cols - 1) if j == cols // 2 else b - 1
        if j == cols - 1:
            return wrap(b + (2 * cols if half(b) == 0 else -2 * cols) - cols + 1)
        return wrap(b + 2 * cols + 1) if j == cols // 2 - 1 else b + 1

    sources = {
        "above": lambda b: wrap(b + 1),
        "below": lambda b: wrap(b - 1),
        "x_above": lambda b: wrap(b + x_step),
        "x_below": lambda b: wrap(b - x_step),
        "near": lambda b: b + far_step if core(b) == 0 else b - far_step,
        "far": lambda b: wrap(b - far_step if core(b) == 0 else b + far_step),
        "far17": far17,
    }
    return {name: [(source(b), b) for b in range(count)] for name, source in sources.items()}


def exp_tile(mine, theirs):
    scores = lax.dot_general(
        mine, theirs, (((1,), (1,)), ((), ())), preferred_element_type=jnp.float32
    )
    exps = jnp.exp(scores * inverse_temp)
    return exps


def on_device(embeddings, positives):
    row_count = embeddings.shape[0]
    rows, cols = lax.axis_size("row"), lax.axis_size("col")
    route = routes(rows, cols)
    row, col = lax.axis_index("row"), lax.axis_index("col")
    core0 = row % 2 == 0

    def send(block, name):
        return lax.ppermute(block, both, route[name])

    wide = embeddings.astype(jnp.float32)
    normed = (wide * lax.rsqrt(jnp.sum(wide * wide, axis=-1, keepdims=True) + epsilon)).astype(
        jnp.bfloat16
    )
    matched = jnp.take(normed, positives, axis=0).astype(jnp.float32)

    far = send(normed, "far")
    above = send(normed, "above")
    below = send(normed, "below")
    x_above = send(normed, "x_above")
    x_below = send(normed, "x_below")
    near = send(normed, "near")
    last = jnp.where(core0, cols - 1, 0)
    turn = jnp.where(core0, cols // 2 - 1, cols // 2)
    crossing = (row // 2) % 2 == jnp.where(core0, 1, 0)
    passed = jnp.where(
        col == last,
        jnp.where(crossing, jnp.where(core0, x_below, x_above), normed),
        jnp.where(col == turn, near, far),
    )
    far17 = send(passed, "far17")
    near17 = send(jnp.where(core0, below, above), "near")

    diagonal = jnp.arange(row_count)[:, None] == jnp.arange(row_count)[None, :]
    self_tile = jnp.where(diagonal, jnp.float32(0.0), exp_tile(normed, normed))
    denoms = jnp.sum(self_tile, axis=1)
    blocks = [near, above, below, x_above, x_below, far, near17, far17]
    tiles = []
    for block in blocks:
        tile = exp_tile(normed, block)
        denoms = denoms + jnp.sum(tile, axis=1)
        tiles.append(tile.astype(jnp.bfloat16))
    d_above = send(denoms, "above")
    d_below = send(denoms, "below")
    d_x_above = send(denoms, "x_above")
    d_x_below = send(denoms, "x_below")
    trio = jnp.stack([denoms, d_above, d_below])
    near_trio = send(trio, "near")
    far_trio = send(trio, "far")
    d_near, d_far = near_trio[0], far_trio[0]
    d_near17 = jnp.where(core0, near_trio[1], near_trio[2])
    d_far17 = jnp.where(core0, far_trio[2], far_trio[1])
    norms = [d_near, d_above, d_below, d_x_above, d_x_below, d_far, d_near17, d_far17]
    recips = 1.0 / denoms

    def weigh_tile(exps, others):
        return (exps * (recips[:, None] + 1.0 / others[None, :])).astype(jnp.bfloat16)

    gradient = jnp.dot(weigh_tile(self_tile, denoms), normed, preferred_element_type=jnp.float32)
    order = [3, 4, 1, 2, 0, 5, 6, 7]
    for number in order:
        weights = weigh_tile(tiles[number].astype(jnp.float32), norms[number])
        gradient = gradient + jnp.dot(weights, blocks[number], preferred_element_type=jnp.float32)
    return inverse_temp * gradient - 2.0 * inverse_temp * matched


def solution(mesh):
    placed = (P(("row", "col"), None), P(("row", "col")))
    return jax.shard_map(
        on_device, mesh=mesh, in_specs=placed, out_specs=P(("row", "col"), None), check_vma=False
    )
```

time: 112 us -> 93.2 us (0.83)
  waiting for transfers between devices: 47.1 us -> 9.25 us
  starting transfers between devices: 34.2 us -> 50.4 us
  other arithmetic: 2.79 us -> 5.55 us
    ppermute x16 -> x14, waiting for transfers between devices: 47.1 us -> 9.25 us  [send(): return lax.ppermute(block, both, route[name])]
    ppermute x16 -> x14, starting transfers between devices: 34.2 us -> 50.4 us  [send(): return lax.ppermute(block, both, route[name])]
    select_n x0 -> x2, other arithmetic: none -> 2.7 us  [the longest x1 1.45 us: on_device(): jnp.where(col == last, jnp.where(crossing, jnp.where(core0, x_below, x_ab...]
  transfers between devices with their start and end apart: 16 -> 14, of which waited for: 5 -> 3; matrix products, arithmetic and copies ran while one was open for 12% -> 26% of each run, Pallas kernels for 0% -> 0%
where the time goes in v1:
time: 93.2 us; the launch traced here: 92.8 us
  starting transfers between devices  50.4 us (54%)
  matrix products  24.5 us (26%)
  waiting for transfers between devices  9.25 us (10%)
  other arithmetic  5.55 us (6%)
  local copies, waits for them, and re-layouts  2.7 us (3%)
    ppermute x14, starting transfers between devices, send(): return lax.ppermute(block, both, route[name])  50.4 us
    dot_general x8, matrix products, on_device(): jnp.dot(weights, blocks[number], preferred_element_type=jnp.float32)  12.7 us
    dot_general x9, matrix products, exp_tile(): lax.dot_general(mine, theirs, (((1,), (1,)), ((), ())), preferred_element...  10.9 us
    ppermute x14, waiting for transfers between devices, send(): return lax.ppermute(block, both, route[name])  9.25 us
    gather x1, local copies, waits for them, and re-layouts, on_device(): matched = jnp.take(normed, positives, axis=0).astype(jnp.float32)  2.68 us
  transfers between devices with their start and end apart: 14, of which 3 were waited for; matrix products, arithmetic and copies ran while one was open for 26% of the time, Pallas kernels for 0%

profile of v1, /device:TPU:1, one launch (start us, length us, event | category | flops | bytes accessed | tf_op | source)
XLA Modules:
  0.0 92.8 jit_solution(870352863988287626)
XLA Ops:
  0.0 0.0 copy-start.1
  0.0 1.4 %fusion.17 = f32[768]{0:T(1024)S(1)} fusion(bf16[768,512]{1,0:T(8,128)(2,1)} %param.2), kind=kLoop, calls=%fused_computation.39 | loop fusion | flops 1178880 | bytes 789504 | tf_op jit(solution)/shard_map/reduce_sum | solution.py:66
  1.4 1.4 %fusion.18 = bf16[768,512]{1,0:T(8,128)(2,1)S(1)} fusion(bf16[768,512]{1,0:T(8,128)(2,1)} %param.2, f32[768]{0:T(1024)S(1)} %add_rsqrt_fusion), kind=kLoop, calls=%fused_computation.40 | loop fusion | flops 1179648 | bytes 1575936 | tf_op jit(solution)/shard_map/convert_element_type | solution.py:66
  2.8 3.3 %collective-permute-start = (bf16[768,512]{1,0:T(8,128)(2,1)S(1)}, bf16[768,512]{1,0:T(8,128)(2,1)S(1)}, u32[]{:S(2)}, u32[]{:S(2)}) collective-permute-start(bf16[768,512]{1,0:T(8,128)(2,1)S(1)} %fusion.18), channel_id=1, source_target_pairs={{16,0},{17,1},{18,2},{19,3},{20,4},{21,5},{22,6},{23,7},{24,8},{25... | collective-permute-start | bytes 2359304 | tf_op jit(solution)/shard_map/ppermute | solution.py:63
  6.1 0.8 collective-permute-start.3
  6.8 0.7 collective-permute-start.4
  7.6 2.4 %collective-permute-start.5 = (bf16[768,512]{1,0:T(8,128)(2,1)S(1)}, bf16[768,512]{1,0:T(8,128)(2,1)S(1)}, u32[]{:S(2)}, u32[]{:S(2)}) collective-permute-start(bf16[768,512]{1,0:T(8,128)(2,1)S(1)} %fusion.18), channel_id=1, source_target_pairs={{240,0},{241,1},{242,2},{243,3},{244,4},{245,5},{246,6},{247,7},{2... | collective-permute-start | bytes 2359304 | tf_op jit(solution)/shard_map/ppermute | solution.py:63
  10.0 8.1 %collective-permute-start.1 = (bf16[768,512]{1,0:T(8,128)(2,1)S(1)}, bf16[768,512]{1,0:T(8,128)(2,1)}, u32[]{:S(2)}, u32[]{:S(2)}) collective-permute-start(bf16[768,512]{1,0:T(8,128)(2,1)S(1)} %fusion.18), channel_id=1, source_target_pairs={{1,0},{2,1},{3,2},{4,3},{5,4},{6,5},{7,6},{8,7},{9,8},{10,9},{11,1... | collective-permute-start | bytes 2359304 | tf_op jit(solution)/shard_map/ppermute | solution.py:63
  18.1 0.0 copy-done.1
  18.1 2.7 %gather_fusion = bf16[768,512]{1,0:T(8,128)(2,1)S(1)} fusion(bf16[768,512]{1,0:T(8,128)(2,1)S(1)} %fusion.18, s32[1024]{0:T(1024)S(1)} %pad_clamp_fusion), kind=kCustom, calls=%fused_computation | custom fusion | bytes 1575936 | tf_op jit(solution)/shard_map/jit(_take)/gather | solution.py:69
  20.8 0.0 collective-permute-done
  20.8 0.1 collective-permute-start.2
  21.0 0.0 copy-start
  21.0 0.9 fusion.16
  21.8 3.5 %collective-permute-done.3 = bf16[768,512]{1,0:T(8,128)(2,1)} collective-permute-done((bf16[768,512]{1,0:T(8,128)(2,1)S(1)}, bf16[768,512]{1,0:T(8,128)(2,1)}, u32[]{:S(2)}, u32[]{:S(2)}) %collective-permute-start.3) | collective-permute-done | bytes 786464 | tf_op jit(solution)/shard_map/ppermute | solution.py:63
  25.3 1.6 %collective-permute-done.4 = bf16[768,512]{1,0:T(8,128)(2,1)} collective-permute-done((bf16[768,512]{1,0:T(8,128)(2,1)S(1)}, bf16[768,512]{1,0:T(8,128)(2,1)}, u32[]{:S(2)}, u32[]{:S(2)}) %collective-permute-start.4) | collective-permute-done | bytes 786464 | tf_op jit(solution)/shard_map/ppermute | solution.py:63
  26.9 0.0 collective-permute-done.5
  26.9 0.0 copy-done
  26.9 1.5 %select_select_fusion = bf16[768,512]{1,0:T(8,128)(2,1)S(1)} fusion(bf16[768,512]{1,0:T(8,128)(2,1)S(1)} %collective-permute-done, bf16[768,512]{1,0:T(8,128)(2,1)S(1)} %collective-permute-done.5, bf16[768,512]{1,0:T(8,128)(2,1)} %collective-permute-done.4, bf16[768,512]{1,0:T(8,128)(2,1)} %collective-permute-done.3, pred[]{:T(512)S(6)} %eq.34, pred[]{:T(512)S(6)} %eq.33, ...), kind=kLoop, calls=%fused_computation.79 | loop fusion | flops 2752512 | bytes 4721668 | tf_op jit(solution)/shard_map/jit(_where)/select_n | solution.py:80
  28.4 20.7 %collective-permute-start.7 = (bf16[768,512]{1,0:T(8,128)(2,1)S(1)}, bf16[768,512]{1,0:T(8,128)(2,1)S(1)}, u32[]{:S(2)}, u32[]{:S(2)}) collective-permute-start(bf16[768,512]{1,0:T(8,128)(2,1)S(1)} %select_select_fusion), channel_id=1, source_target_pairs={{47,0},{0,1},{1,2},{2,3},{3,4},{4,5},{5,6},{6,7},{231,8},{8,9},{9,... | collective-permute-start | bytes 2359304 | tf_op jit(solution)/shard_map/ppermute | solution.py:63
  49.1 0.0 collective-permute-done.1
  49.1 0.0 collective-permute-done.2
  49.1 1.2 %broadcast_select_fusion = bf16[768,512]{1,0:T(8,128)(2,1)S(1)} fusion(bf16[768,512]{1,0:T(8,128)(2,1)S(1)} %collective-permute-done.2, bf16[768,512]{1,0:T(8,128)(2,1)} %collective-permute-done.1, pred[]{:T(512)S(6)} %eq.31), kind=kLoop, calls=%fused_computation.80 | loop fusion | flops 393216 | bytes 2359297 | tf_op jit(solution)/shard_map/jit(_where)/select_n | solution.py:86
  50.4 0.3 collective-permute-start.6
  50.7 0.8 fusion.11
  51.5 2.0 %fusion.9 = (f32[768]{0:T(1024)S(1)}, f32[768,768]{0,1:T(8,128)S(1)}) fusion(bf16[768,512]{1,0:T(8,128)(2,1)S(1)} %fusion.18, bf16[768,512]{1,0:T(8,128)(2,1)} %collective-permute-done.4), kind=kOutput, calls=%fused_computation.29 | convolution fusion | flops 605158656 | bytes 3935232 | tf_op jit(solution)/shard_map/dot_general | solution.py:48
  53.5 2.0 %fusion.7 = (f32[768]{0:T(1024)S(1)}, f32[768,768]{0,1:T(8,128)S(1)}) fusion(bf16[768,512]{1,0:T(8,128)(2,1)S(1)} %fusion.18, bf16[768,512]{1,0:T(8,128)(2,1)} %collective-permute-done.3), kind=kOutput, calls=%fused_computation.27 | convolution fusion | flops 605158656 | bytes 3935232 | tf_op jit(solution)/shard_map/dot_general | solution.py:48
  55.4 0.8 fusion.5
  56.2 2.0 %fusion.3 = (f32[768]{0:T(1024)S(1)}, f32[768,768]{0,1:T(8,128)S(1)}) fusion(bf16[768,512]{1,0:T(8,128)(2,1)S(1)} %fusion.18, bf16[768,512]{1,0:T(8,128)(2,1)} %collective-permute-done.1), kind=kOutput, calls=%fused_computation.23 | convolution fusion | flops 605158656 | bytes 3935232 | tf_op jit(solution)/shard_map/dot_general | solution.py:48
  58.2 0.8 fusion.1
  59.0 0.0 collective-permute-done.7
  59.1 0.8 fusion.15
  59.9 0.0 collective-permute-done.6
  59.9 0.8 fusion.13
  60.8 2.4 %collective-permute-start.8 = (f32[768]{0:T(1024)S(1)}, f32[768]{0:T(1024)S(1)}, u32[]{:S(2)}, u32[]{:S(2)}) collective-permute-start(f32[768]{0:T(1024)S(1)} %get-tuple-element.10), channel_id=1, source_target_pairs={{64,0},{65,1},{66,2},{67,3},{68,4},{69,5},{70,6},{71,7},{72,8},{73... | collective-permute-start | bytes 9224 | tf_op jit(solution)/shard_map/ppermute | solution.py:63
  63.2 0.0 collective-permute-start.9
  63.2 5.1 %collective-permute-start.10 = (f32[768]{0:T(1024)S(1)}, f32[768]{0:T(1024)S(1)}, u32[]{:S(2)}, u32[]{:S(2)}) collective-permute-start(f32[768]{0:T(1024)S(1)} %get-tuple-element.10), channel_id=1, source_target_pairs={{1,0},{2,1},{3,2},{4,3},{5,4},{6,5},{7,6},{8,7},{9,8},{10,9},{11,1... | collective-permute-start | bytes 9224 | tf_op jit(solution)/shard_map/ppermute | solution.py:63
  68.3 0.0 collective-permute-start.11
  68.3 1.0 %fusion.19 = f32[768,512]{1,0:T(8,128)S(1)} fusion(bf16[768,512]{1,0:T(8,128)(2,1)S(1)} %fusion.18, f32[768,768]{0,1:T(8,128)S(1)} %get-tuple-element.26, f32[768]{0:T(1024)S(1)} %get-tuple-element.9), kind=kOutput, calls=%fused_computation.42 | convolution fusion | flops 607518720 | bytes 4721664 | tf_op jit(solution)/shard_map/dot_general | solution.py:113
  69.2 0.0 collective-permute-done.10
  69.3 4.1 %collective-permute-done.11 = f32[768]{0:T(1024)S(1)} collective-permute-done((f32[768]{0:T(1024)S(1)}, f32[768]{0:T(1024)S(1)}, u32[]{:S(2)}, u32[]{:S(2)}) %collective-permute-start.11) | collective-permute-done | bytes 3104 | tf_op jit(solution)/shard_map/ppermute | solution.py:63
  73.4 6.5 %collective-permute-start.12 = (f32[3,768]{1,0:T(4,128)S(1)}, f32[3,768]{1,0:T(4,128)S(1)}, u32[]{:S(2)}, u32[]{:S(2)}) collective-permute-start(f32[3,768]{1,0:T(4,128)S(1)} %pad_maximum_fusion), channel_id=1, source_target_pairs={{16,0},{17,1},{18,2},{19,3},{20,4},{21,5},{22,6},{23,7},{24,8},{25... | collective-permute-start | bytes 27656 | tf_op jit(solution)/shard_map/ppermute | solution.py:63
  79.9 0.0 collective-permute-start.13
  79.9 0.0 collective-permute-done.8
  79.9 0.0 collective-permute-done.9
  79.9 2.1 %fusion.20 = f32[768,512]{1,0:T(8,128)S(1)} fusion(bf16[768,512]{1,0:T(8,128)(2,1)} %collective-permute-done.3, f32[768,768]{0,1:T(8,128)S(1)} %get-tuple-element.20, f32[768]{0:T(1024)S(1)} %broadcast_divide_fusion.3, f32[768]{0:T(1024)S(1)} %get-tuple-element.9), kind=kOutput, calls=%fused_computation.43 | convolution fusion | flops 607518720 | bytes 4724736 | tf_op jit(solution)/shard_map/dot_general | solution.py:117
  82.0 2.1 %fusion.21 = f32[768,512]{1,0:T(8,128)S(1)} fusion(bf16[768,512]{1,0:T(8,128)(2,1)} %collective-permute-done.4, f32[768,768]{0,1:T(8,128)S(1)} %get-tuple-element.18, f32[768]{0:T(1024)S(1)} %broadcast_divide_fusion.2, f32[768]{0:T(1024)S(1)} %get-tuple-element.9), kind=kOutput, calls=%fused_computation.44 | convolution fusion | flops 607518720 | bytes 4724736 | tf_op jit(solution)/shard_map/dot_general | solution.py:117
  84.1 2.1 %fusion.22 = f32[768,512]{1,0:T(8,128)S(1)} fusion(bf16[768,512]{1,0:T(8,128)(2,1)} %collective-permute-done.1, f32[768,768]{0,1:T(8,128)S(1)} %get-tuple-element.24, f32[768]{0:T(1024)S(1)} %broadcast_divide_fusion.1, f32[768]{0:T(1024)S(1)} %get-tuple-element.9), kind=kOutput, calls=%fused_computation.45 | convolution fusion | flops 607518720 | bytes 4724736 | tf_op jit(solution)/shard_map/dot_general | solution.py:117
  86.2 1.0 %fusion.23 = f32[768,512]{1,0:T(8,128)S(1)} fusion(bf16[768,512]{1,0:T(8,128)(2,1)S(1)} %collective-permute-done.2, f32[768,768]{0,1:T(8,128)S(1)} %get-tuple-element.22, f32[768]{0:T(1024)S(1)} %broadcast_divide_fusion, f32[768]{0:T(1024)S(1)} %get-tuple-element.9), kind=kOutput, calls=%fused_computation.46 | convolution fusion | flops 607518720 | bytes 4724736 | tf_op jit(solution)/shard_map/dot_general | solution.py:117
  87.2 0.0 collective-permute-done.12
  87.2 0.0 collective-permute-done.13
  87.3 0.9 %fusion.24 = f32[768,512]{1,0:T(8,128)S(1)} fusion(bf16[768,512]{1,0:T(8,128)(2,1)S(1)} %collective-permute-done, f32[768,768]{0,1:T(8,128)S(1)} %get-tuple-element.28, f32[768]{0:T(1024)S(1)} %get-tuple-element.7, f32[768]{0:T(1024)S(1)} %get-tuple-element.9), kind=kOutput, calls=%fused_computation.47 | convolution fusion | flops 607518720 | bytes 4724736 | tf_op jit(solution)/shard_map/dot_general | solution.py:117
  88.2 0.9 %fusion.25 = f32[768,512]{1,0:T(8,128)S(1)} fusion(bf16[768,512]{1,0:T(8,128)(2,1)S(1)} %collective-permute-done.5, f32[768,768]{0,1:T(8,128)S(1)} %get-tuple-element.16, f32[768]{0:T(1024)S(1)} %get-tuple-element.6, f32[768]{0:T(1024)S(1)} %get-tuple-element.9), kind=kOutput, calls=%fused_computation.48 | convolution fusion | flops 607518720 | bytes 4724736 | tf_op jit(solution)/shard_map/dot_general | solution.py:117
  89.2 1.0 %fusion.26 = f32[768,512]{1,0:T(8,128)S(1)} fusion(bf16[768,512]{1,0:T(8,128)(2,1)S(1)} %collective-permute-done.6, f32[768,768]{0,1:T(8,128)S(1)} %get-tuple-element.14, f32[768]{0:T(1024)S(1)} %get-tuple-element.8, f32[768]{0:T(1024)S(1)} %get-tuple-element.9), kind=kOutput, calls=%fused_computation.49 | convolution fusion | flops 607518720 | bytes 4724736 | tf_op jit(solution)/shard_map/dot_general | solution.py:117
  90.1 2.6 %multiply_subtract_fusion = f32[768,512]{1,0:T(8,128)} fusion(f32[768,512]{1,0:T(8,128)S(1)} %fusion.26, f32[768,512]{1,0:T(8,128)S(1)} %fusion.25, f32[768,512]{1,0:T(8,128)S(1)} %fusion.24, f32[768,512]{1,0:T(8,128)S(1)} %fusion.23, f32[768,512]{1,0:T(8,128)S(1)} %fusion.22, f32[768,512]{1,0:T(8,128)S(1)} %fusion.21, f32[768,512]{1,0:T(8,128)S(1)} %fusion.19, ...), kind=kOutput, calls=%fused_computation.41 | convolution fusion | flops 612630528 | bytes 18094848 | tf_op jit(solution)/shard_map/dot_general | solution.py:117
  (15 shorter events, 0.1 us)
Async XLA Ops:
  0.0 18.1 %copy-start.1 = (s32[768]{0:T(1024)S(1)}, s32[768]{0:T(1024)}, u32[]{:S(2)}) copy-start(s32[768]{0:T(1024)} %param.3) | copy-start | bytes 9220
  2.8 18.1 %collective-permute-start = (bf16[768,512]{1,0:T(8,128)(2,1)S(1)}, bf16[768,512]{1,0:T(8,128)(2,1)S(1)}, u32[]{:S(2)}, u32[]{:S(2)}) collective-permute-start(bf16[768,512]{1,0:T(8,128)(2,1)S(1)} %fusion.18), channel_id=1, source_target_pairs={{16,0},{17,1},{18,2},{19,3},{20,4},{21,5},{22,6},{23,7},{24,8},{25... | collective-permute-start | bytes 2359304 | tf_op jit(solution)/shard_map/ppermute | solution.py:63
  6.1 19.2 %collective-permute-start.3 = (bf16[768,512]{1,0:T(8,128)(2,1)S(1)}, bf16[768,512]{1,0:T(8,128)(2,1)}, u32[]{:S(2)}, u32[]{:S(2)}) collective-permute-start(bf16[768,512]{1,0:T(8,128)(2,1)S(1)} %fusion.18), channel_id=1, source_target_pairs={{64,0},{65,1},{66,2},{67,3},{68,4},{69,5},{70,6},{71,7},{72,8},{73... | collective-permute-start | bytes 2359304 | tf_op jit(solution)/shard_map/ppermute | solution.py:63
  6.8 20.1 %collective-permute-start.4 = (bf16[768,512]{1,0:T(8,128)(2,1)S(1)}, bf16[768,512]{1,0:T(8,128)(2,1)}, u32[]{:S(2)}, u32[]{:S(2)}) collective-permute-start(bf16[768,512]{1,0:T(8,128)(2,1)S(1)} %fusion.18), channel_id=1, source_target_pairs={{192,0},{193,1},{194,2},{195,3},{196,4},{197,5},{198,6},{199,7},{2... | collective-permute-start | bytes 2359304 | tf_op jit(solution)/shard_map/ppermute | solution.py:63
  7.6 19.4 %collective-permute-start.5 = (bf16[768,512]{1,0:T(8,128)(2,1)S(1)}, bf16[768,512]{1,0:T(8,128)(2,1)S(1)}, u32[]{:S(2)}, u32[]{:S(2)}) collective-permute-start(bf16[768,512]{1,0:T(8,128)(2,1)S(1)} %fusion.18), channel_id=1, source_target_pairs={{240,0},{241,1},{242,2},{243,3},{244,4},{245,5},{246,6},{247,7},{2... | collective-permute-start | bytes 2359304 | tf_op jit(solution)/shard_map/ppermute | solution.py:63
  10.0 39.1 %collective-permute-start.1 = (bf16[768,512]{1,0:T(8,128)(2,1)S(1)}, bf16[768,512]{1,0:T(8,128)(2,1)}, u32[]{:S(2)}, u32[]{:S(2)}) collective-permute-start(bf16[768,512]{1,0:T(8,128)(2,1)S(1)} %fusion.18), channel_id=1, source_target_pairs={{1,0},{2,1},{3,2},{4,3},{5,4},{6,5},{7,6},{8,7},{9,8},{10,9},{11,1... | collective-permute-start | bytes 2359304 | tf_op jit(solution)/shard_map/ppermute | solution.py:63
  20.8 28.3 %collective-permute-start.2 = (bf16[768,512]{1,0:T(8,128)(2,1)S(1)}, bf16[768,512]{1,0:T(8,128)(2,1)S(1)}, u32[]{:S(2)}, u32[]{:S(2)}) collective-permute-start(bf16[768,512]{1,0:T(8,128)(2,1)S(1)} %fusion.18), channel_id=1, source_target_pairs={{255,0},{0,1},{1,2},{2,3},{3,4},{4,5},{5,6},{6,7},{7,8},{8,9},{9,1... | collective-permute-start | bytes 2359304 | tf_op jit(solution)/shard_map/ppermute | solution.py:63
  21.0 6.0 %copy-start = (bf16[768,512]{1,0:T(8,128)(2,1)S(1)}, bf16[768,512]{1,0:T(8,128)(2,1)}, u32[]{:S(2)}) copy-start(bf16[768,512]{1,0:T(8,128)(2,1)} %param.2) | copy-start | bytes 2359300
  28.4 30.7 %collective-permute-start.7 = (bf16[768,512]{1,0:T(8,128)(2,1)S(1)}, bf16[768,512]{1,0:T(8,128)(2,1)S(1)}, u32[]{:S(2)}, u32[]{:S(2)}) collective-permute-start(bf16[768,512]{1,0:T(8,128)(2,1)S(1)} %select_select_fusion), channel_id=1, source_target_pairs={{47,0},{0,1},{1,2},{2,3},{3,4},{4,5},{5,6},{6,7},{231,8},{8,9},{9,... | collective-permute-start | bytes 2359304 | tf_op jit(solution)/shard_map/ppermute | solution.py:63
  50.4 9.5 %collective-permute-start.6 = (bf16[768,512]{1,0:T(8,128)(2,1)S(1)}, bf16[768,512]{1,0:T(8,128)(2,1)S(1)}, u32[]{:S(2)}, u32[]{:S(2)}) collective-permute-start(bf16[768,512]{1,0:T(8,128)(2,1)S(1)} %broadcast_select_fusion), channel_id=1, source_target_pairs={{16,0},{17,1},{18,2},{19,3},{20,4},{21,5},{22,6},{23,7},{24,8},{25... | collective-permute-start | bytes 2359304 | tf_op jit(solution)/shard_map/ppermute | solution.py:63
  60.8 19.1 %collective-permute-start.8 = (f32[768]{0:T(1024)S(1)}, f32[768]{0:T(1024)S(1)}, u32[]{:S(2)}, u32[]{:S(2)}) collective-permute-start(f32[768]{0:T(1024)S(1)} %get-tuple-element.10), channel_id=1, source_target_pairs={{64,0},{65,1},{66,2},{67,3},{68,4},{69,5},{70,6},{71,7},{72,8},{73... | collective-permute-start | bytes 9224 | tf_op jit(solution)/shard_map/ppermute | solution.py:63
  63.2 16.7 %collective-permute-start.9 = (f32[768]{0:T(1024)S(1)}, f32[768]{0:T(1024)S(1)}, u32[]{:S(2)}, u32[]{:S(2)}) collective-permute-start(f32[768]{0:T(1024)S(1)} %get-tuple-element.10), channel_id=1, source_target_pairs={{192,0},{193,1},{194,2},{195,3},{196,4},{197,5},{198,6},{199,7},{2... | collective-permute-start | bytes 9224 | tf_op jit(solution)/shard_map/ppermute | solution.py:63
  63.2 6.1 %collective-permute-start.10 = (f32[768]{0:T(1024)S(1)}, f32[768]{0:T(1024)S(1)}, u32[]{:S(2)}, u32[]{:S(2)}) collective-permute-start(f32[768]{0:T(1024)S(1)} %get-tuple-element.10), channel_id=1, source_target_pairs={{1,0},{2,1},{3,2},{4,3},{5,4},{6,5},{7,6},{8,7},{9,8},{10,9},{11,1... | collective-permute-start | bytes 9224 | tf_op jit(solution)/shard_map/ppermute | solution.py:63
  68.3 5.1 %collective-permute-start.11 = (f32[768]{0:T(1024)S(1)}, f32[768]{0:T(1024)S(1)}, u32[]{:S(2)}, u32[]{:S(2)}) collective-permute-start(f32[768]{0:T(1024)S(1)} %get-tuple-element.10), channel_id=1, source_target_pairs={{255,0},{0,1},{1,2},{2,3},{3,4},{4,5},{5,6},{6,7},{7,8},{8,9},{9,1... | collective-permute-start | bytes 9224 | tf_op jit(solution)/shard_map/ppermute | solution.py:63
  73.4 13.8 %collective-permute-start.12 = (f32[3,768]{1,0:T(4,128)S(1)}, f32[3,768]{1,0:T(4,128)S(1)}, u32[]{:S(2)}, u32[]{:S(2)}) collective-permute-start(f32[3,768]{1,0:T(4,128)S(1)} %pad_maximum_fusion), channel_id=1, source_target_pairs={{16,0},{17,1},{18,2},{19,3},{20,4},{21,5},{22,6},{23,7},{24,8},{25... | collective-permute-start | bytes 27656 | tf_op jit(solution)/shard_map/ppermute | solution.py:63
  79.9 7.4 %collective-permute-start.13 = (f32[3,768]{1,0:T(4,128)S(1)}, f32[3,768]{1,0:T(4,128)S(1)}, u32[]{:S(2)}, u32[]{:S(2)}) collective-permute-start(f32[3,768]{1,0:T(4,128)S(1)} %pad_maximum_fusion), channel_id=1, source_target_pairs={{240,0},{241,1},{242,2},{243,3},{244,4},{245,5},{246,6},{247,7},{2... | collective-permute-start | bytes 27656 | tf_op jit(solution)/shard_map/ppermute | solution.py:63

commit v2 on v1

v2 whole, which is shorter than its diff:
```python
import functools

import jax
import jax.numpy as jnp
from jax import lax
from jax.experimental import pallas as pl
from jax.experimental.pallas import tpu as pltpu
from jax.sharding import PartitionSpec as P

inverse_temp = 5.0
epsilon = 1e-06
both = ("row", "col")
lanes = 128
chunk = 256


def routes(rows, cols):
    count = rows * cols
    far_step = cols
    x_step = count // 4
    line = cols // 2

    def wrap(value):
        return value % count

    def core(b):
        return (b // cols) % 2

    def half(b):
        return (b // (2 * cols)) % 2

    def far17(b):
        j = b % cols
        if core(b) == 0:
            if j == 0:
                return wrap(b + (2 * cols if half(b) == 0 else -2 * cols) + cols - 1)
            return wrap(b - 2 * cols - 1) if j == cols // 2 else b - 1
        if j == cols - 1:
            return wrap(b + (2 * cols if half(b) == 0 else -2 * cols) - cols + 1)
        return wrap(b + 2 * cols + 1) if j == cols // 2 - 1 else b + 1

    def ring(step):
        return lambda b: b - b % line + (b + step) % line

    def turn(b):
        return wrap(b + 1) if (b + 1) % line == 0 else wrap(b - 1) if b % line == 0 else b

    def turn_source(b):
        taken = turn(b)
        if taken == b:
            return b
        return taken + line - 1 if taken % line == 0 else taken - line + 1

    sources = {
        "above": lambda b: wrap(b + 1),
        "below": lambda b: wrap(b - 1),
        "ring_above": ring(1),
        "ring_below": ring(-1),
        "turn": turn_source,
        "x_above": lambda b: wrap(b + x_step),
        "x_below": lambda b: wrap(b - x_step),
        "near": lambda b: b + far_step if core(b) == 0 else b - far_step,
        "far": lambda b: wrap(b - far_step if core(b) == 0 else b + far_step),
        "far17": far17,
    }
    return {name: [(source(b), b) for b in range(count)] for name, source in sources.items()}


vmem_limit = 5 * 1024 * 1024
held = pl.BlockSpec(memory_space=pltpu.VMEM)
small = pl.BlockSpec(memory_space=pltpu.VMEM)
anywhere = pl.BlockSpec(memory_space=pl.ANY)


def hold(*arrays):
    return [pltpu.with_memory_space_constraint(array, pltpu.VMEM) for array in arrays]


def call(kernel, name, in_specs, out_specs, out_shape, flops, moved, exps=0, scratch=()):
    return pl.pallas_call(
        kernel,
        in_specs=in_specs,
        out_specs=out_specs,
        out_shape=out_shape,
        scratch_shapes=scratch,
        compiler_params=pltpu.CompilerParams(vmem_limit_bytes=vmem_limit),
        cost_estimate=pl.CostEstimate(flops=flops, bytes_accessed=moved, transcendentals=exps),
        name=name,
    )


def parts(rows):
    return [slice(start, start + chunk) for start in range(0, rows, chunk)]


def normalize_kernel(rows_ref, out_ref, held_ref, sems):
    rows = rows_ref.shape[0]
    copies = []
    for number, part in enumerate(parts(rows)):
        copy = pltpu.make_async_copy(rows_ref.at[part], held_ref.at[part], sems.at[number])
        copy.start()
        copies.append(copy)
    for copy, part in zip(copies, parts(rows)):
        copy.wait()
        wide = held_ref[part, :].astype(jnp.float32)
        scale = lax.rsqrt(jnp.sum(wide * wide, axis=-1, keepdims=True) + epsilon)
        out_ref[part, :] = (wide * scale).astype(jnp.bfloat16)


def normalize(embeddings):
    rows, width = embeddings.shape
    return call(
        normalize_kernel,
        "normalize",
        [anywhere],
        held,
        pltpu.VMEM((rows, width), jnp.bfloat16),
        4 * rows * width,
        4 * rows * width,
        scratch=[
            pltpu.VMEM((rows, width), jnp.bfloat16),
            pltpu.SemaphoreType.DMA((rows // chunk,)),
        ],
    )(pltpu.with_memory_space_constraint(embeddings, pltpu.HBM))


def exps_of(mine, theirs):
    scores = lax.dot_general(
        mine, theirs, (((1,), (1,)), ((), ())), preferred_element_type=jnp.float32
    )
    return jnp.exp(scores * inverse_temp)


def fold(exps):
    total = exps[:, :lanes]
    for start in range(lanes, exps.shape[1], lanes):
        total = total + exps[:, start : start + lanes]
    return total


def self_kernel(mine_ref, pos_ref, exps_ref, sums_ref, matched_ref):
    rows = mine_ref.shape[0]
    pairs = [pos_ref[number : number + 1, :] for number in range(rows // lanes)]
    partners = jnp.concatenate(pairs, axis=1)
    for part in parts(rows):
        k = lax.broadcasted_iota(jnp.int32, (chunk, rows), 0) + part.start
        j = lax.broadcasted_iota(jnp.int32, (chunk, rows), 1)
        exps = jnp.where(k == j, 0.0, exps_of(mine_ref[part, :], mine_ref[...]))
        exps_ref[part, :] = exps.astype(jnp.bfloat16)
        sums_ref[part, :] = fold(exps)
        picks = jnp.where(k == partners, 1.0, 0.0).astype(jnp.bfloat16)
        matched = jnp.dot(picks, mine_ref[...], preferred_element_type=jnp.float32)
        matched_ref[part, :] = matched.astype(jnp.bfloat16)


def self_tile(normed, positives):
    rows, width = normed.shape
    return call(
        self_kernel,
        "self_tile",
        [held, small],
        [held] * 3,
        [
            pltpu.VMEM((rows, rows), jnp.bfloat16),
            pltpu.VMEM((rows, lanes), jnp.float32),
            pltpu.VMEM((rows, width), jnp.bfloat16),
        ],
        4 * rows * rows * width,
        4 * rows * width + 2 * rows * rows,
        rows * rows,
    )(*hold(normed), positives)


def tile_kernel(mine_ref, theirs_ref, before_ref, exps_ref, sums_ref):
    for part in parts(mine_ref.shape[0]):
        exps = exps_of(mine_ref[part, :], theirs_ref[...])
        exps_ref[part, :] = exps.astype(jnp.bfloat16)
        sums_ref[part, :] = before_ref[part, :] + fold(exps)


def pair_tile(normed, block, sums):
    rows, width = normed.shape
    return call(
        tile_kernel,
        "pair_tile",
        [held] * 3,
        [held] * 2,
        [pltpu.VMEM((rows, rows), jnp.bfloat16), pltpu.VMEM((rows, lanes), jnp.float32)],
        2 * rows * rows * width,
        4 * rows * width + 2 * rows * rows,
        rows * rows,
    )(*hold(normed, block, sums))


def last_kernel(mine_ref, theirs_ref, before_ref, exps_ref, sums_ref, denoms_ref):
    for part in parts(mine_ref.shape[0]):
        exps = exps_of(mine_ref[part, :], theirs_ref[...])
        exps_ref[part, :] = exps.astype(jnp.bfloat16)
        sums = before_ref[part, :] + fold(exps)
        sums_ref[part, :] = sums
        denoms_ref[:, part] = jnp.sum(sums.T, axis=0, keepdims=True)


def last_tile(normed, block, sums):
    rows, width = normed.shape
    return call(
        last_kernel,
        "last_tile",
        [held] * 3,
        [held] * 3,
        [
            pltpu.VMEM((rows, rows), jnp.bfloat16),
            pltpu.VMEM((rows, lanes), jnp.float32),
            pltpu.VMEM((1, rows), jnp.float32),
        ],
        2 * rows * rows * width,
        4 * rows * width + 2 * rows * rows,
        rows * rows,
    )(*hold(normed, block, sums))


def far17_kernel(far_ref, near_ref, mine_ref, x_below_ref, x_above_ref, out_ref):
    cols, col = lax.axis_size("col"), lax.axis_index("col")
    row = lax.axis_index("row")
    core0 = row % 2 == 0
    half0 = (row // 2) % 2 == 0
    last = col == jnp.where(core0, cols - 1, 0)
    turn = col == jnp.where(core0, cols // 2 - 1, cols // 2)
    crossing = last & (core0 != half0)
    choices = [
        (crossing & core0, x_below_ref),
        (crossing & ~core0, x_above_ref),
        (last & ~crossing, mine_ref),
        (turn, near_ref),
        (~last & ~turn, far_ref),
    ]
    for chosen, ref in choices:

        @pl.when(chosen)
        def _():
            out_ref[...] = ref[...]


def turn_kernel(above_ref, below_ref, out_ref):
    line = lax.axis_size("col") // 2
    place = lax.axis_index("col") % line

    @pl.when(place == line - 1)
    def _():
        out_ref[...] = above_ref[...]

    @pl.when(place == 0)
    def _():
        out_ref[...] = below_ref[...]


def merge_kernel(shift, ring_ref, turn_ref, out_ref):
    turns = (lax.axis_index("col") + shift) % (lax.axis_size("col") // 2) == 0

    @pl.when(turns)
    def _():
        out_ref[...] = turn_ref[...]

    @pl.when(~turns)
    def _():
        out_ref[...] = ring_ref[...]


def near17_kernel(below_ref, above_ref, out_ref):
    core0 = lax.axis_index("row") % 2 == 0

    @pl.when(core0)
    def _():
        out_ref[...] = below_ref[...]

    @pl.when(~core0)
    def _():
        out_ref[...] = above_ref[...]


def choose(kernel, name, *choices):
    shape = choices[0].shape
    return call(
        kernel,
        name,
        [held] * len(choices),
        held,
        pltpu.VMEM(shape, jnp.bfloat16),
        0,
        4 * shape[0] * shape[1],
    )(*hold(*choices))


def weighted(sums_ref, others, exps_refs, block_refs, part):
    mine = 1.0 / jnp.sum(sums_ref[part, :], axis=1, keepdims=True)
    total = None
    for other, exps_ref, block_ref in zip(others, exps_refs, block_refs):
        weights = exps_ref[part, :].astype(jnp.float32) * (mine + other)
        term = jnp.dot(
            weights.astype(jnp.bfloat16), block_ref[...], preferred_element_type=jnp.float32
        )
        total = term if total is None else total + term
    return total


def first_kernel(count, sums_ref, matched_ref, *refs):
    exps_refs, block_refs = refs[:count], refs[count : 2 * count]
    norm_refs, out_ref = refs[2 * count : 3 * count], refs[3 * count]
    others = [1.0 / norm_ref[...] for norm_ref in norm_refs]
    for part in parts(sums_ref.shape[0]):
        total = weighted(sums_ref, others, exps_refs, block_refs, part)
        out_ref[part, :] = total - 2.0 * matched_ref[part, :].astype(jnp.float32)


def final_kernel(count, sums_ref, first_ref, *refs):
    exps_refs, block_refs = refs[:count], refs[count : 2 * count]
    near_ref, far_ref, out_ref, held_ref, sems = refs[2 * count :]
    core0 = lax.axis_index("row") % 2 == 0
    near17 = jnp.where(core0, near_ref[1:2, :], near_ref[2:3, :])
    far17 = jnp.where(core0, far_ref[2:3, :], far_ref[1:2, :])
    others = [1.0 / norm for norm in (near_ref[0:1, :], far_ref[0:1, :], near17, far17)]
    copies = []
    for number, part in enumerate(parts(sums_ref.shape[0])):
        total = weighted(sums_ref, others, exps_refs, block_refs, part)
        held_ref[part, :] = inverse_temp * (first_ref[part, :] + total)
        copy = pltpu.make_async_copy(held_ref.at[part], out_ref.at[part], sems.at[number])
        copy.start()
        copies.append(copy)
    for copy in copies:
        copy.wait()


def gather_first(sums, matched, exps, blocks, norms):
    count, (rows, width) = len(exps), matched.shape
    return call(
        functools.partial(first_kernel, count),
        "gather_first",
        [held] * (3 * count + 2),
        held,
        pltpu.VMEM((rows, width), jnp.float32),
        2 * count * rows * rows * width,
        count * 2 * rows * (rows + width) + 8 * rows * width,
    )(*hold(sums, matched, *exps, *blocks, *norms))


def gather_final(sums, first, exps, blocks, near_trio, far_trio):
    count, (rows, width) = len(exps), first.shape
    return call(
        functools.partial(final_kernel, count),
        "gather_final",
        [held] * (2 * count + 4),
        anywhere,
        jax.ShapeDtypeStruct((rows, width), jnp.float32),
        2 * count * rows * rows * width,
        count * 2 * rows * (rows + width) + 8 * rows * width,
        scratch=[
            pltpu.VMEM((rows, width), jnp.float32),
            pltpu.SemaphoreType.DMA((rows // chunk,)),
        ],
    )(*hold(sums, first, *exps, *blocks, near_trio, far_trio))


def join_kernel(*refs):
    *parts_refs, out_ref = refs
    for number, ref in enumerate(parts_refs):
        out_ref[number : number + 1, :] = ref[...]


def join(*rows):
    width = rows[0].shape[1]
    return call(
        join_kernel,
        "join",
        [held] * len(rows),
        held,
        pltpu.VMEM((len(rows), width), jnp.float32),
        0,
        8 * len(rows) * width,
    )(*hold(*rows))


def on_device(embeddings, positives):
    rows, cols = lax.axis_size("row"), lax.axis_size("col")
    route = routes(rows, cols)

    def send(block, name):
        return lax.ppermute(block, both, route[name])

    normed = normalize(embeddings)
    near = send(normed, "near")
    ring_above = send(normed, "ring_above")
    ring_below = send(normed, "ring_below")
    far = send(normed, "far")
    x_below = send(normed, "x_below")
    self_exps, sums, matched = self_tile(normed, positives.reshape(-1, lanes))
    later, near, sums = lax.optimization_barrier((normed, near, sums))
    x_above = send(later, "x_above")
    turn = send(choose(turn_kernel, "turn", ring_above, ring_below), "turn")
    passed = choose(far17_kernel, "far17", far, near, normed, x_below, x_above)
    far17 = send(passed, "far17")
    exps, blocks = {}, {}

    def add(sums, **some):
        for name, block in some.items():
            blocks[name] = block
            exps[name], sums = pair_tile(normed, block, sums)
        return sums

    sums = add(sums, near=near, far=far, x_below=x_below, x_above=x_above)
    turn, sums = lax.optimization_barrier((turn, sums))
    above = choose(functools.partial(merge_kernel, 1), "above", ring_above, turn)
    below = choose(functools.partial(merge_kernel, 0), "below", ring_below, turn)
    near17 = send(choose(near17_kernel, "near17", below, above), "near")
    sums = add(sums, above=above, below=below, far17=far17)
    blocks["near17"] = near17
    exps["near17"], sums, denoms = last_tile(normed, near17, sums)

    d_above = send(denoms, "above")
    d_below = send(denoms, "below")
    d_x_above = send(denoms, "x_above")
    d_x_below = send(denoms, "x_below")
    trio = join(denoms, d_above, d_below)
    near_trio = send(trio, "near")
    far_trio = send(trio, "far")

    names = ["above", "below", "x_above", "x_below"]
    first = gather_first(
        sums,
        matched,
        [self_exps] + [exps[name] for name in names],
        [normed] + [blocks[name] for name in names],
        [denoms, d_above, d_below, d_x_above, d_x_below],
    )
    names = ["near", "far", "near17", "far17"]
    return gather_final(
        sums,
        first,
        [exps[name] for name in names],
        [blocks[name] for name in names],
        near_trio,
        far_trio,
    )


def solution(mesh):
    placed = (P(("row", "col"), None), P(("row", "col")))
    return jax.shard_map(
        on_device, mesh=mesh, in_specs=placed, out_specs=P(("row", "col"), None), check_vma=False
    )
```

time: 93.2 us -> 78.4 us (0.84)
  matrix products: 24.5 us -> 0 us
  Pallas kernels: 0 us -> 17 us
  waiting for transfers between devices: 9.25 us -> 15.5 us
  other arithmetic: 5.55 us -> 0 us
  starting transfers between devices: 50.4 us -> 45.1 us
  local copies, waits for them, and re-layouts: 2.7 us -> 0.01 us
    dot_general x18 -> x0, matrix products: 24.5 us -> none  [the longest x8 12.7 us: on_device(): jnp.dot(weights, blocks[number], preferred_element_type=jnp.float32)]
    pallas_call x0 -> x18, Pallas kernels: none -> 17 us  [the longest x7 5.9 us: pair_tile(): call(tile_kernel, 'pair_tile', [held] * 3, [held] * 2, [pltpu.VMEM((rows,...]
    ppermute x14 -> x15, waiting for transfers between devices: 9.25 us -> 15.5 us  [send(): return lax.ppermute(block, both, route[name])]
    ppermute x14 -> x15, starting transfers between devices: 50.4 us -> 45.1 us  [send(): return lax.ppermute(block, both, route[name])]
    select_n x3 -> x0, other arithmetic: 2.7 us -> none  [the longest x1 1.45 us: on_device(): jnp.where(col == last, jnp.where(crossing, jnp.where(core0, x_below, x_ab...]
    gather x1 -> x0, local copies, waits for them, and re-layouts: 2.68 us -> none  [on_device(): matched = jnp.take(normed, positives, axis=0).astype(jnp.float32)]
    reduce_sum x1 -> x0, other arithmetic: 1.37 us -> none  [on_device(): jnp.sum(wide * wide, axis=-1, keepdims=True) + epsilon]
    convert_element_type x1 -> x0, other arithmetic: 1.36 us -> none  [on_device(): (wide * lax.rsqrt(jnp.sum(wide * wide, axis=-1, keepdims=True) + epsilon)...]
  transfers between devices with their start and end apart: 14 -> 15, of which waited for: 3 -> 4; matrix products, arithmetic and copies ran while one was open for 26% -> 0% of each run, Pallas kernels for 0% -> 14%
where the time goes in v2:
time: 78.4 us; the launch traced here: 78 us
  starting transfers between devices  45.1 us (58%)
  Pallas kernels  17 us (22%)
  waiting for transfers between devices  15.5 us (20%)
    ppermute x15, starting transfers between devices, send(): return lax.ppermute(block, both, route[name])  45.1 us
    ppermute x15, waiting for transfers between devices, send(): return lax.ppermute(block, both, route[name])  15.5 us
    pallas_call x7, Pallas kernels, pair_tile(): call(tile_kernel, 'pair_tile', [held] * 3, [held] * 2, [pltpu.VMEM((rows,...  5.9 us
    pallas_call x1, Pallas kernels, gather_final(): call(functools.partial(final_kernel, count), 'gather_final', [held] * (2...  3.53 us
    pallas_call x1, Pallas kernels, gather_first(): call(functools.partial(first_kernel, count), 'gather_first', [held] * (3...  3.38 us
  transfers between devices with their start and end apart: 15, of which 4 were waited for; matrix products, arithmetic and copies ran while one was open for 0% of the time, Pallas kernels for 14%

profile of v2, /device:TPU:1, one launch (start us, length us, event | category | flops | bytes accessed | tf_op | source)
XLA Modules:
  0.0 78.0 jit_solution(18110458919052247284)
XLA Ops:
  0.0 0.0 copy-start
  0.0 1.4 %normalize.1.mine_ref.refs_5_ = bf16[768,512]{1,0:T(8,128)(2,1)S(1)} custom-call(bf16[768,512]{1,0:T(8,128)(2,1)} %rows_ref.1), custom_call_target="tpu_custom_call" | custom-call | flops 1572864 | bytes 1572864 | tf_op jit(solution)/shard_map/normalize/pallas_call | solution.py:112
  1.4 3.3 %collective-permute-start.3 = (bf16[768,512]{1,0:T(8,128)(2,1)S(1)}, bf16[768,512]{1,0:T(8,128)(2,1)S(1)}, u32[]{:S(2)}, u32[]{:S(2)}) collective-permute-start(bf16[768,512]{1,0:T(8,128)(2,1)S(1)} %normalize.1.mine_ref.refs_5_), channel_id=1, source_target_pairs={{16,0},{17,1},{18,2},{19,3},{20,4},{21,5},{22,6},{23,7},{24,8},{25... | collective-permute-start | bytes 2359304 | tf_op jit(solution)/shard_map/ppermute | solution.py:387
  4.7 3.9 %collective-permute-start.1 = (bf16[768,512]{1,0:T(8,128)(2,1)S(1)}, bf16[768,512]{1,0:T(8,128)(2,1)S(1)}, u32[]{:S(2)}, u32[]{:S(2)}) collective-permute-start(bf16[768,512]{1,0:T(8,128)(2,1)S(1)} %normalize.1.mine_ref.refs_5_), channel_id=1, source_target_pairs={{1,0},{2,1},{3,2},{4,3},{5,4},{6,5},{7,6},{0,7},{9,8},{10,9},{11,1... | collective-permute-start | bytes 2359304 | tf_op jit(solution)/shard_map/ppermute | solution.py:387
  8.6 0.0 collective-permute-start
  8.6 3.2 %collective-permute-start.6 = (bf16[768,512]{1,0:T(8,128)(2,1)S(1)}, bf16[768,512]{1,0:T(8,128)(2,1)S(1)}, u32[]{:S(2)}, u32[]{:S(2)}) collective-permute-start(bf16[768,512]{1,0:T(8,128)(2,1)S(1)} %normalize.1.mine_ref.refs_5_), channel_id=1, source_target_pairs={{240,0},{241,1},{242,2},{243,3},{244,4},{245,5},{246,6},{247,7},{2... | collective-permute-start | bytes 2359304 | tf_op jit(solution)/shard_map/ppermute | solution.py:387
  11.7 1.2 %collective-permute-start.5 = (bf16[768,512]{1,0:T(8,128)(2,1)S(1)}, bf16[768,512]{1,0:T(8,128)(2,1)S(1)}, u32[]{:S(2)}, u32[]{:S(2)}) collective-permute-start(bf16[768,512]{1,0:T(8,128)(2,1)S(1)} %normalize.1.mine_ref.refs_5_), channel_id=1, source_target_pairs={{192,0},{193,1},{194,2},{195,3},{196,4},{197,5},{198,6},{199,7},{2... | collective-permute-start | bytes 2359304 | tf_op jit(solution)/shard_map/ppermute | solution.py:387
  13.0 0.0 copy-done
  13.0 1.5 %self_tile.1 = (bf16[768,768]{1,0:T(8,128)(2,1)S(1)}, f32[768,128]{1,0:T(8,128)S(1)}, bf16[768,512]{1,0:T(8,128)(2,1)S(1)}) custom-call(bf16[768,512]{1,0:T(8,128)(2,1)S(1)} %normalize.1.mine_ref.refs_5_, s32[6,128]{1,0:T(8,128)S(1)} %bitcast.1), custom_call_target="tpu_custom_call" | custom-call | flops 1207959552 | bytes 2752512 | tf_op jit(solution)/shard_map/self_tile/pallas_call | solution.py:158
  14.5 0.0 collective-permute-done.3.theirs_ref.near_ref.refs_4_
  14.5 1.5 %collective-permute-start.4 = (bf16[768,512]{1,0:T(8,128)(2,1)S(1)}, bf16[768,512]{1,0:T(8,128)(2,1)S(1)}, u32[]{:S(2)}, u32[]{:S(2)}) collective-permute-start(bf16[768,512]{1,0:T(8,128)(2,1)S(1)} %normalize.1.mine_ref.refs_5_), channel_id=1, source_target_pairs={{64,0},{65,1},{66,2},{67,3},{68,4},{69,5},{70,6},{71,7},{72,8},{73... | collective-permute-start | bytes 2359304 | tf_op jit(solution)/shard_map/ppermute | solution.py:387
  16.1 9.4 %collective-permute-done.1.above_ref.ring_ref = bf16[768,512]{1,0:T(8,128)(2,1)S(1)} collective-permute-done((bf16[768,512]{1,0:T(8,128)(2,1)S(1)}, bf16[768,512]{1,0:T(8,128)(2,1)S(1)}, u32[]{:S(2)}, u32[]{:S(2)}) %collective-permute-start.1) | collective-permute-done | bytes 786464 | tf_op jit(solution)/shard_map/ppermute | solution.py:387
  25.5 3.1 %collective-permute-done.below_ref.ring_ref = bf16[768,512]{1,0:T(8,128)(2,1)S(1)} collective-permute-done((bf16[768,512]{1,0:T(8,128)(2,1)S(1)}, bf16[768,512]{1,0:T(8,128)(2,1)S(1)}, u32[]{:S(2)}, u32[]{:S(2)}) %collective-permute-start) | collective-permute-done | bytes 786464 | tf_op jit(solution)/shard_map/ppermute | solution.py:387
  28.6 0.1 turn.1
  28.6 3.2 %collective-permute-start.2 = (bf16[768,512]{1,0:T(8,128)(2,1)S(1)}, bf16[768,512]{1,0:T(8,128)(2,1)S(1)}, u32[]{:S(2)}, u32[]{:S(2)}) collective-permute-start(bf16[768,512]{1,0:T(8,128)(2,1)S(1)} %turn.1), channel_id=1, source_target_pairs={{248,0},{1,1},{2,2},{3,3},{4,4},{5,5},{6,6},{15,7},{0,8},{9,9},{10... | collective-permute-start | bytes 2359304 | tf_op jit(solution)/shard_map/ppermute | solution.py:387
  31.8 0.8 %pair_tile.7 = (bf16[768,768]{1,0:T(8,128)(2,1)S(1)}, f32[768,128]{1,0:T(8,128)S(1)}) custom-call(bf16[768,512]{1,0:T(8,128)(2,1)S(1)} %normalize.1.mine_ref.refs_5_, bf16[768,512]{1,0:T(8,128)(2,1)S(1)} %collective-permute-done.3.theirs_ref.near_ref.refs_4_, f32[768,128]{1,0:T(8,128)S(1)} %get-tuple-element.33.before_ref), custom_call_target="tpu_custom_call" | custom-call | flops 603979776 | bytes 2752512 | tf_op jit(solution)/shard_map/pair_tile/pallas_call | solution.py:183
  32.7 0.0 collective-permute-done.6.theirs_ref.far_ref.refs_5_
  32.7 0.8 %pair_tile.8 = (bf16[768,768]{1,0:T(8,128)(2,1)S(1)}, f32[768,128]{1,0:T(8,128)S(1)}) custom-call(bf16[768,512]{1,0:T(8,128)(2,1)S(1)} %normalize.1.mine_ref.refs_5_, bf16[768,512]{1,0:T(8,128)(2,1)S(1)} %collective-permute-done.6.theirs_ref.far_ref.refs_5_, f32[768,128]{1,0:T(8,128)S(1)} %get-tuple-element.34.before_ref), custom_call_target="tpu_custom_call" | custom-call | flops 603979776 | bytes 2752512 | tf_op jit(solution)/shard_map/pair_tile/pallas_call | solution.py:183
  33.5 0.0 collective-permute-done.5.theirs_ref.x_below_ref.refs_9_
  33.6 0.8 %pair_tile.9 = (bf16[768,768]{1,0:T(8,128)(2,1)S(1)}, f32[768,128]{1,0:T(8,128)S(1)}) custom-call(bf16[768,512]{1,0:T(8,128)(2,1)S(1)} %normalize.1.mine_ref.refs_5_, bf16[768,512]{1,0:T(8,128)(2,1)S(1)} %collective-permute-done.5.theirs_ref.x_below_ref.refs_9_, f32[768,128]{1,0:T(8,128)S(1)} %get-tuple-element.35.before_ref), custom_call_target="tpu_custom_call" | custom-call | flops 603979776 | bytes 2752512 | tf_op jit(solution)/shard_map/pair_tile/pallas_call | solution.py:183
  34.4 0.0 collective-permute-done.4.theirs_ref.x_above_ref.refs_8_
  34.4 0.1 far17.1
  34.5 10.3 %collective-permute-start.8 = (bf16[768,512]{1,0:T(8,128)(2,1)S(1)}, bf16[768,512]{1,0:T(8,128)(2,1)S(1)}, u32[]{:S(2)}, u32[]{:S(2)}) collective-permute-start(bf16[768,512]{1,0:T(8,128)(2,1)S(1)} %far17.1), channel_id=1, source_target_pairs={{47,0},{0,1},{1,2},{2,3},{3,4},{4,5},{5,6},{6,7},{231,8},{8,9},{9,... | collective-permute-start | bytes 2359304 | tf_op jit(solution)/shard_map/ppermute | solution.py:387
  44.9 0.8 %pair_tile.10 = (bf16[768,768]{1,0:T(8,128)(2,1)S(1)}, f32[768,128]{1,0:T(8,128)S(1)}) custom-call(bf16[768,512]{1,0:T(8,128)(2,1)S(1)} %normalize.1.mine_ref.refs_5_, bf16[768,512]{1,0:T(8,128)(2,1)S(1)} %collective-permute-done.4.theirs_ref.x_above_ref.refs_8_, f32[768,128]{1,0:T(8,128)S(1)} %get-tuple-element.36.before_ref), custom_call_target="tpu_custom_call" | custom-call | flops 603979776 | bytes 2752512 | tf_op jit(solution)/shard_map/pair_tile/pallas_call | solution.py:183
  45.7 1.8 %collective-permute-done.2.turn_ref = bf16[768,512]{1,0:T(8,128)(2,1)S(1)} collective-permute-done((bf16[768,512]{1,0:T(8,128)(2,1)S(1)}, bf16[768,512]{1,0:T(8,128)(2,1)S(1)}, u32[]{:S(2)}, u32[]{:S(2)}) %collective-permute-start.2) | collective-permute-done | bytes 786464 | tf_op jit(solution)/shard_map/ppermute | solution.py:387
  47.5 0.1 above.1.above_ref.theirs_ref.refs_6_
  47.5 0.1 below.1.below_ref.theirs_ref.refs_7_
  47.6 0.1 near17.1
  47.7 5.3 %collective-permute-start.7 = (bf16[768,512]{1,0:T(8,128)(2,1)S(1)}, bf16[768,512]{1,0:T(8,128)(2,1)S(1)}, u32[]{:S(2)}, u32[]{:S(2)}) collective-permute-start(bf16[768,512]{1,0:T(8,128)(2,1)S(1)} %near17.1), channel_id=1, source_target_pairs={{16,0},{17,1},{18,2},{19,3},{20,4},{21,5},{22,6},{23,7},{24,8},{25... | collective-permute-start | bytes 2359304 | tf_op jit(solution)/shard_map/ppermute | solution.py:387
  53.0 0.8 %pair_tile.11 = (bf16[768,768]{1,0:T(8,128)(2,1)S(1)}, f32[768,128]{1,0:T(8,128)S(1)}) custom-call(bf16[768,512]{1,0:T(8,128)(2,1)S(1)} %normalize.1.mine_ref.refs_5_, bf16[768,512]{1,0:T(8,128)(2,1)S(1)} %above.1.above_ref.theirs_ref.refs_6_, f32[768,128]{1,0:T(8,128)S(1)} %get-tuple-element.39.before_ref), custom_call_target="tpu_custom_call" | custom-call | flops 603979776 | bytes 2752512 | tf_op jit(solution)/shard_map/pair_tile/pallas_call | solution.py:183
  53.8 0.9 %pair_tile.12 = (bf16[768,768]{1,0:T(8,128)(2,1)S(1)}, f32[768,128]{1,0:T(8,128)S(1)}) custom-call(bf16[768,512]{1,0:T(8,128)(2,1)S(1)} %normalize.1.mine_ref.refs_5_, bf16[768,512]{1,0:T(8,128)(2,1)S(1)} %below.1.below_ref.theirs_ref.refs_7_, f32[768,128]{1,0:T(8,128)S(1)} %get-tuple-element.40.before_ref), custom_call_target="tpu_custom_call" | custom-call | flops 603979776 | bytes 2752512 | tf_op jit(solution)/shard_map/pair_tile/pallas_call | solution.py:183
  54.7 1.2 %collective-permute-done.8.theirs_ref.refs_7_ = bf16[768,512]{1,0:T(8,128)(2,1)S(1)} collective-permute-done((bf16[768,512]{1,0:T(8,128)(2,1)S(1)}, bf16[768,512]{1,0:T(8,128)(2,1)S(1)}, u32[]{:S(2)}, u32[]{:S(2)}) %collective-permute-start.8) | collective-permute-done | bytes 786464 | tf_op jit(solution)/shard_map/ppermute | solution.py:387
  55.9 0.8 %pair_tile.13 = (bf16[768,768]{1,0:T(8,128)(2,1)S(1)}, f32[768,128]{1,0:T(8,128)S(1)}) custom-call(bf16[768,512]{1,0:T(8,128)(2,1)S(1)} %normalize.1.mine_ref.refs_5_, bf16[768,512]{1,0:T(8,128)(2,1)S(1)} %collective-permute-done.8.theirs_ref.refs_7_, f32[768,128]{1,0:T(8,128)S(1)} %get-tuple-element.41.before_ref), custom_call_target="tpu_custom_call" | custom-call | flops 603979776 | bytes 2752512 | tf_op jit(solution)/shard_map/pair_tile/pallas_call | solution.py:183
  56.7 0.0 collective-permute-done.7.theirs_ref.refs_6_
  56.7 0.9 %last_tile.1 = (bf16[768,768]{1,0:T(8,128)(2,1)S(1)}, f32[768,128]{1,0:T(8,128)S(1)}, f32[1,768]{1,0:T(1,128)S(1)}) custom-call(bf16[768,512]{1,0:T(8,128)(2,1)S(1)} %normalize.1.mine_ref.refs_5_, bf16[768,512]{1,0:T(8,128)(2,1)S(1)} %collective-permute-done.7.theirs_ref.refs_6_, f32[768,128]{1,0:T(8,128)S(1)} %get-tuple-element.42.before_ref), custom_call_target="tpu_custom_call" | custom-call | flops 603979776 | bytes 2752512 | tf_op jit(solution)/shard_map/last_tile/pallas_call | solution.py:206
  57.7 0.1 collective-permute-start.10
  57.8 3.8 %collective-permute-start.9 = (f32[1,768]{1,0:T(1,128)S(1)}, f32[1,768]{1,0:T(1,128)S(1)}, u32[]{:S(2)}, u32[]{:S(2)}) collective-permute-start(f32[1,768]{1,0:T(1,128)S(1)} %get-tuple-element.50.refs_10_.refs_0_), channel_id=1, source_target_pairs={{1,0},{2,1},{3,2},{4,3},{5,4},{6,5},{7,6},{8,7},{9,8},{10,9},{11,1... | collective-permute-start | bytes 9224 | tf_op jit(solution)/shard_map/ppermute | solution.py:387
  61.6 1.2 %collective-permute-start.12 = (f32[1,768]{1,0:T(1,128)S(1)}, f32[1,768]{1,0:T(1,128)S(1)}, u32[]{:S(2)}, u32[]{:S(2)}) collective-permute-start(f32[1,768]{1,0:T(1,128)S(1)} %get-tuple-element.50.refs_10_.refs_0_), channel_id=1, source_target_pairs={{192,0},{193,1},{194,2},{195,3},{196,4},{197,5},{198,6},{199,7},{2... | collective-permute-start | bytes 9224 | tf_op jit(solution)/shard_map/ppermute | solution.py:387
  62.8 2.4 %collective-permute-start.11 = (f32[1,768]{1,0:T(1,128)S(1)}, f32[1,768]{1,0:T(1,128)S(1)}, u32[]{:S(2)}, u32[]{:S(2)}) collective-permute-start(f32[1,768]{1,0:T(1,128)S(1)} %get-tuple-element.50.refs_10_.refs_0_), channel_id=1, source_target_pairs={{64,0},{65,1},{66,2},{67,3},{68,4},{69,5},{70,6},{71,7},{72,8},{73... | collective-permute-start | bytes 9224 | tf_op jit(solution)/shard_map/ppermute | solution.py:387
  65.3 0.0 collective-permute-done.10.refs_12_.refs_2_
  65.3 0.0 collective-permute-done.9.refs_11_.refs_1_
  65.3 0.1 collective-permute-start.14
  65.4 5.5 %collective-permute-start.13 = (f32[3,768]{1,0:T(4,128)S(1)}, f32[3,768]{1,0:T(4,128)S(1)}, u32[]{:S(2)}, u32[]{:S(2)}) collective-permute-start(f32[3,768]{1,0:T(4,128)S(1)} %join.1), channel_id=1, source_target_pairs={{16,0},{17,1},{18,2},{19,3},{20,4},{21,5},{22,6},{23,7},{24,8},{25... | collective-permute-start | bytes 27656 | tf_op jit(solution)/shard_map/ppermute | solution.py:387
  70.9 0.0 collective-permute-done.12.refs_14_
  70.9 0.0 collective-permute-done.11.refs_13_
  70.9 3.4 %gather_first.1.first_ref = f32[768,512]{1,0:T(8,128)S(1)} custom-call(f32[768,128]{1,0:T(8,128)S(1)} %get-tuple-element.43.sums_ref, bf16[768,512]{1,0:T(8,128)(2,1)S(1)} %get-tuple-element.44.matched_ref, bf16[768,768]{1,0:T(8,128)(2,1)S(1)} %get-tuple-element.45.refs_0_, bf16[768,768]{1,0:T(8,128)(2,1)S(1)} %get-tuple-element.46.refs_1_, ...), custom_call_target="tpu_custom_call" | custom-call | flops 3019898880 | bytes 12976128 | tf_op jit(solution)/shard_map/gather_first/pallas_call | solution.py:335
  74.3 0.0 collective-permute-done.14.refs_9_
  74.3 0.0 collective-permute-done.13.refs_8_
  74.3 3.5 %gather_final.1 = f32[768,512]{1,0:T(8,128)} custom-call(f32[768,128]{1,0:T(8,128)S(1)} %get-tuple-element.43.sums_ref, f32[768,512]{1,0:T(8,128)S(1)} %gather_first.1.first_ref, bf16[768,768]{1,0:T(8,128)(2,1)S(1)} %get-tuple-element.51.refs_0_, bf16[768,768]{1,0:T(8,128)(2,1)S(1)} %get-tuple-element.52.refs_1_, ...), custom_call_target="tpu_custom_call" | custom-call | flops 2415919104 | bytes 11010048 | tf_op jit(solution)/shard_map/gather_final/pallas_call | solution.py:348
  (1 shorter events, 0.0 us)
Async XLA Ops:
  0.0 13.0 %copy-start = (s32[768]{0:T(1024)S(1)}, s32[768]{0:T(1024)}, u32[]{:S(2)}) copy-start(s32[768]{0:T(1024)} %param.3) | copy-start | bytes 9220
  1.4 13.1 %collective-permute-start.3 = (bf16[768,512]{1,0:T(8,128)(2,1)S(1)}, bf16[768,512]{1,0:T(8,128)(2,1)S(1)}, u32[]{:S(2)}, u32[]{:S(2)}) collective-permute-start(bf16[768,512]{1,0:T(8,128)(2,1)S(1)} %normalize.1.mine_ref.refs_5_), channel_id=1, source_target_pairs={{16,0},{17,1},{18,2},{19,3},{20,4},{21,5},{22,6},{23,7},{24,8},{25... | collective-permute-start | bytes 2359304 | tf_op jit(solution)/shard_map/ppermute | solution.py:387
  4.7 20.7 %collective-permute-start.1 = (bf16[768,512]{1,0:T(8,128)(2,1)S(1)}, bf16[768,512]{1,0:T(8,128)(2,1)S(1)}, u32[]{:S(2)}, u32[]{:S(2)}) collective-permute-start(bf16[768,512]{1,0:T(8,128)(2,1)S(1)} %normalize.1.mine_ref.refs_5_), channel_id=1, source_target_pairs={{1,0},{2,1},{3,2},{4,3},{5,4},{6,5},{7,6},{0,7},{9,8},{10,9},{11,1... | collective-permute-start | bytes 2359304 | tf_op jit(solution)/shard_map/ppermute | solution.py:387
  8.6 20.0 %collective-permute-start = (bf16[768,512]{1,0:T(8,128)(2,1)S(1)}, bf16[768,512]{1,0:T(8,128)(2,1)S(1)}, u32[]{:S(2)}, u32[]{:S(2)}) collective-permute-start(bf16[768,512]{1,0:T(8,128)(2,1)S(1)} %normalize.1.mine_ref.refs_5_), channel_id=1, source_target_pairs={{7,0},{0,1},{1,2},{2,3},{3,4},{4,5},{5,6},{6,7},{15,8},{8,9},{9,10... | collective-permute-start | bytes 2359304 | tf_op jit(solution)/shard_map/ppermute | solution.py:387
  8.6 24.1 %collective-permute-start.6 = (bf16[768,512]{1,0:T(8,128)(2,1)S(1)}, bf16[768,512]{1,0:T(8,128)(2,1)S(1)}, u32[]{:S(2)}, u32[]{:S(2)}) collective-permute-start(bf16[768,512]{1,0:T(8,128)(2,1)S(1)} %normalize.1.mine_ref.refs_5_), channel_id=1, source_target_pairs={{240,0},{241,1},{242,2},{243,3},{244,4},{245,5},{246,6},{247,7},{2... | collective-permute-start | bytes 2359304 | tf_op jit(solution)/shard_map/ppermute | solution.py:387
  11.7 21.8 %collective-permute-start.5 = (bf16[768,512]{1,0:T(8,128)(2,1)S(1)}, bf16[768,512]{1,0:T(8,128)(2,1)S(1)}, u32[]{:S(2)}, u32[]{:S(2)}) collective-permute-start(bf16[768,512]{1,0:T(8,128)(2,1)S(1)} %normalize.1.mine_ref.refs_5_), channel_id=1, source_target_pairs={{192,0},{193,1},{194,2},{195,3},{196,4},{197,5},{198,6},{199,7},{2... | collective-permute-start | bytes 2359304 | tf_op jit(solution)/shard_map/ppermute | solution.py:387
  14.5 19.9 %collective-permute-start.4 = (bf16[768,512]{1,0:T(8,128)(2,1)S(1)}, bf16[768,512]{1,0:T(8,128)(2,1)S(1)}, u32[]{:S(2)}, u32[]{:S(2)}) collective-permute-start(bf16[768,512]{1,0:T(8,128)(2,1)S(1)} %normalize.1.mine_ref.refs_5_), channel_id=1, source_target_pairs={{64,0},{65,1},{66,2},{67,3},{68,4},{69,5},{70,6},{71,7},{72,8},{73... | collective-permute-start | bytes 2359304 | tf_op jit(solution)/shard_map/ppermute | solution.py:387
  28.6 18.8 %collective-permute-start.2 = (bf16[768,512]{1,0:T(8,128)(2,1)S(1)}, bf16[768,512]{1,0:T(8,128)(2,1)S(1)}, u32[]{:S(2)}, u32[]{:S(2)}) collective-permute-start(bf16[768,512]{1,0:T(8,128)(2,1)S(1)} %turn.1), channel_id=1, source_target_pairs={{248,0},{1,1},{2,2},{3,3},{4,4},{5,5},{6,6},{15,7},{0,8},{9,9},{10... | collective-permute-start | bytes 2359304 | tf_op jit(solution)/shard_map/ppermute | solution.py:387
  34.5 21.4 %collective-permute-start.8 = (bf16[768,512]{1,0:T(8,128)(2,1)S(1)}, bf16[768,512]{1,0:T(8,128)(2,1)S(1)}, u32[]{:S(2)}, u32[]{:S(2)}) collective-permute-start(bf16[768,512]{1,0:T(8,128)(2,1)S(1)} %far17.1), channel_id=1, source_target_pairs={{47,0},{0,1},{1,2},{2,3},{3,4},{4,5},{5,6},{6,7},{231,8},{8,9},{9,... | collective-permute-start | bytes 2359304 | tf_op jit(solution)/shard_map/ppermute | solution.py:387
  47.7 9.1 %collective-permute-start.7 = (bf16[768,512]{1,0:T(8,128)(2,1)S(1)}, bf16[768,512]{1,0:T(8,128)(2,1)S(1)}, u32[]{:S(2)}, u32[]{:S(2)}) collective-permute-start(bf16[768,512]{1,0:T(8,128)(2,1)S(1)} %near17.1), channel_id=1, source_target_pairs={{16,0},{17,1},{18,2},{19,3},{20,4},{21,5},{22,6},{23,7},{24,8},{25... | collective-permute-start | bytes 2359304 | tf_op jit(solution)/shard_map/ppermute | solution.py:387
  57.7 7.6 %collective-permute-start.10 = (f32[1,768]{1,0:T(1,128)S(1)}, f32[1,768]{1,0:T(1,128)S(1)}, u32[]{:S(2)}, u32[]{:S(2)}) collective-permute-start(f32[1,768]{1,0:T(1,128)S(1)} %get-tuple-element.50.refs_10_.refs_0_), channel_id=1, source_target_pairs={{255,0},{0,1},{1,2},{2,3},{3,4},{4,5},{5,6},{6,7},{7,8},{8,9},{9,1... | collective-permute-start | bytes 9224 | tf_op jit(solution)/shard_map/ppermute | solution.py:387
  57.8 7.5 %collective-permute-start.9 = (f32[1,768]{1,0:T(1,128)S(1)}, f32[1,768]{1,0:T(1,128)S(1)}, u32[]{:S(2)}, u32[]{:S(2)}) collective-permute-start(f32[1,768]{1,0:T(1,128)S(1)} %get-tuple-element.50.refs_10_.refs_0_), channel_id=1, source_target_pairs={{1,0},{2,1},{3,2},{4,3},{5,4},{6,5},{7,6},{8,7},{9,8},{10,9},{11,1... | collective-permute-start | bytes 9224 | tf_op jit(solution)/shard_map/ppermute | solution.py:387
  61.6 9.3 %collective-permute-start.12 = (f32[1,768]{1,0:T(1,128)S(1)}, f32[1,768]{1,0:T(1,128)S(1)}, u32[]{:S(2)}, u32[]{:S(2)}) collective-permute-start(f32[1,768]{1,0:T(1,128)S(1)} %get-tuple-element.50.refs_10_.refs_0_), channel_id=1, source_target_pairs={{192,0},{193,1},{194,2},{195,3},{196,4},{197,5},{198,6},{199,7},{2... | collective-permute-start | bytes 9224 | tf_op jit(solution)/shard_map/ppermute | solution.py:387
  62.8 8.1 %collective-permute-start.11 = (f32[1,768]{1,0:T(1,128)S(1)}, f32[1,768]{1,0:T(1,128)S(1)}, u32[]{:S(2)}, u32[]{:S(2)}) collective-permute-start(f32[1,768]{1,0:T(1,128)S(1)} %get-tuple-element.50.refs_10_.refs_0_), channel_id=1, source_target_pairs={{64,0},{65,1},{66,2},{67,3},{68,4},{69,5},{70,6},{71,7},{72,8},{73... | collective-permute-start | bytes 9224 | tf_op jit(solution)/shard_map/ppermute | solution.py:387
  65.3 9.0 %collective-permute-start.14 = (f32[3,768]{1,0:T(4,128)S(1)}, f32[3,768]{1,0:T(4,128)S(1)}, u32[]{:S(2)}, u32[]{:S(2)}) collective-permute-start(f32[3,768]{1,0:T(4,128)S(1)} %join.1), channel_id=1, source_target_pairs={{240,0},{241,1},{242,2},{243,3},{244,4},{245,5},{246,6},{247,7},{2... | collective-permute-start | bytes 27656 | tf_op jit(solution)/shard_map/ppermute | solution.py:387
  65.4 8.9 %collective-permute-start.13 = (f32[3,768]{1,0:T(4,128)S(1)}, f32[3,768]{1,0:T(4,128)S(1)}, u32[]{:S(2)}, u32[]{:S(2)}) collective-permute-start(f32[3,768]{1,0:T(4,128)S(1)} %join.1), channel_id=1, source_target_pairs={{16,0},{17,1},{18,2},{19,3},{20,4},{21,5},{22,6},{23,7},{24,8},{25... | collective-permute-start | bytes 27656 | tf_op jit(solution)/shard_map/ppermute | solution.py:387

commit v3 on v2

--- a/solution.py
+++ b/solution.py
@@ -52,18 +52,27 @@
         return taken + line - 1 if taken % line == 0 else taken - line + 1
 
     sources = {
-        "above": lambda b: wrap(b + 1),
-        "below": lambda b: wrap(b - 1),
+        "even": lambda b: b ^ 1,
+        "odd": lambda b: wrap(b - 1 if b % 2 == 0 else b + 1),
         "ring_above": ring(1),
         "ring_below": ring(-1),
         "turn": turn_source,
+        "x_even": lambda b: wrap(b + x_step if (b // x_step) % 2 == 0 else b - x_step),
+        "x_odd": lambda b: wrap(b - x_step if (b // x_step) % 2 == 0 else b + x_step),
         "x_above": lambda b: wrap(b + x_step),
         "x_below": lambda b: wrap(b - x_step),
         "near": lambda b: b + far_step if core(b) == 0 else b - far_step,
         "far": lambda b: wrap(b - far_step if core(b) == 0 else b + far_step),
         "far17": far17,
     }
-    return {name: [(source(b), b) for b in range(count)] for name, source in sources.items()}
+    corners = [b for b in range(count) if b % cols == (0, cols - 1)[core(b)] and half(b) == core(b)]
+    pairs = {name: [(source(b), b) for b in range(count)] for name, source in sources.items()}
+    pairs["corner_down"] = [(s, b) for s, b in pairs["far17"] if b in corners and core(b) == 0]
+    pairs["corner_up"] = [(s, b) for s, b in pairs["far17"] if b in corners and core(b) == 1]
+    pairs["far17"] = [(s, b) for s, b in pairs["far17"] if b not in corners]
+    pairs["row"] = [(b + cols - 1 if b % cols == 0 else b - cols + 1, b) for b in corners]
+    pairs["turn"] = [(s, b) for s, b in pairs["turn"] if b not in corners]
+    return pairs
 
 
 vmem_limit = 5 * 1024 * 1024
@@ -219,28 +228,34 @@
     )(*hold(normed, block, sums))
 
 
-def far17_kernel(far_ref, near_ref, mine_ref, x_below_ref, x_above_ref, out_ref):
+def far17_kernel(far_ref, near_ref, mine_ref, out_ref):
     cols, col = lax.axis_size("col"), lax.axis_index("col")
-    row = lax.axis_index("row")
-    core0 = row % 2 == 0
-    half0 = (row // 2) % 2 == 0
+    core0 = lax.axis_index("row") % 2 == 0
     last = col == jnp.where(core0, cols - 1, 0)
     turn = col == jnp.where(core0, cols // 2 - 1, cols // 2)
-    crossing = last & (core0 != half0)
-    choices = [
-        (crossing & core0, x_below_ref),
-        (crossing & ~core0, x_above_ref),
-        (last & ~crossing, mine_ref),
-        (turn, near_ref),
-        (~last & ~turn, far_ref),
-    ]
-    for chosen, ref in choices:
+    for chosen, ref in [(last, mine_ref), (turn, near_ref), (~last & ~turn, far_ref)]:
 
         @pl.when(chosen)
         def _():
             out_ref[...] = ref[...]
 
 
+def at_corner():
+    cols, row = lax.axis_size("col"), lax.axis_index("row")
+    core, half = row % 2, (row // 2) % 2
+    return (lax.axis_index("col") == core * (cols - 1)) & (half == core)
+
+
+def corner_kernel(far17_ref, down_ref, up_ref, out_ref):
+    corner = at_corner()
+    core0 = lax.axis_index("row") % 2 == 0
+    for chosen, ref in [(~corner, far17_ref), (corner & core0, down_ref), (corner & ~core0, up_ref)]:
+
+        @pl.when(chosen)
+        def _():
+            out_ref[...] = ref[...]
+
+
 def turn_kernel(above_ref, below_ref, out_ref):
     line = lax.axis_size("col") // 2
     place = lax.axis_index("col") % line
@@ -254,16 +269,14 @@
         out_ref[...] = below_ref[...]
 
 
-def merge_kernel(shift, ring_ref, turn_ref, out_ref):
+def merge_kernel(shift, core, ring_ref, turn_ref, row_ref, out_ref):
     turns = (lax.axis_index("col") + shift) % (lax.axis_size("col") // 2) == 0
-
-    @pl.when(turns)
-    def _():
-        out_ref[...] = turn_ref[...]
-
-    @pl.when(~turns)
-    def _():
-        out_ref[...] = ring_ref[...]
+    corner = at_corner() & (lax.axis_index("row") % 2 == core)
+    for chosen, ref in [(~turns, ring_ref), (turns & ~corner, turn_ref), (corner, row_ref)]:
+
+        @pl.when(chosen)
+        def _():
+            out_ref[...] = ref[...]
 
 
 def near17_kernel(below_ref, above_ref, out_ref):
@@ -305,8 +318,12 @@
 
 def first_kernel(count, sums_ref, matched_ref, *refs):
     exps_refs, block_refs = refs[:count], refs[count : 2 * count]
-    norm_refs, out_ref = refs[2 * count : 3 * count], refs[3 * count]
-    others = [1.0 / norm_ref[...] for norm_ref in norm_refs]
+    trio_ref, x_even_ref, x_odd_ref, out_ref = refs[2 * count :]
+    even = (lax.axis_index("row") // (lax.axis_size("row") // 4)) % 2 == 0
+    x_above = jnp.where(even, x_even_ref[...], x_odd_ref[...])
+    x_below = jnp.where(even, x_odd_ref[...], x_even_ref[...])
+    norms = [trio_ref[0:1, :], trio_ref[1:2, :], trio_ref[2:3, :], x_above, x_below]
+    others = [1.0 / norm for norm in norms]
     for part in parts(sums_ref.shape[0]):
         total = weighted(sums_ref, others, exps_refs, block_refs, part)
         out_ref[part, :] = total - 2.0 * matched_ref[part, :].astype(jnp.float32)
@@ -320,7 +337,9 @@
     far17 = jnp.where(core0, far_ref[2:3, :], far_ref[1:2, :])
     others = [1.0 / norm for norm in (near_ref[0:1, :], far_ref[0:1, :], near17, far17)]
     copies = []
-    for number, part in enumerate(parts(sums_ref.shape[0])):
+    *most, last = parts(sums_ref.shape[0])
+    half = (last.start + last.stop) // 2
+    for number, part in enumerate([*most, slice(last.start, half), slice(half, last.stop)]):
         total = weighted(sums_ref, others, exps_refs, block_refs, part)
         held_ref[part, :] = inverse_temp * (first_ref[part, :] + total)
         copy = pltpu.make_async_copy(held_ref.at[part], out_ref.at[part], sems.at[number])
@@ -335,7 +354,7 @@
     return call(
         functools.partial(first_kernel, count),
         "gather_first",
-        [held] * (3 * count + 2),
+        [held] * (2 * count + 5),
         held,
         pltpu.VMEM((rows, width), jnp.float32),
         2 * count * rows * rows * width,
@@ -355,28 +374,29 @@
         count * 2 * rows * (rows + width) + 8 * rows * width,
         scratch=[
             pltpu.VMEM((rows, width), jnp.float32),
-            pltpu.SemaphoreType.DMA((rows // chunk,)),
+            pltpu.SemaphoreType.DMA((rows // chunk + 1,)),
         ],
     )(*hold(sums, first, *exps, *blocks, near_trio, far_trio))
 
 
-def join_kernel(*refs):
-    *parts_refs, out_ref = refs
-    for number, ref in enumerate(parts_refs):
-        out_ref[number : number + 1, :] = ref[...]
-
-
-def join(*rows):
-    width = rows[0].shape[1]
-    return call(
-        join_kernel,
-        "join",
-        [held] * len(rows),
+def trio_kernel(mine_ref, even_ref, odd_ref, out_ref):
+    even = lax.axis_index("col") % 2 == 0
+    out_ref[0:1, :] = mine_ref[...]
+    out_ref[1:2, :] = jnp.where(even, even_ref[...], odd_ref[...])
+    out_ref[2:3, :] = jnp.where(even, odd_ref[...], even_ref[...])
+
+
+def trio_of(mine, even, odd):
+    width = mine.shape[1]
+    return call(
+        trio_kernel,
+        "trio",
+        [held] * 3,
         held,
-        pltpu.VMEM((len(rows), width), jnp.float32),
+        pltpu.VMEM((3, width), jnp.float32),
         0,
-        8 * len(rows) * width,
-    )(*hold(*rows))
+        24 * width,
+    )(*hold(mine, even, odd))
 
 
 def on_device(embeddings, positives):
@@ -391,13 +411,17 @@
     ring_above = send(normed, "ring_above")
     ring_below = send(normed, "ring_below")
     far = send(normed, "far")
-    x_below = send(normed, "x_below")
     self_exps, sums, matched = self_tile(normed, positives.reshape(-1, lanes))
     later, near, sums = lax.optimization_barrier((normed, near, sums))
+    x_below = send(later, "x_below")
     x_above = send(later, "x_above")
+    ring_above, sums = lax.optimization_barrier((ring_above, sums))
     turn = send(choose(turn_kernel, "turn", ring_above, ring_below), "turn")
-    passed = choose(far17_kernel, "far17", far, near, normed, x_below, x_above)
+    passed = choose(far17_kernel, "far17", far, near, normed)
     far17 = send(passed, "far17")
+    across = send(far, "row")
+    corner_down = send(x_below, "corner_down")
+    corner_up = send(x_above, "corner_up")
     exps, blocks = {}, {}
 
     def add(sums, **some):
@@ -408,18 +432,17 @@
 
     sums = add(sums, near=near, far=far, x_below=x_below, x_above=x_above)
     turn, sums = lax.optimization_barrier((turn, sums))
-    above = choose(functools.partial(merge_kernel, 1), "above", ring_above, turn)
-    below = choose(functools.partial(merge_kernel, 0), "below", ring_below, turn)
+    above = choose(functools.partial(merge_kernel, 1, 1), "above", ring_above, turn, across)
+    below = choose(functools.partial(merge_kernel, 0, 0), "below", ring_below, turn, across)
     near17 = send(choose(near17_kernel, "near17", below, above), "near")
-    sums = add(sums, above=above, below=below, far17=far17)
+    sums = add(sums, above=above, below=below)
+    sums = add(sums, far17=choose(corner_kernel, "corner", far17, corner_down, corner_up))
     blocks["near17"] = near17
     exps["near17"], sums, denoms = last_tile(normed, near17, sums)
 
-    d_above = send(denoms, "above")
-    d_below = send(denoms, "below")
-    d_x_above = send(denoms, "x_above")
-    d_x_below = send(denoms, "x_below")
-    trio = join(denoms, d_above, d_below)
+    trio = trio_of(denoms, send(denoms, "even"), send(denoms, "odd"))
+    d_x_even = send(denoms, "x_even")
+    d_x_odd = send(denoms, "x_odd")
     near_trio = send(trio, "near")
     far_trio = send(trio, "far")
 
@@ -429,7 +452,7 @@
         matched,
         [self_exps] + [exps[name] for name in names],
         [normed] + [blocks[name] for name in names],
-        [denoms, d_above, d_below, d_x_above, d_x_below],
+        [trio, d_x_even, d_x_odd],
     )
     names = ["near", "far", "near17", "far17"]
     return gather_final(

time: 78.4 us -> 75.2 us (0.959)
  starting transfers between devices: 45.1 us -> 38.7 us
  waiting for transfers between devices: 15.5 us -> 18.7 us
    ppermute x15 -> x18, starting transfers between devices: 45.1 us -> 38.7 us  [send(): return lax.ppermute(block, both, route[name])]
    ppermute x15 -> x18, waiting for transfers between devices: 15.5 us -> 18.7 us  [send(): return lax.ppermute(block, both, route[name])]
  transfers between devices with their start and end apart: 15 -> 18, of which waited for: 4 -> 5; matrix products, arithmetic and copies ran while one was open for 0% -> 0% of each run, Pallas kernels for 14% -> 15%
where the time goes in v3:
time: 75.2 us; the launch traced here: 75 us
  starting transfers between devices  38.7 us (51%)
  waiting for transfers between devices  18.7 us (25%)
  Pallas kernels  17.2 us (23%)
    ppermute x18, starting transfers between devices, send(): return lax.ppermute(block, both, route[name])  38.7 us
    ppermute x18, waiting for transfers between devices, send(): return lax.ppermute(block, both, route[name])  18.7 us
    pallas_call x7, Pallas kernels, pair_tile(): call(tile_kernel, 'pair_tile', [held] * 3, [held] * 2, [pltpu.VMEM((rows,...  5.88 us
    pallas_call x1, Pallas kernels, gather_final(): call(functools.partial(final_kernel, count), 'gather_final', [held] * (2...  3.46 us
    pallas_call x1, Pallas kernels, gather_first(): call(functools.partial(first_kernel, count), 'gather_first', [held] * (2...  3.37 us
    pallas_call x1, Pallas kernels, self_tile(): call(self_kernel, 'self_tile', [held, small], [held] * 3, [pltpu.VMEM((ro...  1.53 us
  transfers between devices with their start and end apart: 18, of which 5 were waited for; matrix products, arithmetic and copies ran while one was open for 0% of the time, Pallas kernels for 15%

profile of v3, /device:TPU:1, one launch (start us, length us, event | category | flops | bytes accessed | tf_op | source)
XLA Modules:
  0.0 75.0 jit_solution(7421033446067601363)
XLA Ops:
  0.0 0.0 copy-start
  0.0 1.4 %normalize.1.mine_ref.refs_5_ = bf16[768,512]{1,0:T(8,128)(2,1)S(1)} custom-call(bf16[768,512]{1,0:T(8,128)(2,1)} %rows_ref.1), custom_call_target="tpu_custom_call" | custom-call | flops 1572864 | bytes 1572864 | tf_op jit(solution)/shard_map/normalize/pallas_call | solution.py:121
  1.4 3.3 %collective-permute-start.2 = (bf16[768,512]{1,0:T(8,128)(2,1)S(1)}, bf16[768,512]{1,0:T(8,128)(2,1)S(1)}, u32[]{:S(2)}, u32[]{:S(2)}) collective-permute-start(bf16[768,512]{1,0:T(8,128)(2,1)S(1)} %normalize.1.mine_ref.refs_5_), channel_id=1, source_target_pairs={{16,0},{17,1},{18,2},{19,3},{20,4},{21,5},{22,6},{23,7},{24,8},{25... | collective-permute-start | bytes 2359304 | tf_op jit(solution)/shard_map/ppermute | solution.py:407
  4.7 3.9 %collective-permute-start.1 = (bf16[768,512]{1,0:T(8,128)(2,1)S(1)}, bf16[768,512]{1,0:T(8,128)(2,1)S(1)}, u32[]{:S(2)}, u32[]{:S(2)}) collective-permute-start(bf16[768,512]{1,0:T(8,128)(2,1)S(1)} %normalize.1.mine_ref.refs_5_), channel_id=1, source_target_pairs={{1,0},{2,1},{3,2},{4,3},{5,4},{6,5},{7,6},{0,7},{9,8},{10,9},{11,1... | collective-permute-start | bytes 2359304 | tf_op jit(solution)/shard_map/ppermute | solution.py:407
  8.6 0.0 collective-permute-start
  8.6 3.2 %collective-permute-start.6 = (bf16[768,512]{1,0:T(8,128)(2,1)S(1)}, bf16[768,512]{1,0:T(8,128)(2,1)S(1)}, u32[]{:S(2)}, u32[]{:S(2)}) collective-permute-start(bf16[768,512]{1,0:T(8,128)(2,1)S(1)} %normalize.1.mine_ref.refs_5_), channel_id=1, source_target_pairs={{240,0},{241,1},{242,2},{243,3},{244,4},{245,5},{246,6},{247,7},{2... | collective-permute-start | bytes 2359304 | tf_op jit(solution)/shard_map/ppermute | solution.py:407
  11.7 0.0 copy-done
  11.7 1.5 %self_tile.1 = (bf16[768,768]{1,0:T(8,128)(2,1)S(1)}, f32[768,128]{1,0:T(8,128)S(1)}, bf16[768,512]{1,0:T(8,128)(2,1)S(1)}) custom-call(bf16[768,512]{1,0:T(8,128)(2,1)S(1)} %normalize.1.mine_ref.refs_5_, s32[6,128]{1,0:T(8,128)S(1)} %bitcast.1), custom_call_target="tpu_custom_call" | custom-call | flops 1207959552 | bytes 2752512 | tf_op jit(solution)/shard_map/self_tile/pallas_call | solution.py:167
  13.3 0.0 collective-permute-done.2.theirs_ref.near_ref.refs_4_
  13.3 1.3 %collective-permute-start.5 = (bf16[768,512]{1,0:T(8,128)(2,1)S(1)}, bf16[768,512]{1,0:T(8,128)(2,1)S(1)}, u32[]{:S(2)}, u32[]{:S(2)}) collective-permute-start(bf16[768,512]{1,0:T(8,128)(2,1)S(1)} %normalize.1.mine_ref.refs_5_), channel_id=1, source_target_pairs={{192,0},{193,1},{194,2},{195,3},{196,4},{197,5},{198,6},{199,7},{2... | collective-permute-start | bytes 2359304 | tf_op jit(solution)/shard_map/ppermute | solution.py:407
  14.6 1.5 %collective-permute-start.4 = (bf16[768,512]{1,0:T(8,128)(2,1)S(1)}, bf16[768,512]{1,0:T(8,128)(2,1)S(1)}, u32[]{:S(2)}, u32[]{:S(2)}) collective-permute-start(bf16[768,512]{1,0:T(8,128)(2,1)S(1)} %normalize.1.mine_ref.refs_5_), channel_id=1, source_target_pairs={{64,0},{65,1},{66,2},{67,3},{68,4},{69,5},{70,6},{71,7},{72,8},{73... | collective-permute-start | bytes 2359304 | tf_op jit(solution)/shard_map/ppermute | solution.py:407
  16.1 9.4 %collective-permute-done.1.above_ref.ring_ref = bf16[768,512]{1,0:T(8,128)(2,1)S(1)} collective-permute-done((bf16[768,512]{1,0:T(8,128)(2,1)S(1)}, bf16[768,512]{1,0:T(8,128)(2,1)S(1)}, u32[]{:S(2)}, u32[]{:S(2)}) %collective-permute-start.1) | collective-permute-done | bytes 786464 | tf_op jit(solution)/shard_map/ppermute | solution.py:407
  25.5 3.1 %collective-permute-done.below_ref.ring_ref = bf16[768,512]{1,0:T(8,128)(2,1)S(1)} collective-permute-done((bf16[768,512]{1,0:T(8,128)(2,1)S(1)}, bf16[768,512]{1,0:T(8,128)(2,1)S(1)}, u32[]{:S(2)}, u32[]{:S(2)}) %collective-permute-start) | collective-permute-done | bytes 786464 | tf_op jit(solution)/shard_map/ppermute | solution.py:407
  28.6 0.1 turn.1
  28.6 3.2 %collective-permute-start.3 = (bf16[768,512]{1,0:T(8,128)(2,1)S(1)}, bf16[768,512]{1,0:T(8,128)(2,1)S(1)}, u32[]{:S(2)}, u32[]{:S(2)}) collective-permute-start(bf16[768,512]{1,0:T(8,128)(2,1)S(1)} %turn.1), channel_id=1, source_target_pairs={{1,1},{2,2},{3,3},{4,4},{5,5},{6,6},{15,7},{0,8},{9,9},{10,10},{11... | collective-permute-start | bytes 2359304 | tf_op jit(solution)/shard_map/ppermute | solution.py:407
  31.8 0.0 collective-permute-done.6.theirs_ref.far_ref.refs_5_
  31.9 0.7 collective-permute-start.7
  32.6 0.1 far17.1
  32.7 1.3 %collective-permute-start.9 = (bf16[768,512]{1,0:T(8,128)(2,1)S(1)}, bf16[768,512]{1,0:T(8,128)(2,1)S(1)}, u32[]{:S(2)}, u32[]{:S(2)}) collective-permute-start(bf16[768,512]{1,0:T(8,128)(2,1)S(1)} %far17.1), channel_id=1, source_target_pairs={{0,1},{1,2},{2,3},{3,4},{4,5},{5,6},{6,7},{231,8},{8,9},{9,10},{10... | collective-permute-start | bytes 2359304 | tf_op jit(solution)/shard_map/ppermute | solution.py:407
  34.0 0.8 %pair_tile.7 = (bf16[768,768]{1,0:T(8,128)(2,1)S(1)}, f32[768,128]{1,0:T(8,128)S(1)}) custom-call(bf16[768,512]{1,0:T(8,128)(2,1)S(1)} %normalize.1.mine_ref.refs_5_, bf16[768,512]{1,0:T(8,128)(2,1)S(1)} %collective-permute-done.2.theirs_ref.near_ref.refs_4_, f32[768,128]{1,0:T(8,128)S(1)} %get-tuple-element.37.before_ref), custom_call_target="tpu_custom_call" | custom-call | flops 603979776 | bytes 2752512 | tf_op jit(solution)/shard_map/pair_tile/pallas_call | solution.py:192
  34.8 0.8 %pair_tile.8 = (bf16[768,768]{1,0:T(8,128)(2,1)S(1)}, f32[768,128]{1,0:T(8,128)S(1)}) custom-call(bf16[768,512]{1,0:T(8,128)(2,1)S(1)} %normalize.1.mine_ref.refs_5_, bf16[768,512]{1,0:T(8,128)(2,1)S(1)} %collective-permute-done.6.theirs_ref.far_ref.refs_5_, f32[768,128]{1,0:T(8,128)S(1)} %get-tuple-element.38.before_ref), custom_call_target="tpu_custom_call" | custom-call | flops 603979776 | bytes 2752512 | tf_op jit(solution)/shard_map/pair_tile/pallas_call | solution.py:192
  35.6 0.0 collective-permute-done.5.theirs_ref.refs_9_
  35.7 0.7 collective-permute-start.10
  36.4 0.0 collective-permute-done.4.theirs_ref.refs_8_
  36.4 10.1 %collective-permute-start.11 = (bf16[768,512]{1,0:T(8,128)(2,1)S(1)}, bf16[768,512]{1,0:T(8,128)(2,1)S(1)}, u32[]{:S(2)}, u32[]{:S(2)}) collective-permute-start(bf16[768,512]{1,0:T(8,128)(2,1)S(1)} %collective-permute-done.4.theirs_ref.refs_8_), channel_id=1, source_target_pairs={{16,63},{80,127},{144,191},{208,255}} | collective-permute-start | bytes 2359304 | tf_op jit(solution)/shard_map/ppermute | solution.py:407
  46.5 0.8 %pair_tile.9 = (bf16[768,768]{1,0:T(8,128)(2,1)S(1)}, f32[768,128]{1,0:T(8,128)S(1)}) custom-call(bf16[768,512]{1,0:T(8,128)(2,1)S(1)} %normalize.1.mine_ref.refs_5_, bf16[768,512]{1,0:T(8,128)(2,1)S(1)} %collective-permute-done.5.theirs_ref.refs_9_, f32[768,128]{1,0:T(8,128)S(1)} %get-tuple-element.39.before_ref), custom_call_target="tpu_custom_call" | custom-call | flops 603979776 | bytes 2752512 | tf_op jit(solution)/shard_map/pair_tile/pallas_call | solution.py:192
  47.4 0.8 %pair_tile.10 = (bf16[768,768]{1,0:T(8,128)(2,1)S(1)}, f32[768,128]{1,0:T(8,128)S(1)}) custom-call(bf16[768,512]{1,0:T(8,128)(2,1)S(1)} %normalize.1.mine_ref.refs_5_, bf16[768,512]{1,0:T(8,128)(2,1)S(1)} %collective-permute-done.4.theirs_ref.refs_8_, f32[768,128]{1,0:T(8,128)S(1)} %get-tuple-element.40.before_ref), custom_call_target="tpu_custom_call" | custom-call | flops 603979776 | bytes 2752512 | tf_op jit(solution)/shard_map/pair_tile/pallas_call | solution.py:192
  48.2 3.1 %collective-permute-done.3.turn_ref = bf16[768,512]{1,0:T(8,128)(2,1)S(1)} collective-permute-done((bf16[768,512]{1,0:T(8,128)(2,1)S(1)}, bf16[768,512]{1,0:T(8,128)(2,1)S(1)}, u32[]{:S(2)}, u32[]{:S(2)}) %collective-permute-start.3) | collective-permute-done | bytes 786464 | tf_op jit(solution)/shard_map/ppermute | solution.py:407
  51.3 0.0 collective-permute-done.7.row_ref
  51.3 0.1 above.1.above_ref.theirs_ref.refs_6_
  51.4 0.1 below.1.below_ref.theirs_ref.refs_7_
  51.4 0.1 near17.1
  51.5 0.1 collective-permute-start.8
  51.6 0.8 %pair_tile.11 = (bf16[768,768]{1,0:T(8,128)(2,1)S(1)}, f32[768,128]{1,0:T(8,128)S(1)}) custom-call(bf16[768,512]{1,0:T(8,128)(2,1)S(1)} %normalize.1.mine_ref.refs_5_, bf16[768,512]{1,0:T(8,128)(2,1)S(1)} %above.1.above_ref.theirs_ref.refs_6_, f32[768,128]{1,0:T(8,128)S(1)} %get-tuple-element.43.before_ref), custom_call_target="tpu_custom_call" | custom-call | flops 603979776 | bytes 2752512 | tf_op jit(solution)/shard_map/pair_tile/pallas_call | solution.py:192
  52.5 0.8 %pair_tile.12 = (bf16[768,768]{1,0:T(8,128)(2,1)S(1)}, f32[768,128]{1,0:T(8,128)S(1)}) custom-call(bf16[768,512]{1,0:T(8,128)(2,1)S(1)} %normalize.1.mine_ref.refs_5_, bf16[768,512]{1,0:T(8,128)(2,1)S(1)} %below.1.below_ref.theirs_ref.refs_7_, f32[768,128]{1,0:T(8,128)S(1)} %get-tuple-element.44.before_ref), custom_call_target="tpu_custom_call" | custom-call | flops 603979776 | bytes 2752512 | tf_op jit(solution)/shard_map/pair_tile/pallas_call | solution.py:192
  53.3 0.0 collective-permute-done.9.far17_ref
  53.3 0.0 collective-permute-done.10.down_ref
  53.3 2.1 %collective-permute-done.11.up_ref = bf16[768,512]{1,0:T(8,128)(2,1)S(1)} collective-permute-done((bf16[768,512]{1,0:T(8,128)(2,1)S(1)}, bf16[768,512]{1,0:T(8,128)(2,1)S(1)}, u32[]{:S(2)}, u32[]{:S(2)}) %collective-permute-start.11) | collective-permute-done | bytes 786464 | tf_op jit(solution)/shard_map/ppermute | solution.py:407
  55.4 0.2 corner.1.theirs_ref.refs_7_
  55.6 0.8 %pair_tile.13 = (bf16[768,768]{1,0:T(8,128)(2,1)S(1)}, f32[768,128]{1,0:T(8,128)S(1)}) custom-call(bf16[768,512]{1,0:T(8,128)(2,1)S(1)} %normalize.1.mine_ref.refs_5_, bf16[768,512]{1,0:T(8,128)(2,1)S(1)} %corner.1.theirs_ref.refs_7_, f32[768,128]{1,0:T(8,128)S(1)} %get-tuple-element.45.before_ref), custom_call_target="tpu_custom_call" | custom-call | flops 603979776 | bytes 2752512 | tf_op jit(solution)/shard_map/pair_tile/pallas_call | solution.py:192
  56.5 0.0 collective-permute-done.8.theirs_ref.refs_6_
  56.5 1.0 %last_tile.1 = (bf16[768,768]{1,0:T(8,128)(2,1)S(1)}, f32[768,128]{1,0:T(8,128)S(1)}, f32[1,768]{1,0:T(1,128)S(1)}) custom-call(bf16[768,512]{1,0:T(8,128)(2,1)S(1)} %normalize.1.mine_ref.refs_5_, bf16[768,512]{1,0:T(8,128)(2,1)S(1)} %collective-permute-done.8.theirs_ref.refs_6_, f32[768,128]{1,0:T(8,128)S(1)} %get-tuple-element.46.before_ref), custom_call_target="tpu_custom_call" | custom-call | flops 603979776 | bytes 2752512 | tf_op jit(solution)/shard_map/last_tile/pallas_call | solution.py:215
  57.5 1.7 %collective-permute-start.13 = (f32[1,768]{1,0:T(1,128)S(1)}, f32[1,768]{1,0:T(1,128)S(1)}, u32[]{:S(2)}, u32[]{:S(2)}) collective-permute-start(f32[1,768]{1,0:T(1,128)S(1)} %get-tuple-element.54.mine_ref), channel_id=1, source_target_pairs={{255,0},{2,1},{1,2},{4,3},{3,4},{6,5},{5,6},{8,7},{7,8},{10,9},{9,... | collective-permute-start | bytes 9224 | tf_op jit(solution)/shard_map/ppermute | solution.py:407
  59.2 0.0 collective-permute-start.12
  59.2 2.5 %collective-permute-start.15 = (f32[1,768]{1,0:T(1,128)S(1)}, f32[1,768]{1,0:T(1,128)S(1)}, u32[]{:S(2)}, u32[]{:S(2)}) collective-permute-start(f32[1,768]{1,0:T(1,128)S(1)} %get-tuple-element.54.mine_ref), channel_id=1, source_target_pairs={{192,0},{193,1},{194,2},{195,3},{196,4},{197,5},{198,6},{199,7},{2... | collective-permute-start | bytes 9224 | tf_op jit(solution)/shard_map/ppermute | solution.py:407
  61.7 0.0 collective-permute-start.14
  61.7 1.0 %collective-permute-done.13.odd_ref = f32[1,768]{1,0:T(1,128)S(1)} collective-permute-done((f32[1,768]{1,0:T(1,128)S(1)}, f32[1,768]{1,0:T(1,128)S(1)}, u32[]{:S(2)}, u32[]{:S(2)}) %collective-permute-start.13) | collective-permute-done | bytes 3104 | tf_op jit(solution)/shard_map/ppermute | solution.py:407
  62.7 0.0 collective-permute-done.12.even_ref
  62.7 4.2 %collective-permute-start.17 = (f32[3,768]{1,0:T(4,128)S(1)}, f32[3,768]{1,0:T(4,128)S(1)}, u32[]{:S(2)}, u32[]{:S(2)}) collective-permute-start(f32[3,768]{1,0:T(4,128)S(1)} %trio.1.refs_10_), channel_id=1, source_target_pairs={{240,0},{241,1},{242,2},{243,3},{244,4},{245,5},{246,6},{247,7},{2... | collective-permute-start | bytes 27656 | tf_op jit(solution)/shard_map/ppermute | solution.py:407
  66.9 1.1 %collective-permute-start.16 = (f32[3,768]{1,0:T(4,128)S(1)}, f32[3,768]{1,0:T(4,128)S(1)}, u32[]{:S(2)}, u32[]{:S(2)}) collective-permute-start(f32[3,768]{1,0:T(4,128)S(1)} %trio.1.refs_10_), channel_id=1, source_target_pairs={{16,0},{17,1},{18,2},{19,3},{20,4},{21,5},{22,6},{23,7},{24,8},{25... | collective-permute-start | bytes 27656 | tf_op jit(solution)/shard_map/ppermute | solution.py:407
  68.0 0.0 collective-permute-done.15.refs_12_
  68.0 0.0 collective-permute-done.14.refs_11_
  68.0 3.4 %gather_first.1.first_ref = f32[768,512]{1,0:T(8,128)S(1)} custom-call(f32[768,128]{1,0:T(8,128)S(1)} %get-tuple-element.47.sums_ref, bf16[768,512]{1,0:T(8,128)(2,1)S(1)} %get-tuple-element.48.matched_ref, bf16[768,768]{1,0:T(8,128)(2,1)S(1)} %get-tuple-element.49.refs_0_, bf16[768,768]{1,0:T(8,128)(2,1)S(1)} %get-tuple-element.50.refs_1_, ...), custom_call_target="tpu_custom_call" | custom-call | flops 3019898880 | bytes 12976128 | tf_op jit(solution)/shard_map/gather_first/pallas_call | solution.py:354
  71.4 0.0 collective-permute-done.17.refs_9_
  71.4 0.0 collective-permute-done.16.refs_8_
  71.4 3.5 %gather_final.1 = f32[768,512]{1,0:T(8,128)} custom-call(f32[768,128]{1,0:T(8,128)S(1)} %get-tuple-element.47.sums_ref, f32[768,512]{1,0:T(8,128)S(1)} %gather_first.1.first_ref, bf16[768,768]{1,0:T(8,128)(2,1)S(1)} %get-tuple-element.55.refs_0_, bf16[768,768]{1,0:T(8,128)(2,1)S(1)} %get-tuple-element.56.refs_1_, ...), custom_call_target="tpu_custom_call" | custom-call | flops 2415919104 | bytes 11010048 | tf_op jit(solution)/shard_map/gather_final/pallas_call | solution.py:367
  (1 shorter events, 0.0 us)
Async XLA Ops:
  0.0 11.7 %copy-start = (s32[768]{0:T(1024)S(1)}, s32[768]{0:T(1024)}, u32[]{:S(2)}) copy-start(s32[768]{0:T(1024)} %param.3) | copy-start | bytes 9220
  1.4 11.9 %collective-permute-start.2 = (bf16[768,512]{1,0:T(8,128)(2,1)S(1)}, bf16[768,512]{1,0:T(8,128)(2,1)S(1)}, u32[]{:S(2)}, u32[]{:S(2)}) collective-permute-start(bf16[768,512]{1,0:T(8,128)(2,1)S(1)} %normalize.1.mine_ref.refs_5_), channel_id=1, source_target_pairs={{16,0},{17,1},{18,2},{19,3},{20,4},{21,5},{22,6},{23,7},{24,8},{25... | collective-permute-start | bytes 2359304 | tf_op jit(solution)/shard_map/ppermute | solution.py:407
  4.7 20.7 %collective-permute-start.1 = (bf16[768,512]{1,0:T(8,128)(2,1)S(1)}, bf16[768,512]{1,0:T(8,128)(2,1)S(1)}, u32[]{:S(2)}, u32[]{:S(2)}) collective-permute-start(bf16[768,512]{1,0:T(8,128)(2,1)S(1)} %normalize.1.mine_ref.refs_5_), channel_id=1, source_target_pairs={{1,0},{2,1},{3,2},{4,3},{5,4},{6,5},{7,6},{0,7},{9,8},{10,9},{11,1... | collective-permute-start | bytes 2359304 | tf_op jit(solution)/shard_map/ppermute | solution.py:407
  8.6 20.0 %collective-permute-start = (bf16[768,512]{1,0:T(8,128)(2,1)S(1)}, bf16[768,512]{1,0:T(8,128)(2,1)S(1)}, u32[]{:S(2)}, u32[]{:S(2)}) collective-permute-start(bf16[768,512]{1,0:T(8,128)(2,1)S(1)} %normalize.1.mine_ref.refs_5_), channel_id=1, source_target_pairs={{7,0},{0,1},{1,2},{2,3},{3,4},{4,5},{5,6},{6,7},{15,8},{8,9},{9,10... | collective-permute-start | bytes 2359304 | tf_op jit(solution)/shard_map/ppermute | solution.py:407
  8.6 23.3 %collective-permute-start.6 = (bf16[768,512]{1,0:T(8,128)(2,1)S(1)}, bf16[768,512]{1,0:T(8,128)(2,1)S(1)}, u32[]{:S(2)}, u32[]{:S(2)}) collective-permute-start(bf16[768,512]{1,0:T(8,128)(2,1)S(1)} %normalize.1.mine_ref.refs_5_), channel_id=1, source_target_pairs={{240,0},{241,1},{242,2},{243,3},{244,4},{245,5},{246,6},{247,7},{2... | collective-permute-start | bytes 2359304 | tf_op jit(solution)/shard_map/ppermute | solution.py:407
  13.3 22.4 %collective-permute-start.5 = (bf16[768,512]{1,0:T(8,128)(2,1)S(1)}, bf16[768,512]{1,0:T(8,128)(2,1)S(1)}, u32[]{:S(2)}, u32[]{:S(2)}) collective-permute-start(bf16[768,512]{1,0:T(8,128)(2,1)S(1)} %normalize.1.mine_ref.refs_5_), channel_id=1, source_target_pairs={{192,0},{193,1},{194,2},{195,3},{196,4},{197,5},{198,6},{199,7},{2... | collective-permute-start | bytes 2359304 | tf_op jit(solution)/shard_map/ppermute | solution.py:407
  14.6 21.8 %collective-permute-start.4 = (bf16[768,512]{1,0:T(8,128)(2,1)S(1)}, bf16[768,512]{1,0:T(8,128)(2,1)S(1)}, u32[]{:S(2)}, u32[]{:S(2)}) collective-permute-start(bf16[768,512]{1,0:T(8,128)(2,1)S(1)} %normalize.1.mine_ref.refs_5_), channel_id=1, source_target_pairs={{64,0},{65,1},{66,2},{67,3},{68,4},{69,5},{70,6},{71,7},{72,8},{73... | collective-permute-start | bytes 2359304 | tf_op jit(solution)/shard_map/ppermute | solution.py:407
  28.6 22.7 %collective-permute-start.3 = (bf16[768,512]{1,0:T(8,128)(2,1)S(1)}, bf16[768,512]{1,0:T(8,128)(2,1)S(1)}, u32[]{:S(2)}, u32[]{:S(2)}) collective-permute-start(bf16[768,512]{1,0:T(8,128)(2,1)S(1)} %turn.1), channel_id=1, source_target_pairs={{1,1},{2,2},{3,3},{4,4},{5,5},{6,6},{15,7},{0,8},{9,9},{10,10},{11... | collective-permute-start | bytes 2359304 | tf_op jit(solution)/shard_map/ppermute | solution.py:407
  31.9 19.4 %collective-permute-start.7 = (bf16[768,512]{1,0:T(8,128)(2,1)S(1)}, bf16[768,512]{1,0:T(8,128)(2,1)S(1)}, u32[]{:S(2)}, u32[]{:S(2)}) collective-permute-start(bf16[768,512]{1,0:T(8,128)(2,1)S(1)} %collective-permute-done.6.theirs_ref.far_ref.refs_5_), channel_id=1, source_target_pairs={{15,0},{48,63},{79,64},{112,127},{143,128},{176,191},{207,192},{24... | collective-permute-start | bytes 2359304 | tf_op jit(solution)/shard_map/ppermute | solution.py:407
  32.7 20.7 %collective-permute-start.9 = (bf16[768,512]{1,0:T(8,128)(2,1)S(1)}, bf16[768,512]{1,0:T(8,128)(2,1)S(1)}, u32[]{:S(2)}, u32[]{:S(2)}) collective-permute-start(bf16[768,512]{1,0:T(8,128)(2,1)S(1)} %far17.1), channel_id=1, source_target_pairs={{0,1},{1,2},{2,3},{3,4},{4,5},{5,6},{6,7},{231,8},{8,9},{9,10},{10... | collective-permute-start | bytes 2359304 | tf_op jit(solution)/shard_map/ppermute | solution.py:407
  35.7 17.7 %collective-permute-start.10 = (bf16[768,512]{1,0:T(8,128)(2,1)S(1)}, bf16[768,512]{1,0:T(8,128)(2,1)S(1)}, u32[]{:S(2)}, u32[]{:S(2)}) collective-permute-start(bf16[768,512]{1,0:T(8,128)(2,1)S(1)} %collective-permute-done.5.theirs_ref.refs_9_), channel_id=1, source_target_pairs={{47,0},{111,64},{175,128},{239,192}} | collective-permute-start | bytes 2359304 | tf_op jit(solution)/shard_map/ppermute | solution.py:407
  36.4 19.0 %collective-permute-start.11 = (bf16[768,512]{1,0:T(8,128)(2,1)S(1)}, bf16[768,512]{1,0:T(8,128)(2,1)S(1)}, u32[]{:S(2)}, u32[]{:S(2)}) collective-permute-start(bf16[768,512]{1,0:T(8,128)(2,1)S(1)} %collective-permute-done.4.theirs_ref.refs_8_), channel_id=1, source_target_pairs={{16,63},{80,127},{144,191},{208,255}} | collective-permute-start | bytes 2359304 | tf_op jit(solution)/shard_map/ppermute | solution.py:407
  51.5 5.0 %collective-permute-start.8 = (bf16[768,512]{1,0:T(8,128)(2,1)S(1)}, bf16[768,512]{1,0:T(8,128)(2,1)S(1)}, u32[]{:S(2)}, u32[]{:S(2)}) collective-permute-start(bf16[768,512]{1,0:T(8,128)(2,1)S(1)} %near17.1), channel_id=1, source_target_pairs={{16,0},{17,1},{18,2},{19,3},{20,4},{21,5},{22,6},{23,7},{24,8},{25... | collective-permute-start | bytes 2359304 | tf_op jit(solution)/shard_map/ppermute | solution.py:407
  57.5 5.2 %collective-permute-start.13 = (f32[1,768]{1,0:T(1,128)S(1)}, f32[1,768]{1,0:T(1,128)S(1)}, u32[]{:S(2)}, u32[]{:S(2)}) collective-permute-start(f32[1,768]{1,0:T(1,128)S(1)} %get-tuple-element.54.mine_ref), channel_id=1, source_target_pairs={{255,0},{2,1},{1,2},{4,3},{3,4},{6,5},{5,6},{8,7},{7,8},{10,9},{9,... | collective-permute-start | bytes 9224 | tf_op jit(solution)/shard_map/ppermute | solution.py:407
  59.2 3.5 %collective-permute-start.12 = (f32[1,768]{1,0:T(1,128)S(1)}, f32[1,768]{1,0:T(1,128)S(1)}, u32[]{:S(2)}, u32[]{:S(2)}) collective-permute-start(f32[1,768]{1,0:T(1,128)S(1)} %get-tuple-element.54.mine_ref), channel_id=1, source_target_pairs={{1,0},{0,1},{3,2},{2,3},{5,4},{4,5},{7,6},{6,7},{9,8},{8,9},{11,10... | collective-permute-start | bytes 9224 | tf_op jit(solution)/shard_map/ppermute | solution.py:407
  59.2 8.8 %collective-permute-start.15 = (f32[1,768]{1,0:T(1,128)S(1)}, f32[1,768]{1,0:T(1,128)S(1)}, u32[]{:S(2)}, u32[]{:S(2)}) collective-permute-start(f32[1,768]{1,0:T(1,128)S(1)} %get-tuple-element.54.mine_ref), channel_id=1, source_target_pairs={{192,0},{193,1},{194,2},{195,3},{196,4},{197,5},{198,6},{199,7},{2... | collective-permute-start | bytes 9224 | tf_op jit(solution)/shard_map/ppermute | solution.py:407
  61.7 6.3 %collective-permute-start.14 = (f32[1,768]{1,0:T(1,128)S(1)}, f32[1,768]{1,0:T(1,128)S(1)}, u32[]{:S(2)}, u32[]{:S(2)}) collective-permute-start(f32[1,768]{1,0:T(1,128)S(1)} %get-tuple-element.54.mine_ref), channel_id=1, source_target_pairs={{64,0},{65,1},{66,2},{67,3},{68,4},{69,5},{70,6},{71,7},{72,8},{73... | collective-permute-start | bytes 9224 | tf_op jit(solution)/shard_map/ppermute | solution.py:407
  62.7 8.7 %collective-permute-start.17 = (f32[3,768]{1,0:T(4,128)S(1)}, f32[3,768]{1,0:T(4,128)S(1)}, u32[]{:S(2)}, u32[]{:S(2)}) collective-permute-start(f32[3,768]{1,0:T(4,128)S(1)} %trio.1.refs_10_), channel_id=1, source_target_pairs={{240,0},{241,1},{242,2},{243,3},{244,4},{245,5},{246,6},{247,7},{2... | collective-permute-start | bytes 27656 | tf_op jit(solution)/shard_map/ppermute | solution.py:407
  66.9 4.5 %collective-permute-start.16 = (f32[3,768]{1,0:T(4,128)S(1)}, f32[3,768]{1,0:T(4,128)S(1)}, u32[]{:S(2)}, u32[]{:S(2)}) collective-permute-start(f32[3,768]{1,0:T(4,128)S(1)} %trio.1.refs_10_), channel_id=1, source_target_pairs={{16,0},{17,1},{18,2},{19,3},{20,4},{21,5},{22,6},{23,7},{24,8},{25... | collective-permute-start | bytes 27656 | tf_op jit(solution)/shard_map/ppermute | solution.py:407

commit v4 on v3

--- a/solution.py
+++ b/solution.py
@@ -39,6 +39,9 @@
             return wrap(b + (2 * cols if half(b) == 0 else -2 * cols) - cols + 1)
         return wrap(b + 2 * cols + 1) if j == cols // 2 - 1 else b + 1
 
+    def near(b):
+        return b + far_step if core(b) == 0 else b - far_step
+
     def ring(step):
         return lambda b: b - b % line + (b + step) % line
 
@@ -48,7 +51,7 @@
     def turn_source(b):
         taken = turn(b)
         if taken == b:
-            return b
+            return near(b)
         return taken + line - 1 if taken % line == 0 else taken - line + 1
 
     sources = {
@@ -59,19 +62,24 @@
         "turn": turn_source,
         "x_even": lambda b: wrap(b + x_step if (b // x_step) % 2 == 0 else b - x_step),
         "x_odd": lambda b: wrap(b - x_step if (b // x_step) % 2 == 0 else b + x_step),
-        "x_above": lambda b: wrap(b + x_step),
-        "x_below": lambda b: wrap(b - x_step),
-        "near": lambda b: b + far_step if core(b) == 0 else b - far_step,
+        "x_first": lambda b: wrap(b - x_step if core(b) == 0 else b + x_step),
+        "x_second": lambda b: wrap(b + x_step if core(b) == 0 else b - x_step),
+        "near": near,
         "far": lambda b: wrap(b - far_step if core(b) == 0 else b + far_step),
         "far17": far17,
     }
     corners = [b for b in range(count) if b % cols == (0, cols - 1)[core(b)] and half(b) == core(b)]
     pairs = {name: [(source(b), b) for b in range(count)] for name, source in sources.items()}
-    pairs["corner_down"] = [(s, b) for s, b in pairs["far17"] if b in corners and core(b) == 0]
-    pairs["corner_up"] = [(s, b) for s, b in pairs["far17"] if b in corners and core(b) == 1]
-    pairs["far17"] = [(s, b) for s, b in pairs["far17"] if b not in corners]
+    crossing = {s: b for s, b in pairs["far17"] if b in corners}
+    idle = {b: near(b) for b in corners}
+    idle.update({b: near(b) for b in range(count) if b not in crossing and b not in corners})
+    idle.update(crossing)
+    pairs["corner"] = sorted(idle.items())
     pairs["row"] = [(b + cols - 1 if b % cols == 0 else b - cols + 1, b) for b in corners]
-    pairs["turn"] = [(s, b) for s, b in pairs["turn"] if b not in corners]
+    free = {s: near(s) for s, b in pairs["far17"] if b in corners}
+    pairs["far17"] = [(s, free.get(s, b)) for s, b in pairs["far17"]]
+    free = {s: s + line - 1 if s % line == 0 else s - line + 1 for s, b in pairs["turn"] if b in corners}
+    pairs["turn"] = [(s, free.get(s, b)) for s, b in pairs["turn"]]
     return pairs
 
 
@@ -246,14 +254,16 @@
     return (lax.axis_index("col") == core * (cols - 1)) & (half == core)
 
 
-def corner_kernel(far17_ref, down_ref, up_ref, out_ref):
+def corner_kernel(far17_ref, corner_ref, out_ref):
     corner = at_corner()
-    core0 = lax.axis_index("row") % 2 == 0
-    for chosen, ref in [(~corner, far17_ref), (corner & core0, down_ref), (corner & ~core0, up_ref)]:
-
-        @pl.when(chosen)
-        def _():
-            out_ref[...] = ref[...]
+
+    @pl.when(corner)
+    def _():
+        out_ref[...] = corner_ref[...]
+
+    @pl.when(~corner)
+    def _():
+        out_ref[...] = far17_ref[...]
 
 
 def turn_kernel(above_ref, below_ref, out_ref):
@@ -319,10 +329,11 @@
 def first_kernel(count, sums_ref, matched_ref, *refs):
     exps_refs, block_refs = refs[:count], refs[count : 2 * count]
     trio_ref, x_even_ref, x_odd_ref, out_ref = refs[2 * count :]
-    even = (lax.axis_index("row") // (lax.axis_size("row") // 4)) % 2 == 0
-    x_above = jnp.where(even, x_even_ref[...], x_odd_ref[...])
-    x_below = jnp.where(even, x_odd_ref[...], x_even_ref[...])
-    norms = [trio_ref[0:1, :], trio_ref[1:2, :], trio_ref[2:3, :], x_above, x_below]
+    row = lax.axis_index("row")
+    even = (row // (lax.axis_size("row") // 4)) % 2 == row % 2
+    x_first = jnp.where(even, x_odd_ref[...], x_even_ref[...])
+    x_second = jnp.where(even, x_even_ref[...], x_odd_ref[...])
+    norms = [trio_ref[0:1, :], trio_ref[1:2, :], trio_ref[2:3, :], x_first, x_second]
     others = [1.0 / norm for norm in norms]
     for part in parts(sums_ref.shape[0]):
         total = weighted(sums_ref, others, exps_refs, block_refs, part)
@@ -413,15 +424,15 @@
     far = send(normed, "far")
     self_exps, sums, matched = self_tile(normed, positives.reshape(-1, lanes))
     later, near, sums = lax.optimization_barrier((normed, near, sums))
-    x_below = send(later, "x_below")
-    x_above = send(later, "x_above")
+    x_first = send(later, "x_first")
+    x_second = send(later, "x_second")
     ring_above, sums = lax.optimization_barrier((ring_above, sums))
     turn = send(choose(turn_kernel, "turn", ring_above, ring_below), "turn")
     passed = choose(far17_kernel, "far17", far, near, normed)
     far17 = send(passed, "far17")
+    far, passed = lax.optimization_barrier((far, passed))
     across = send(far, "row")
-    corner_down = send(x_below, "corner_down")
-    corner_up = send(x_above, "corner_up")
+    corner = send(x_first, "corner")
     exps, blocks = {}, {}
 
     def add(sums, **some):
@@ -430,13 +441,13 @@
             exps[name], sums = pair_tile(normed, block, sums)
         return sums
 
-    sums = add(sums, near=near, far=far, x_below=x_below, x_above=x_above)
+    sums = add(sums, near=near, far=far, x_first=x_first, x_second=x_second)
     turn, sums = lax.optimization_barrier((turn, sums))
     above = choose(functools.partial(merge_kernel, 1, 1), "above", ring_above, turn, across)
     below = choose(functools.partial(merge_kernel, 0, 0), "below", ring_below, turn, across)
     near17 = send(choose(near17_kernel, "near17", below, above), "near")
     sums = add(sums, above=above, below=below)
-    sums = add(sums, far17=choose(corner_kernel, "corner", far17, corner_down, corner_up))
+    sums = add(sums, far17=choose(corner_kernel, "corner", far17, corner))
     blocks["near17"] = near17
     exps["near17"], sums, denoms = last_tile(normed, near17, sums)
 
@@ -446,7 +457,7 @@
     near_trio = send(trio, "near")
     far_trio = send(trio, "far")
 
-    names = ["above", "below", "x_above", "x_below"]
+    names = ["above", "below", "x_first", "x_second"]
     first = gather_first(
         sums,
         matched,

time: 75.2 us -> 72.7 us (0.967)
  starting transfers between devices: 38.7 us -> 32.1 us
  waiting for transfers between devices: 18.7 us -> 23.1 us
    ppermute x18 -> x17, starting transfers between devices: 38.7 us -> 32.1 us  [send(): return lax.ppermute(block, both, route[name])]
    ppermute x18 -> x17, waiting for transfers between devices: 18.7 us -> 23.1 us  [send(): return lax.ppermute(block, both, route[name])]
  transfers between devices with their start and end apart: 18 -> 17, of which waited for: 5 -> 3; matrix products, arithmetic and copies ran while one was open for 0% -> 0% of each run, Pallas kernels for 15% -> 15%
where the time goes in v4:
time: 72.7 us; the launch traced here: 72.5 us
  starting transfers between devices  32.1 us (44%)
  waiting for transfers between devices  23.1 us (32%)
  Pallas kernels  17 us (23%)
    ppermute x17, starting transfers between devices, send(): return lax.ppermute(block, both, route[name])  32.1 us
    ppermute x17, waiting for transfers between devices, send(): return lax.ppermute(block, both, route[name])  23.1 us
    pallas_call x7, Pallas kernels, pair_tile(): call(tile_kernel, 'pair_tile', [held] * 3, [held] * 2, [pltpu.VMEM((rows,...  5.86 us
    pallas_call x1, Pallas kernels, gather_final(): call(functools.partial(final_kernel, count), 'gather_final', [held] * (2...  3.42 us
    pallas_call x1, Pallas kernels, gather_first(): call(functools.partial(first_kernel, count), 'gather_first', [held] * (2...  3.38 us
    pallas_call x1, Pallas kernels, self_tile(): call(self_kernel, 'self_tile', [held, small], [held] * 3, [pltpu.VMEM((ro...  1.53 us
  transfers between devices with their start and end apart: 17, of which 3 were waited for; matrix products, arithmetic and copies ran while one was open for 0% of the time, Pallas kernels for 15%

profile of v4, /device:TPU:1, one launch (start us, length us, event | category | flops | bytes accessed | tf_op | source)
XLA Modules:
  0.0 72.5 jit_solution(18107014875177042043)
XLA Ops:
  0.0 0.0 copy-start
  0.0 1.4 %normalize.1.mine_ref.refs_5_ = bf16[768,512]{1,0:T(8,128)(2,1)S(1)} custom-call(bf16[768,512]{1,0:T(8,128)(2,1)} %rows_ref.1), custom_call_target="tpu_custom_call" | custom-call | flops 1572864 | bytes 1572864 | tf_op jit(solution)/shard_map/normalize/pallas_call | solution.py:129
  1.4 3.3 %collective-permute-start.2 = (bf16[768,512]{1,0:T(8,128)(2,1)S(1)}, bf16[768,512]{1,0:T(8,128)(2,1)S(1)}, u32[]{:S(2)}, u32[]{:S(2)}) collective-permute-start(bf16[768,512]{1,0:T(8,128)(2,1)S(1)} %normalize.1.mine_ref.refs_5_), channel_id=1, source_target_pairs={{16,0},{17,1},{18,2},{19,3},{20,4},{21,5},{22,6},{23,7},{24,8},{25... | collective-permute-start | bytes 2359304 | tf_op jit(solution)/shard_map/ppermute | solution.py:418
  4.7 3.9 %collective-permute-start.1 = (bf16[768,512]{1,0:T(8,128)(2,1)S(1)}, bf16[768,512]{1,0:T(8,128)(2,1)S(1)}, u32[]{:S(2)}, u32[]{:S(2)}) collective-permute-start(bf16[768,512]{1,0:T(8,128)(2,1)S(1)} %normalize.1.mine_ref.refs_5_), channel_id=1, source_target_pairs={{1,0},{2,1},{3,2},{4,3},{5,4},{6,5},{7,6},{0,7},{9,8},{10,9},{11,1... | collective-permute-start | bytes 2359304 | tf_op jit(solution)/shard_map/ppermute | solution.py:418
  8.6 0.0 collective-permute-start
  8.6 3.2 %collective-permute-start.6 = (bf16[768,512]{1,0:T(8,128)(2,1)S(1)}, bf16[768,512]{1,0:T(8,128)(2,1)S(1)}, u32[]{:S(2)}, u32[]{:S(2)}) collective-permute-start(bf16[768,512]{1,0:T(8,128)(2,1)S(1)} %normalize.1.mine_ref.refs_5_), channel_id=1, source_target_pairs={{240,0},{241,1},{242,2},{243,3},{244,4},{245,5},{246,6},{247,7},{2... | collective-permute-start | bytes 2359304 | tf_op jit(solution)/shard_map/ppermute | solution.py:418
  11.7 0.0 copy-done
  11.7 1.5 %self_tile.1 = (bf16[768,768]{1,0:T(8,128)(2,1)S(1)}, f32[768,128]{1,0:T(8,128)S(1)}, bf16[768,512]{1,0:T(8,128)(2,1)S(1)}) custom-call(bf16[768,512]{1,0:T(8,128)(2,1)S(1)} %normalize.1.mine_ref.refs_5_, s32[6,128]{1,0:T(8,128)S(1)} %bitcast.1), custom_call_target="tpu_custom_call" | custom-call | flops 1207959552 | bytes 2752512 | tf_op jit(solution)/shard_map/self_tile/pallas_call | solution.py:175
  13.3 0.0 collective-permute-done.2.near_ref.theirs_ref.refs_4_
  13.3 2.6 %collective-permute-start.5 = (bf16[768,512]{1,0:T(8,128)(2,1)S(1)}, bf16[768,512]{1,0:T(8,128)(2,1)S(1)}, u32[]{:S(2)}, u32[]{:S(2)}) collective-permute-start(bf16[768,512]{1,0:T(8,128)(2,1)S(1)} %normalize.1.mine_ref.refs_5_), channel_id=1, source_target_pairs={{192,0},{193,1},{194,2},{195,3},{196,4},{197,5},{198,6},{199,7},{2... | collective-permute-start | bytes 2359304 | tf_op jit(solution)/shard_map/ppermute | solution.py:418
  15.9 0.0 collective-permute-start.4
  15.9 9.6 %collective-permute-done.1.above_ref.ring_ref = bf16[768,512]{1,0:T(8,128)(2,1)S(1)} collective-permute-done((bf16[768,512]{1,0:T(8,128)(2,1)S(1)}, bf16[768,512]{1,0:T(8,128)(2,1)S(1)}, u32[]{:S(2)}, u32[]{:S(2)}) %collective-permute-start.1) | collective-permute-done | bytes 786464 | tf_op jit(solution)/shard_map/ppermute | solution.py:418
  25.5 3.1 %collective-permute-done.below_ref.ring_ref = bf16[768,512]{1,0:T(8,128)(2,1)S(1)} collective-permute-done((bf16[768,512]{1,0:T(8,128)(2,1)S(1)}, bf16[768,512]{1,0:T(8,128)(2,1)S(1)}, u32[]{:S(2)}, u32[]{:S(2)}) %collective-permute-start) | collective-permute-done | bytes 786464 | tf_op jit(solution)/shard_map/ppermute | solution.py:418
  28.6 0.1 turn.1
  28.6 1.4 %collective-permute-start.3 = (bf16[768,512]{1,0:T(8,128)(2,1)S(1)}, bf16[768,512]{1,0:T(8,128)(2,1)S(1)}, u32[]{:S(2)}, u32[]{:S(2)}) collective-permute-start(bf16[768,512]{1,0:T(8,128)(2,1)S(1)} %turn.1), channel_id=1, source_target_pairs={{248,255},{17,1},{18,2},{19,3},{20,4},{21,5},{22,6},{15,7},{0,8},{... | collective-permute-start | bytes 2359304 | tf_op jit(solution)/shard_map/ppermute | solution.py:418
  30.0 0.0 collective-permute-done.6.far_ref.theirs_ref.refs_5_
  30.0 0.1 far17.1
  30.1 0.7 collective-permute-start.7
  30.8 2.1 %collective-permute-start.9 = (bf16[768,512]{1,0:T(8,128)(2,1)S(1)}, bf16[768,512]{1,0:T(8,128)(2,1)S(1)}, u32[]{:S(2)}, u32[]{:S(2)}) collective-permute-start(bf16[768,512]{1,0:T(8,128)(2,1)S(1)} %far17.1), channel_id=1, source_target_pairs={{47,63},{0,1},{1,2},{2,3},{3,4},{4,5},{5,6},{6,7},{231,8},{8,9},{9... | collective-permute-start | bytes 2359304 | tf_op jit(solution)/shard_map/ppermute | solution.py:418
  32.9 0.8 %pair_tile.7 = (bf16[768,768]{1,0:T(8,128)(2,1)S(1)}, f32[768,128]{1,0:T(8,128)S(1)}) custom-call(bf16[768,512]{1,0:T(8,128)(2,1)S(1)} %normalize.1.mine_ref.refs_5_, bf16[768,512]{1,0:T(8,128)(2,1)S(1)} %collective-permute-done.2.near_ref.theirs_ref.refs_4_, f32[768,128]{1,0:T(8,128)S(1)} %get-tuple-element.39.before_ref), custom_call_target="tpu_custom_call" | custom-call | flops 603979776 | bytes 2752512 | tf_op jit(solution)/shard_map/pair_tile/pallas_call | solution.py:200
  33.8 0.8 %pair_tile.8 = (bf16[768,768]{1,0:T(8,128)(2,1)S(1)}, f32[768,128]{1,0:T(8,128)S(1)}) custom-call(bf16[768,512]{1,0:T(8,128)(2,1)S(1)} %normalize.1.mine_ref.refs_5_, bf16[768,512]{1,0:T(8,128)(2,1)S(1)} %collective-permute-done.6.far_ref.theirs_ref.refs_5_, f32[768,128]{1,0:T(8,128)S(1)} %get-tuple-element.40.before_ref), custom_call_target="tpu_custom_call" | custom-call | flops 603979776 | bytes 2752512 | tf_op jit(solution)/shard_map/pair_tile/pallas_call | solution.py:200
  34.6 0.0 collective-permute-done.5.theirs_ref.refs_8_
  34.6 2.8 %collective-permute-start.10 = (bf16[768,512]{1,0:T(8,128)(2,1)S(1)}, bf16[768,512]{1,0:T(8,128)(2,1)S(1)}, u32[]{:S(2)}, u32[]{:S(2)}) collective-permute-start(bf16[768,512]{1,0:T(8,128)(2,1)S(1)} %collective-permute-done.5.theirs_ref.refs_8_), channel_id=1, source_target_pairs={{0,16},{1,17},{2,18},{3,19},{4,20},{5,21},{6,22},{7,23},{8,24},{9,... | collective-permute-start | bytes 2359304 | tf_op jit(solution)/shard_map/ppermute | solution.py:418
  37.4 0.8 %pair_tile.9 = (bf16[768,768]{1,0:T(8,128)(2,1)S(1)}, f32[768,128]{1,0:T(8,128)S(1)}) custom-call(bf16[768,512]{1,0:T(8,128)(2,1)S(1)} %normalize.1.mine_ref.refs_5_, bf16[768,512]{1,0:T(8,128)(2,1)S(1)} %collective-permute-done.5.theirs_ref.refs_8_, f32[768,128]{1,0:T(8,128)S(1)} %get-tuple-element.41.before_ref), custom_call_target="tpu_custom_call" | custom-call | flops 603979776 | bytes 2752512 | tf_op jit(solution)/shard_map/pair_tile/pallas_call | solution.py:200
  38.2 0.0 collective-permute-done.4.theirs_ref.refs_9_
  38.2 0.8 %pair_tile.10 = (bf16[768,768]{1,0:T(8,128)(2,1)S(1)}, f32[768,128]{1,0:T(8,128)S(1)}) custom-call(bf16[768,512]{1,0:T(8,128)(2,1)S(1)} %normalize.1.mine_ref.refs_5_, bf16[768,512]{1,0:T(8,128)(2,1)S(1)} %collective-permute-done.4.theirs_ref.refs_9_, f32[768,128]{1,0:T(8,128)S(1)} %get-tuple-element.42.before_ref), custom_call_target="tpu_custom_call" | custom-call | flops 603979776 | bytes 2752512 | tf_op jit(solution)/shard_map/pair_tile/pallas_call | solution.py:200
  39.1 10.4 %collective-permute-done.3.turn_ref = bf16[768,512]{1,0:T(8,128)(2,1)S(1)} collective-permute-done((bf16[768,512]{1,0:T(8,128)(2,1)S(1)}, bf16[768,512]{1,0:T(8,128)(2,1)S(1)}, u32[]{:S(2)}, u32[]{:S(2)}) %collective-permute-start.3) | collective-permute-done | bytes 786464 | tf_op jit(solution)/shard_map/ppermute | solution.py:418
  49.5 0.0 collective-permute-done.7.row_ref
  49.5 0.1 above.1.above_ref.theirs_ref.refs_6_
  49.5 0.1 below.1.below_ref.theirs_ref.refs_7_
  49.6 0.1 near17.1
  49.7 0.3 collective-permute-start.8
  50.0 0.8 %pair_tile.11 = (bf16[768,768]{1,0:T(8,128)(2,1)S(1)}, f32[768,128]{1,0:T(8,128)S(1)}) custom-call(bf16[768,512]{1,0:T(8,128)(2,1)S(1)} %normalize.1.mine_ref.refs_5_, bf16[768,512]{1,0:T(8,128)(2,1)S(1)} %above.1.above_ref.theirs_ref.refs_6_, f32[768,128]{1,0:T(8,128)S(1)} %get-tuple-element.45.before_ref), custom_call_target="tpu_custom_call" | custom-call | flops 603979776 | bytes 2752512 | tf_op jit(solution)/shard_map/pair_tile/pallas_call | solution.py:200
  50.8 0.8 %pair_tile.12 = (bf16[768,768]{1,0:T(8,128)(2,1)S(1)}, f32[768,128]{1,0:T(8,128)S(1)}) custom-call(bf16[768,512]{1,0:T(8,128)(2,1)S(1)} %normalize.1.mine_ref.refs_5_, bf16[768,512]{1,0:T(8,128)(2,1)S(1)} %below.1.below_ref.theirs_ref.refs_7_, f32[768,128]{1,0:T(8,128)S(1)} %get-tuple-element.46.before_ref), custom_call_target="tpu_custom_call" | custom-call | flops 603979776 | bytes 2752512 | tf_op jit(solution)/shard_map/pair_tile/pallas_call | solution.py:200
  51.7 0.0 collective-permute-done.9.far17_ref
  51.7 0.0 collective-permute-done.10.corner_ref
  51.7 0.1 corner.1.theirs_ref.refs_7_
  51.8 0.8 %pair_tile.13 = (bf16[768,768]{1,0:T(8,128)(2,1)S(1)}, f32[768,128]{1,0:T(8,128)S(1)}) custom-call(bf16[768,512]{1,0:T(8,128)(2,1)S(1)} %normalize.1.mine_ref.refs_5_, bf16[768,512]{1,0:T(8,128)(2,1)S(1)} %corner.1.theirs_ref.refs_7_, f32[768,128]{1,0:T(8,128)S(1)} %get-tuple-element.47.before_ref), custom_call_target="tpu_custom_call" | custom-call | flops 603979776 | bytes 2752512 | tf_op jit(solution)/shard_map/pair_tile/pallas_call | solution.py:200
  52.6 0.0 collective-permute-done.8.theirs_ref.refs_6_
  52.6 1.0 %last_tile.1 = (bf16[768,768]{1,0:T(8,128)(2,1)S(1)}, f32[768,128]{1,0:T(8,128)S(1)}, f32[1,768]{1,0:T(1,128)S(1)}) custom-call(bf16[768,512]{1,0:T(8,128)(2,1)S(1)} %normalize.1.mine_ref.refs_5_, bf16[768,512]{1,0:T(8,128)(2,1)S(1)} %collective-permute-done.8.theirs_ref.refs_6_, f32[768,128]{1,0:T(8,128)S(1)} %get-tuple-element.48.before_ref), custom_call_target="tpu_custom_call" | custom-call | flops 603979776 | bytes 2752512 | tf_op jit(solution)/shard_map/last_tile/pallas_call | solution.py:223
  53.6 3.5 %collective-permute-start.12 = (f32[1,768]{1,0:T(1,128)S(1)}, f32[1,768]{1,0:T(1,128)S(1)}, u32[]{:S(2)}, u32[]{:S(2)}) collective-permute-start(f32[1,768]{1,0:T(1,128)S(1)} %get-tuple-element.56.mine_ref), channel_id=1, source_target_pairs={{255,0},{2,1},{1,2},{4,3},{3,4},{6,5},{5,6},{8,7},{7,8},{10,9},{9,... | collective-permute-start | bytes 9224 | tf_op jit(solution)/shard_map/ppermute | solution.py:418
  57.1 0.0 collective-permute-start.11
  57.1 3.0 %collective-permute-start.14 = (f32[1,768]{1,0:T(1,128)S(1)}, f32[1,768]{1,0:T(1,128)S(1)}, u32[]{:S(2)}, u32[]{:S(2)}) collective-permute-start(f32[1,768]{1,0:T(1,128)S(1)} %get-tuple-element.56.mine_ref), channel_id=1, source_target_pairs={{192,0},{193,1},{194,2},{195,3},{196,4},{197,5},{198,6},{199,7},{2... | collective-permute-start | bytes 9224 | tf_op jit(solution)/shard_map/ppermute | solution.py:418
  60.1 0.0 collective-permute-start.13
  60.1 0.0 collective-permute-done.12.odd_ref
  60.1 0.0 collective-permute-done.11.even_ref
  60.1 4.8 %collective-permute-start.16 = (f32[3,768]{1,0:T(4,128)S(1)}, f32[3,768]{1,0:T(4,128)S(1)}, u32[]{:S(2)}, u32[]{:S(2)}) collective-permute-start(f32[3,768]{1,0:T(4,128)S(1)} %trio.1.refs_10_), channel_id=1, source_target_pairs={{240,0},{241,1},{242,2},{243,3},{244,4},{245,5},{246,6},{247,7},{2... | collective-permute-start | bytes 27656 | tf_op jit(solution)/shard_map/ppermute | solution.py:418
  64.9 0.6 collective-permute-start.15
  65.6 0.0 collective-permute-done.14.refs_12_
  65.6 0.0 collective-permute-done.13.refs_11_
  65.6 3.4 %gather_first.1.first_ref = f32[768,512]{1,0:T(8,128)S(1)} custom-call(f32[768,128]{1,0:T(8,128)S(1)} %get-tuple-element.49.sums_ref, bf16[768,512]{1,0:T(8,128)(2,1)S(1)} %get-tuple-element.50.matched_ref, bf16[768,768]{1,0:T(8,128)(2,1)S(1)} %get-tuple-element.51.refs_0_, bf16[768,768]{1,0:T(8,128)(2,1)S(1)} %get-tuple-element.52.refs_1_, ...), custom_call_target="tpu_custom_call" | custom-call | flops 3019898880 | bytes 12976128 | tf_op jit(solution)/shard_map/gather_first/pallas_call | solution.py:365
  68.9 0.0 collective-permute-done.16.refs_9_
  69.0 0.0 collective-permute-done.15.refs_8_
  69.0 3.4 %gather_final.1 = f32[768,512]{1,0:T(8,128)} custom-call(f32[768,128]{1,0:T(8,128)S(1)} %get-tuple-element.49.sums_ref, f32[768,512]{1,0:T(8,128)S(1)} %gather_first.1.first_ref, bf16[768,768]{1,0:T(8,128)(2,1)S(1)} %get-tuple-element.57.refs_0_, bf16[768,768]{1,0:T(8,128)(2,1)S(1)} %get-tuple-element.58.refs_1_, ...), custom_call_target="tpu_custom_call" | custom-call | flops 2415919104 | bytes 11010048 | tf_op jit(solution)/shard_map/gather_final/pallas_call | solution.py:378
  (1 shorter events, 0.0 us)
Async XLA Ops:
  0.0 11.7 %copy-start = (s32[768]{0:T(1024)S(1)}, s32[768]{0:T(1024)}, u32[]{:S(2)}) copy-start(s32[768]{0:T(1024)} %param.3) | copy-start | bytes 9220
  1.4 11.9 %collective-permute-start.2 = (bf16[768,512]{1,0:T(8,128)(2,1)S(1)}, bf16[768,512]{1,0:T(8,128)(2,1)S(1)}, u32[]{:S(2)}, u32[]{:S(2)}) collective-permute-start(bf16[768,512]{1,0:T(8,128)(2,1)S(1)} %normalize.1.mine_ref.refs_5_), channel_id=1, source_target_pairs={{16,0},{17,1},{18,2},{19,3},{20,4},{21,5},{22,6},{23,7},{24,8},{25... | collective-permute-start | bytes 2359304 | tf_op jit(solution)/shard_map/ppermute | solution.py:418
  4.7 20.7 %collective-permute-start.1 = (bf16[768,512]{1,0:T(8,128)(2,1)S(1)}, bf16[768,512]{1,0:T(8,128)(2,1)S(1)}, u32[]{:S(2)}, u32[]{:S(2)}) collective-permute-start(bf16[768,512]{1,0:T(8,128)(2,1)S(1)} %normalize.1.mine_ref.refs_5_), channel_id=1, source_target_pairs={{1,0},{2,1},{3,2},{4,3},{5,4},{6,5},{7,6},{0,7},{9,8},{10,9},{11,1... | collective-permute-start | bytes 2359304 | tf_op jit(solution)/shard_map/ppermute | solution.py:418
  8.6 20.0 %collective-permute-start = (bf16[768,512]{1,0:T(8,128)(2,1)S(1)}, bf16[768,512]{1,0:T(8,128)(2,1)S(1)}, u32[]{:S(2)}, u32[]{:S(2)}) collective-permute-start(bf16[768,512]{1,0:T(8,128)(2,1)S(1)} %normalize.1.mine_ref.refs_5_), channel_id=1, source_target_pairs={{7,0},{0,1},{1,2},{2,3},{3,4},{4,5},{5,6},{6,7},{15,8},{8,9},{9,10... | collective-permute-start | bytes 2359304 | tf_op jit(solution)/shard_map/ppermute | solution.py:418
  8.6 21.4 %collective-permute-start.6 = (bf16[768,512]{1,0:T(8,128)(2,1)S(1)}, bf16[768,512]{1,0:T(8,128)(2,1)S(1)}, u32[]{:S(2)}, u32[]{:S(2)}) collective-permute-start(bf16[768,512]{1,0:T(8,128)(2,1)S(1)} %normalize.1.mine_ref.refs_5_), channel_id=1, source_target_pairs={{240,0},{241,1},{242,2},{243,3},{244,4},{245,5},{246,6},{247,7},{2... | collective-permute-start | bytes 2359304 | tf_op jit(solution)/shard_map/ppermute | solution.py:418
  13.3 21.3 %collective-permute-start.5 = (bf16[768,512]{1,0:T(8,128)(2,1)S(1)}, bf16[768,512]{1,0:T(8,128)(2,1)S(1)}, u32[]{:S(2)}, u32[]{:S(2)}) collective-permute-start(bf16[768,512]{1,0:T(8,128)(2,1)S(1)} %normalize.1.mine_ref.refs_5_), channel_id=1, source_target_pairs={{192,0},{193,1},{194,2},{195,3},{196,4},{197,5},{198,6},{199,7},{2... | collective-permute-start | bytes 2359304 | tf_op jit(solution)/shard_map/ppermute | solution.py:418
  15.9 22.4 %collective-permute-start.4 = (bf16[768,512]{1,0:T(8,128)(2,1)S(1)}, bf16[768,512]{1,0:T(8,128)(2,1)S(1)}, u32[]{:S(2)}, u32[]{:S(2)}) collective-permute-start(bf16[768,512]{1,0:T(8,128)(2,1)S(1)} %normalize.1.mine_ref.refs_5_), channel_id=1, source_target_pairs={{64,0},{65,1},{66,2},{67,3},{68,4},{69,5},{70,6},{71,7},{72,8},{73... | collective-permute-start | bytes 2359304 | tf_op jit(solution)/shard_map/ppermute | solution.py:418
  28.6 20.8 %collective-permute-start.3 = (bf16[768,512]{1,0:T(8,128)(2,1)S(1)}, bf16[768,512]{1,0:T(8,128)(2,1)S(1)}, u32[]{:S(2)}, u32[]{:S(2)}) collective-permute-start(bf16[768,512]{1,0:T(8,128)(2,1)S(1)} %turn.1), channel_id=1, source_target_pairs={{248,255},{17,1},{18,2},{19,3},{20,4},{21,5},{22,6},{15,7},{0,8},{... | collective-permute-start | bytes 2359304 | tf_op jit(solution)/shard_map/ppermute | solution.py:418
  30.1 19.4 %collective-permute-start.7 = (bf16[768,512]{1,0:T(8,128)(2,1)S(1)}, bf16[768,512]{1,0:T(8,128)(2,1)S(1)}, u32[]{:S(2)}, u32[]{:S(2)}) collective-permute-start(bf16[768,512]{1,0:T(8,128)(2,1)S(1)} %collective-permute-done.6.far_ref.theirs_ref.refs_5_), channel_id=1, source_target_pairs={{15,0},{48,63},{79,64},{112,127},{143,128},{176,191},{207,192},{24... | collective-permute-start | bytes 2359304 | tf_op jit(solution)/shard_map/ppermute | solution.py:418
  30.8 20.9 %collective-permute-start.9 = (bf16[768,512]{1,0:T(8,128)(2,1)S(1)}, bf16[768,512]{1,0:T(8,128)(2,1)S(1)}, u32[]{:S(2)}, u32[]{:S(2)}) collective-permute-start(bf16[768,512]{1,0:T(8,128)(2,1)S(1)} %far17.1), channel_id=1, source_target_pairs={{47,63},{0,1},{1,2},{2,3},{3,4},{4,5},{5,6},{6,7},{231,8},{8,9},{9... | collective-permute-start | bytes 2359304 | tf_op jit(solution)/shard_map/ppermute | solution.py:418
  34.6 17.1 %collective-permute-start.10 = (bf16[768,512]{1,0:T(8,128)(2,1)S(1)}, bf16[768,512]{1,0:T(8,128)(2,1)S(1)}, u32[]{:S(2)}, u32[]{:S(2)}) collective-permute-start(bf16[768,512]{1,0:T(8,128)(2,1)S(1)} %collective-permute-done.5.theirs_ref.refs_8_), channel_id=1, source_target_pairs={{0,16},{1,17},{2,18},{3,19},{4,20},{5,21},{6,22},{7,23},{8,24},{9,... | collective-permute-start | bytes 2359304 | tf_op jit(solution)/shard_map/ppermute | solution.py:418
  49.7 2.9 %collective-permute-start.8 = (bf16[768,512]{1,0:T(8,128)(2,1)S(1)}, bf16[768,512]{1,0:T(8,128)(2,1)S(1)}, u32[]{:S(2)}, u32[]{:S(2)}) collective-permute-start(bf16[768,512]{1,0:T(8,128)(2,1)S(1)} %near17.1), channel_id=1, source_target_pairs={{16,0},{17,1},{18,2},{19,3},{20,4},{21,5},{22,6},{23,7},{24,8},{25... | collective-permute-start | bytes 2359304 | tf_op jit(solution)/shard_map/ppermute | solution.py:418
  53.6 6.5 %collective-permute-start.12 = (f32[1,768]{1,0:T(1,128)S(1)}, f32[1,768]{1,0:T(1,128)S(1)}, u32[]{:S(2)}, u32[]{:S(2)}) collective-permute-start(f32[1,768]{1,0:T(1,128)S(1)} %get-tuple-element.56.mine_ref), channel_id=1, source_target_pairs={{255,0},{2,1},{1,2},{4,3},{3,4},{6,5},{5,6},{8,7},{7,8},{10,9},{9,... | collective-permute-start | bytes 9224 | tf_op jit(solution)/shard_map/ppermute | solution.py:418
  57.1 3.0 %collective-permute-start.11 = (f32[1,768]{1,0:T(1,128)S(1)}, f32[1,768]{1,0:T(1,128)S(1)}, u32[]{:S(2)}, u32[]{:S(2)}) collective-permute-start(f32[1,768]{1,0:T(1,128)S(1)} %get-tuple-element.56.mine_ref), channel_id=1, source_target_pairs={{1,0},{0,1},{3,2},{2,3},{5,4},{4,5},{7,6},{6,7},{9,8},{8,9},{11,10... | collective-permute-start | bytes 9224 | tf_op jit(solution)/shard_map/ppermute | solution.py:418
  57.1 8.5 %collective-permute-start.14 = (f32[1,768]{1,0:T(1,128)S(1)}, f32[1,768]{1,0:T(1,128)S(1)}, u32[]{:S(2)}, u32[]{:S(2)}) collective-permute-start(f32[1,768]{1,0:T(1,128)S(1)} %get-tuple-element.56.mine_ref), channel_id=1, source_target_pairs={{192,0},{193,1},{194,2},{195,3},{196,4},{197,5},{198,6},{199,7},{2... | collective-permute-start | bytes 9224 | tf_op jit(solution)/shard_map/ppermute | solution.py:418
  60.1 5.5 %collective-permute-start.13 = (f32[1,768]{1,0:T(1,128)S(1)}, f32[1,768]{1,0:T(1,128)S(1)}, u32[]{:S(2)}, u32[]{:S(2)}) collective-permute-start(f32[1,768]{1,0:T(1,128)S(1)} %get-tuple-element.56.mine_ref), channel_id=1, source_target_pairs={{64,0},{65,1},{66,2},{67,3},{68,4},{69,5},{70,6},{71,7},{72,8},{73... | collective-permute-start | bytes 9224 | tf_op jit(solution)/shard_map/ppermute | solution.py:418
  60.1 8.8 %collective-permute-start.16 = (f32[3,768]{1,0:T(4,128)S(1)}, f32[3,768]{1,0:T(4,128)S(1)}, u32[]{:S(2)}, u32[]{:S(2)}) collective-permute-start(f32[3,768]{1,0:T(4,128)S(1)} %trio.1.refs_10_), channel_id=1, source_target_pairs={{240,0},{241,1},{242,2},{243,3},{244,4},{245,5},{246,6},{247,7},{2... | collective-permute-start | bytes 27656 | tf_op jit(solution)/shard_map/ppermute | solution.py:418
  64.9 4.0 %collective-permute-start.15 = (f32[3,768]{1,0:T(4,128)S(1)}, f32[3,768]{1,0:T(4,128)S(1)}, u32[]{:S(2)}, u32[]{:S(2)}) collective-permute-start(f32[3,768]{1,0:T(4,128)S(1)} %trio.1.refs_10_), channel_id=1, source_target_pairs={{16,0},{17,1},{18,2},{19,3},{20,4},{21,5},{22,6},{23,7},{24,8},{25... | collective-permute-start | bytes 27656 | tf_op jit(solution)/shard_map/ppermute | solution.py:418

commit v5 on v4

--- a/solution.py
+++ b/solution.py
@@ -266,7 +266,7 @@
         out_ref[...] = far17_ref[...]
 
 
-def turn_kernel(above_ref, below_ref, out_ref):
+def turn_kernel(below_ref, above_ref, out_ref):
     line = lax.axis_size("col") // 2
     place = lax.axis_index("col") % line
 
@@ -419,15 +419,15 @@
 
     normed = normalize(embeddings)
     near = send(normed, "near")
+    ring_below = send(normed, "ring_below")
     ring_above = send(normed, "ring_above")
-    ring_below = send(normed, "ring_below")
     far = send(normed, "far")
     self_exps, sums, matched = self_tile(normed, positives.reshape(-1, lanes))
     later, near, sums = lax.optimization_barrier((normed, near, sums))
     x_first = send(later, "x_first")
     x_second = send(later, "x_second")
-    ring_above, sums = lax.optimization_barrier((ring_above, sums))
-    turn = send(choose(turn_kernel, "turn", ring_above, ring_below), "turn")
+    ring_below, sums = lax.optimization_barrier((ring_below, sums))
+    turn = send(choose(turn_kernel, "turn", ring_below, ring_above), "turn")
     passed = choose(far17_kernel, "far17", far, near, normed)
     far17 = send(passed, "far17")
     far, passed = lax.optimization_barrier((far, passed))

time: 72.7 us -> 71.6 us (0.985)
  waiting for transfers between devices: 23.1 us -> 21.8 us
    ppermute x17, waiting for transfers between devices: 23.1 us -> 21.8 us  [send(): return lax.ppermute(block, both, route[name])]
  transfers between devices with their start and end apart: 17 -> 17, of which waited for: 3 -> 3; matrix products, arithmetic and copies ran while one was open for 0% -> 0% of each run, Pallas kernels for 15% -> 16%
where the time goes in v5:
time: 71.6 us; the launch traced here: 71.5 us
  starting transfers between devices  32.4 us (45%)
  waiting for transfers between devices  21.8 us (30%)
  Pallas kernels  17 us (24%)
    ppermute x17, starting transfers between devices, send(): return lax.ppermute(block, both, route[name])  32.4 us
    ppermute x17, waiting for transfers between devices, send(): return lax.ppermute(block, both, route[name])  21.8 us
    pallas_call x7, Pallas kernels, pair_tile(): call(tile_kernel, 'pair_tile', [held] * 3, [held] * 2, [pltpu.VMEM((rows,...  5.89 us
    pallas_call x1, Pallas kernels, gather_final(): call(functools.partial(final_kernel, count), 'gather_final', [held] * (2...  3.43 us
    pallas_call x1, Pallas kernels, gather_first(): call(functools.partial(first_kernel, count), 'gather_first', [held] * (2...  3.38 us
    pallas_call x1, Pallas kernels, self_tile(): call(self_kernel, 'self_tile', [held, small], [held] * 3, [pltpu.VMEM((ro...  1.54 us
  transfers between devices with their start and end apart: 17, of which 3 were waited for; matrix products, arithmetic and copies ran while one was open for 0% of the time, Pallas kernels for 16%

profile of v5, /device:TPU:1, one launch (start us, length us, event | category | flops | bytes accessed | tf_op | source)
XLA Modules:
  0.0 71.5 jit_solution(7830517861976610865)
XLA Ops:
  0.0 0.0 copy-start
  0.0 1.4 %normalize.1.mine_ref.refs_5_ = bf16[768,512]{1,0:T(8,128)(2,1)S(1)} custom-call(bf16[768,512]{1,0:T(8,128)(2,1)} %rows_ref.1), custom_call_target="tpu_custom_call" | custom-call | flops 1572864 | bytes 1572864 | tf_op jit(solution)/shard_map/normalize/pallas_call | solution.py:129
  1.4 3.3 %collective-permute-start.1 = (bf16[768,512]{1,0:T(8,128)(2,1)S(1)}, bf16[768,512]{1,0:T(8,128)(2,1)S(1)}, u32[]{:S(2)}, u32[]{:S(2)}) collective-permute-start(bf16[768,512]{1,0:T(8,128)(2,1)S(1)} %normalize.1.mine_ref.refs_5_), channel_id=1, source_target_pairs={{16,0},{17,1},{18,2},{19,3},{20,4},{21,5},{22,6},{23,7},{24,8},{25... | collective-permute-start | bytes 2359304 | tf_op jit(solution)/shard_map/ppermute | solution.py:418
  4.7 0.0 collective-permute-start
  4.7 3.8 %collective-permute-start.2 = (bf16[768,512]{1,0:T(8,128)(2,1)S(1)}, bf16[768,512]{1,0:T(8,128)(2,1)S(1)}, u32[]{:S(2)}, u32[]{:S(2)}) collective-permute-start(bf16[768,512]{1,0:T(8,128)(2,1)S(1)} %normalize.1.mine_ref.refs_5_), channel_id=1, source_target_pairs={{1,0},{2,1},{3,2},{4,3},{5,4},{6,5},{7,6},{0,7},{9,8},{10,9},{11,1... | collective-permute-start | bytes 2359304 | tf_op jit(solution)/shard_map/ppermute | solution.py:418
  8.6 3.3 %collective-permute-start.6 = (bf16[768,512]{1,0:T(8,128)(2,1)S(1)}, bf16[768,512]{1,0:T(8,128)(2,1)S(1)}, u32[]{:S(2)}, u32[]{:S(2)}) collective-permute-start(bf16[768,512]{1,0:T(8,128)(2,1)S(1)} %normalize.1.mine_ref.refs_5_), channel_id=1, source_target_pairs={{240,0},{241,1},{242,2},{243,3},{244,4},{245,5},{246,6},{247,7},{2... | collective-permute-start | bytes 2359304 | tf_op jit(solution)/shard_map/ppermute | solution.py:418
  11.8 0.0 copy-done
  11.8 1.5 %self_tile.1 = (bf16[768,768]{1,0:T(8,128)(2,1)S(1)}, f32[768,128]{1,0:T(8,128)S(1)}, bf16[768,512]{1,0:T(8,128)(2,1)S(1)}) custom-call(bf16[768,512]{1,0:T(8,128)(2,1)S(1)} %normalize.1.mine_ref.refs_5_, s32[6,128]{1,0:T(8,128)S(1)} %bitcast.1), custom_call_target="tpu_custom_call" | custom-call | flops 1207959552 | bytes 2752512 | tf_op jit(solution)/shard_map/self_tile/pallas_call | solution.py:175
  13.4 0.0 collective-permute-done.1.near_ref.theirs_ref.refs_4_
  13.4 2.5 %collective-permute-start.5 = (bf16[768,512]{1,0:T(8,128)(2,1)S(1)}, bf16[768,512]{1,0:T(8,128)(2,1)S(1)}, u32[]{:S(2)}, u32[]{:S(2)}) collective-permute-start(bf16[768,512]{1,0:T(8,128)(2,1)S(1)} %normalize.1.mine_ref.refs_5_), channel_id=1, source_target_pairs={{192,0},{193,1},{194,2},{195,3},{196,4},{197,5},{198,6},{199,7},{2... | collective-permute-start | bytes 2359304 | tf_op jit(solution)/shard_map/ppermute | solution.py:418
  15.9 0.0 collective-permute-start.4
  15.9 10.5 %collective-permute-done.below_ref.ring_ref = bf16[768,512]{1,0:T(8,128)(2,1)S(1)} collective-permute-done((bf16[768,512]{1,0:T(8,128)(2,1)S(1)}, bf16[768,512]{1,0:T(8,128)(2,1)S(1)}, u32[]{:S(2)}, u32[]{:S(2)}) %collective-permute-start) | collective-permute-done | bytes 786464 | tf_op jit(solution)/shard_map/ppermute | solution.py:418
  26.4 0.0 collective-permute-done.2.above_ref.ring_ref
  26.4 0.1 turn.1
  26.5 1.4 %collective-permute-start.3 = (bf16[768,512]{1,0:T(8,128)(2,1)S(1)}, bf16[768,512]{1,0:T(8,128)(2,1)S(1)}, u32[]{:S(2)}, u32[]{:S(2)}) collective-permute-start(bf16[768,512]{1,0:T(8,128)(2,1)S(1)} %turn.1), channel_id=1, source_target_pairs={{248,255},{17,1},{18,2},{19,3},{20,4},{21,5},{22,6},{15,7},{0,8},{... | collective-permute-start | bytes 2359304 | tf_op jit(solution)/shard_map/ppermute | solution.py:418
  27.8 2.1 %collective-permute-done.6.far_ref.theirs_ref.refs_5_ = bf16[768,512]{1,0:T(8,128)(2,1)S(1)} collective-permute-done((bf16[768,512]{1,0:T(8,128)(2,1)S(1)}, bf16[768,512]{1,0:T(8,128)(2,1)S(1)}, u32[]{:S(2)}, u32[]{:S(2)}) %collective-permute-start.6) | collective-permute-done | bytes 786464 | tf_op jit(solution)/shard_map/ppermute | solution.py:418
  29.9 0.1 far17.1
  30.0 0.7 collective-permute-start.7
  30.7 1.0 %collective-permute-start.9 = (bf16[768,512]{1,0:T(8,128)(2,1)S(1)}, bf16[768,512]{1,0:T(8,128)(2,1)S(1)}, u32[]{:S(2)}, u32[]{:S(2)}) collective-permute-start(bf16[768,512]{1,0:T(8,128)(2,1)S(1)} %far17.1), channel_id=1, source_target_pairs={{47,63},{0,1},{1,2},{2,3},{3,4},{4,5},{5,6},{6,7},{231,8},{8,9},{9... | collective-permute-start | bytes 2359304 | tf_op jit(solution)/shard_map/ppermute | solution.py:418
  31.7 0.8 %pair_tile.7 = (bf16[768,768]{1,0:T(8,128)(2,1)S(1)}, f32[768,128]{1,0:T(8,128)S(1)}) custom-call(bf16[768,512]{1,0:T(8,128)(2,1)S(1)} %normalize.1.mine_ref.refs_5_, bf16[768,512]{1,0:T(8,128)(2,1)S(1)} %collective-permute-done.1.near_ref.theirs_ref.refs_4_, f32[768,128]{1,0:T(8,128)S(1)} %get-tuple-element.39.before_ref), custom_call_target="tpu_custom_call" | custom-call | flops 603979776 | bytes 2752512 | tf_op jit(solution)/shard_map/pair_tile/pallas_call | solution.py:200
  32.5 0.8 %pair_tile.8 = (bf16[768,768]{1,0:T(8,128)(2,1)S(1)}, f32[768,128]{1,0:T(8,128)S(1)}) custom-call(bf16[768,512]{1,0:T(8,128)(2,1)S(1)} %normalize.1.mine_ref.refs_5_, bf16[768,512]{1,0:T(8,128)(2,1)S(1)} %collective-permute-done.6.far_ref.theirs_ref.refs_5_, f32[768,128]{1,0:T(8,128)S(1)} %get-tuple-element.40.before_ref), custom_call_target="tpu_custom_call" | custom-call | flops 603979776 | bytes 2752512 | tf_op jit(solution)/shard_map/pair_tile/pallas_call | solution.py:200
  33.4 0.0 collective-permute-done.5.theirs_ref.refs_8_
  33.4 2.9 %collective-permute-start.10 = (bf16[768,512]{1,0:T(8,128)(2,1)S(1)}, bf16[768,512]{1,0:T(8,128)(2,1)S(1)}, u32[]{:S(2)}, u32[]{:S(2)}) collective-permute-start(bf16[768,512]{1,0:T(8,128)(2,1)S(1)} %collective-permute-done.5.theirs_ref.refs_8_), channel_id=1, source_target_pairs={{0,16},{1,17},{2,18},{3,19},{4,20},{5,21},{6,22},{7,23},{8,24},{9,... | collective-permute-start | bytes 2359304 | tf_op jit(solution)/shard_map/ppermute | solution.py:418
  36.3 0.8 %pair_tile.9 = (bf16[768,768]{1,0:T(8,128)(2,1)S(1)}, f32[768,128]{1,0:T(8,128)S(1)}) custom-call(bf16[768,512]{1,0:T(8,128)(2,1)S(1)} %normalize.1.mine_ref.refs_5_, bf16[768,512]{1,0:T(8,128)(2,1)S(1)} %collective-permute-done.5.theirs_ref.refs_8_, f32[768,128]{1,0:T(8,128)S(1)} %get-tuple-element.41.before_ref), custom_call_target="tpu_custom_call" | custom-call | flops 603979776 | bytes 2752512 | tf_op jit(solution)/shard_map/pair_tile/pallas_call | solution.py:200
  37.1 0.0 collective-permute-done.4.theirs_ref.refs_9_
  37.2 0.8 %pair_tile.10 = (bf16[768,768]{1,0:T(8,128)(2,1)S(1)}, f32[768,128]{1,0:T(8,128)S(1)}) custom-call(bf16[768,512]{1,0:T(8,128)(2,1)S(1)} %normalize.1.mine_ref.refs_5_, bf16[768,512]{1,0:T(8,128)(2,1)S(1)} %collective-permute-done.4.theirs_ref.refs_9_, f32[768,128]{1,0:T(8,128)S(1)} %get-tuple-element.42.before_ref), custom_call_target="tpu_custom_call" | custom-call | flops 603979776 | bytes 2752512 | tf_op jit(solution)/shard_map/pair_tile/pallas_call | solution.py:200
  38.0 9.2 %collective-permute-done.3.turn_ref = bf16[768,512]{1,0:T(8,128)(2,1)S(1)} collective-permute-done((bf16[768,512]{1,0:T(8,128)(2,1)S(1)}, bf16[768,512]{1,0:T(8,128)(2,1)S(1)}, u32[]{:S(2)}, u32[]{:S(2)}) %collective-permute-start.3) | collective-permute-done | bytes 786464 | tf_op jit(solution)/shard_map/ppermute | solution.py:418
  47.2 0.0 collective-permute-done.7.row_ref
  47.2 0.1 above.1.above_ref.theirs_ref.refs_6_
  47.2 0.1 below.1.below_ref.theirs_ref.refs_7_
  47.3 0.1 near17.1
  47.4 0.3 collective-permute-start.8
  47.7 0.9 %pair_tile.11 = (bf16[768,768]{1,0:T(8,128)(2,1)S(1)}, f32[768,128]{1,0:T(8,128)S(1)}) custom-call(bf16[768,512]{1,0:T(8,128)(2,1)S(1)} %normalize.1.mine_ref.refs_5_, bf16[768,512]{1,0:T(8,128)(2,1)S(1)} %above.1.above_ref.theirs_ref.refs_6_, f32[768,128]{1,0:T(8,128)S(1)} %get-tuple-element.45.before_ref), custom_call_target="tpu_custom_call" | custom-call | flops 603979776 | bytes 2752512 | tf_op jit(solution)/shard_map/pair_tile/pallas_call | solution.py:200
  48.6 0.8 %pair_tile.12 = (bf16[768,768]{1,0:T(8,128)(2,1)S(1)}, f32[768,128]{1,0:T(8,128)S(1)}) custom-call(bf16[768,512]{1,0:T(8,128)(2,1)S(1)} %normalize.1.mine_ref.refs_5_, bf16[768,512]{1,0:T(8,128)(2,1)S(1)} %below.1.below_ref.theirs_ref.refs_7_, f32[768,128]{1,0:T(8,128)S(1)} %get-tuple-element.46.before_ref), custom_call_target="tpu_custom_call" | custom-call | flops 603979776 | bytes 2752512 | tf_op jit(solution)/shard_map/pair_tile/pallas_call | solution.py:200
  49.4 0.0 collective-permute-done.9.far17_ref
  49.4 0.0 collective-permute-done.10.corner_ref
  49.4 0.1 corner.1.theirs_ref.refs_7_
  49.5 0.8 %pair_tile.13 = (bf16[768,768]{1,0:T(8,128)(2,1)S(1)}, f32[768,128]{1,0:T(8,128)S(1)}) custom-call(bf16[768,512]{1,0:T(8,128)(2,1)S(1)} %normalize.1.mine_ref.refs_5_, bf16[768,512]{1,0:T(8,128)(2,1)S(1)} %corner.1.theirs_ref.refs_7_, f32[768,128]{1,0:T(8,128)S(1)} %get-tuple-element.47.before_ref), custom_call_target="tpu_custom_call" | custom-call | flops 603979776 | bytes 2752512 | tf_op jit(solution)/shard_map/pair_tile/pallas_call | solution.py:200
  50.4 0.0 collective-permute-done.8.theirs_ref.refs_6_
  50.4 0.9 %last_tile.1 = (bf16[768,768]{1,0:T(8,128)(2,1)S(1)}, f32[768,128]{1,0:T(8,128)S(1)}, f32[1,768]{1,0:T(1,128)S(1)}) custom-call(bf16[768,512]{1,0:T(8,128)(2,1)S(1)} %normalize.1.mine_ref.refs_5_, bf16[768,512]{1,0:T(8,128)(2,1)S(1)} %collective-permute-done.8.theirs_ref.refs_6_, f32[768,128]{1,0:T(8,128)S(1)} %get-tuple-element.48.before_ref), custom_call_target="tpu_custom_call" | custom-call | flops 603979776 | bytes 2752512 | tf_op jit(solution)/shard_map/last_tile/pallas_call | solution.py:223
  51.3 4.6 %collective-permute-start.12 = (f32[1,768]{1,0:T(1,128)S(1)}, f32[1,768]{1,0:T(1,128)S(1)}, u32[]{:S(2)}, u32[]{:S(2)}) collective-permute-start(f32[1,768]{1,0:T(1,128)S(1)} %get-tuple-element.56.mine_ref), channel_id=1, source_target_pairs={{255,0},{2,1},{1,2},{4,3},{3,4},{6,5},{5,6},{8,7},{7,8},{10,9},{9,... | collective-permute-start | bytes 9224 | tf_op jit(solution)/shard_map/ppermute | solution.py:418
  55.9 0.0 collective-permute-start.11
  55.9 3.0 %collective-permute-start.14 = (f32[1,768]{1,0:T(1,128)S(1)}, f32[1,768]{1,0:T(1,128)S(1)}, u32[]{:S(2)}, u32[]{:S(2)}) collective-permute-start(f32[1,768]{1,0:T(1,128)S(1)} %get-tuple-element.56.mine_ref), channel_id=1, source_target_pairs={{192,0},{193,1},{194,2},{195,3},{196,4},{197,5},{198,6},{199,7},{2... | collective-permute-start | bytes 9224 | tf_op jit(solution)/shard_map/ppermute | solution.py:418
  58.8 0.0 collective-permute-start.13
  58.8 0.0 collective-permute-done.12.odd_ref
  58.9 0.0 collective-permute-done.11.even_ref
  58.9 4.8 %collective-permute-start.16 = (f32[3,768]{1,0:T(4,128)S(1)}, f32[3,768]{1,0:T(4,128)S(1)}, u32[]{:S(2)}, u32[]{:S(2)}) collective-permute-start(f32[3,768]{1,0:T(4,128)S(1)} %trio.1.refs_10_), channel_id=1, source_target_pairs={{240,0},{241,1},{242,2},{243,3},{244,4},{245,5},{246,6},{247,7},{2... | collective-permute-start | bytes 27656 | tf_op jit(solution)/shard_map/ppermute | solution.py:418
  63.7 0.8 %collective-permute-start.15 = (f32[3,768]{1,0:T(4,128)S(1)}, f32[3,768]{1,0:T(4,128)S(1)}, u32[]{:S(2)}, u32[]{:S(2)}) collective-permute-start(f32[3,768]{1,0:T(4,128)S(1)} %trio.1.refs_10_), channel_id=1, source_target_pairs={{16,0},{17,1},{18,2},{19,3},{20,4},{21,5},{22,6},{23,7},{24,8},{25... | collective-permute-start | bytes 27656 | tf_op jit(solution)/shard_map/ppermute | solution.py:418
  64.5 0.0 collective-permute-done.14.refs_12_
  64.5 0.0 collective-permute-done.13.refs_11_
  64.5 3.4 %gather_first.1.first_ref = f32[768,512]{1,0:T(8,128)S(1)} custom-call(f32[768,128]{1,0:T(8,128)S(1)} %get-tuple-element.49.sums_ref, bf16[768,512]{1,0:T(8,128)(2,1)S(1)} %get-tuple-element.50.matched_ref, bf16[768,768]{1,0:T(8,128)(2,1)S(1)} %get-tuple-element.51.refs_0_, bf16[768,768]{1,0:T(8,128)(2,1)S(1)} %get-tuple-element.52.refs_1_, ...), custom_call_target="tpu_custom_call" | custom-call | flops 3019898880 | bytes 12976128 | tf_op jit(solution)/shard_map/gather_first/pallas_call | solution.py:365
  67.9 0.0 collective-permute-done.16.refs_9_
  67.9 0.0 collective-permute-done.15.refs_8_
  68.0 3.4 %gather_final.1 = f32[768,512]{1,0:T(8,128)} custom-call(f32[768,128]{1,0:T(8,128)S(1)} %get-tuple-element.49.sums_ref, f32[768,512]{1,0:T(8,128)S(1)} %gather_first.1.first_ref, bf16[768,768]{1,0:T(8,128)(2,1)S(1)} %get-tuple-element.57.refs_0_, bf16[768,768]{1,0:T(8,128)(2,1)S(1)} %get-tuple-element.58.refs_1_, ...), custom_call_target="tpu_custom_call" | custom-call | flops 2415919104 | bytes 11010048 | tf_op jit(solution)/shard_map/gather_final/pallas_call | solution.py:378
  (1 shorter events, 0.0 us)
Async XLA Ops:
  0.0 11.8 %copy-start = (s32[768]{0:T(1024)S(1)}, s32[768]{0:T(1024)}, u32[]{:S(2)}) copy-start(s32[768]{0:T(1024)} %param.3) | copy-start | bytes 9220
  1.4 12.0 %collective-permute-start.1 = (bf16[768,512]{1,0:T(8,128)(2,1)S(1)}, bf16[768,512]{1,0:T(8,128)(2,1)S(1)}, u32[]{:S(2)}, u32[]{:S(2)}) collective-permute-start(bf16[768,512]{1,0:T(8,128)(2,1)S(1)} %normalize.1.mine_ref.refs_5_), channel_id=1, source_target_pairs={{16,0},{17,1},{18,2},{19,3},{20,4},{21,5},{22,6},{23,7},{24,8},{25... | collective-permute-start | bytes 2359304 | tf_op jit(solution)/shard_map/ppermute | solution.py:418
  4.7 21.7 %collective-permute-start = (bf16[768,512]{1,0:T(8,128)(2,1)S(1)}, bf16[768,512]{1,0:T(8,128)(2,1)S(1)}, u32[]{:S(2)}, u32[]{:S(2)}) collective-permute-start(bf16[768,512]{1,0:T(8,128)(2,1)S(1)} %normalize.1.mine_ref.refs_5_), channel_id=1, source_target_pairs={{7,0},{0,1},{1,2},{2,3},{3,4},{4,5},{5,6},{6,7},{15,8},{8,9},{9,10... | collective-permute-start | bytes 2359304 | tf_op jit(solution)/shard_map/ppermute | solution.py:418
  4.7 21.7 %collective-permute-start.2 = (bf16[768,512]{1,0:T(8,128)(2,1)S(1)}, bf16[768,512]{1,0:T(8,128)(2,1)S(1)}, u32[]{:S(2)}, u32[]{:S(2)}) collective-permute-start(bf16[768,512]{1,0:T(8,128)(2,1)S(1)} %normalize.1.mine_ref.refs_5_), channel_id=1, source_target_pairs={{1,0},{2,1},{3,2},{4,3},{5,4},{6,5},{7,6},{0,7},{9,8},{10,9},{11,1... | collective-permute-start | bytes 2359304 | tf_op jit(solution)/shard_map/ppermute | solution.py:418
  8.6 21.4 %collective-permute-start.6 = (bf16[768,512]{1,0:T(8,128)(2,1)S(1)}, bf16[768,512]{1,0:T(8,128)(2,1)S(1)}, u32[]{:S(2)}, u32[]{:S(2)}) collective-permute-start(bf16[768,512]{1,0:T(8,128)(2,1)S(1)} %normalize.1.mine_ref.refs_5_), channel_id=1, source_target_pairs={{240,0},{241,1},{242,2},{243,3},{244,4},{245,5},{246,6},{247,7},{2... | collective-permute-start | bytes 2359304 | tf_op jit(solution)/shard_map/ppermute | solution.py:418
  13.4 20.0 %collective-permute-start.5 = (bf16[768,512]{1,0:T(8,128)(2,1)S(1)}, bf16[768,512]{1,0:T(8,128)(2,1)S(1)}, u32[]{:S(2)}, u32[]{:S(2)}) collective-permute-start(bf16[768,512]{1,0:T(8,128)(2,1)S(1)} %normalize.1.mine_ref.refs_5_), channel_id=1, source_target_pairs={{192,0},{193,1},{194,2},{195,3},{196,4},{197,5},{198,6},{199,7},{2... | collective-permute-start | bytes 2359304 | tf_op jit(solution)/shard_map/ppermute | solution.py:418
  15.9 21.2 %collective-permute-start.4 = (bf16[768,512]{1,0:T(8,128)(2,1)S(1)}, bf16[768,512]{1,0:T(8,128)(2,1)S(1)}, u32[]{:S(2)}, u32[]{:S(2)}) collective-permute-start(bf16[768,512]{1,0:T(8,128)(2,1)S(1)} %normalize.1.mine_ref.refs_5_), channel_id=1, source_target_pairs={{64,0},{65,1},{66,2},{67,3},{68,4},{69,5},{70,6},{71,7},{72,8},{73... | collective-permute-start | bytes 2359304 | tf_op jit(solution)/shard_map/ppermute | solution.py:418
  26.5 20.7 %collective-permute-start.3 = (bf16[768,512]{1,0:T(8,128)(2,1)S(1)}, bf16[768,512]{1,0:T(8,128)(2,1)S(1)}, u32[]{:S(2)}, u32[]{:S(2)}) collective-permute-start(bf16[768,512]{1,0:T(8,128)(2,1)S(1)} %turn.1), channel_id=1, source_target_pairs={{248,255},{17,1},{18,2},{19,3},{20,4},{21,5},{22,6},{15,7},{0,8},{... | collective-permute-start | bytes 2359304 | tf_op jit(solution)/shard_map/ppermute | solution.py:418
  30.0 17.2 %collective-permute-start.7 = (bf16[768,512]{1,0:T(8,128)(2,1)S(1)}, bf16[768,512]{1,0:T(8,128)(2,1)S(1)}, u32[]{:S(2)}, u32[]{:S(2)}) collective-permute-start(bf16[768,512]{1,0:T(8,128)(2,1)S(1)} %collective-permute-done.6.far_ref.theirs_ref.refs_5_), channel_id=1, source_target_pairs={{15,0},{48,63},{79,64},{112,127},{143,128},{176,191},{207,192},{24... | collective-permute-start | bytes 2359304 | tf_op jit(solution)/shard_map/ppermute | solution.py:418
  30.7 18.7 %collective-permute-start.9 = (bf16[768,512]{1,0:T(8,128)(2,1)S(1)}, bf16[768,512]{1,0:T(8,128)(2,1)S(1)}, u32[]{:S(2)}, u32[]{:S(2)}) collective-permute-start(bf16[768,512]{1,0:T(8,128)(2,1)S(1)} %far17.1), channel_id=1, source_target_pairs={{47,63},{0,1},{1,2},{2,3},{3,4},{4,5},{5,6},{6,7},{231,8},{8,9},{9... | collective-permute-start | bytes 2359304 | tf_op jit(solution)/shard_map/ppermute | solution.py:418
  33.4 16.0 %collective-permute-start.10 = (bf16[768,512]{1,0:T(8,128)(2,1)S(1)}, bf16[768,512]{1,0:T(8,128)(2,1)S(1)}, u32[]{:S(2)}, u32[]{:S(2)}) collective-permute-start(bf16[768,512]{1,0:T(8,128)(2,1)S(1)} %collective-permute-done.5.theirs_ref.refs_8_), channel_id=1, source_target_pairs={{0,16},{1,17},{2,18},{3,19},{4,20},{5,21},{6,22},{7,23},{8,24},{9,... | collective-permute-start | bytes 2359304 | tf_op jit(solution)/shard_map/ppermute | solution.py:418
  47.4 3.0 %collective-permute-start.8 = (bf16[768,512]{1,0:T(8,128)(2,1)S(1)}, bf16[768,512]{1,0:T(8,128)(2,1)S(1)}, u32[]{:S(2)}, u32[]{:S(2)}) collective-permute-start(bf16[768,512]{1,0:T(8,128)(2,1)S(1)} %near17.1), channel_id=1, source_target_pairs={{16,0},{17,1},{18,2},{19,3},{20,4},{21,5},{22,6},{23,7},{24,8},{25... | collective-permute-start | bytes 2359304 | tf_op jit(solution)/shard_map/ppermute | solution.py:418
  51.3 7.5 %collective-permute-start.12 = (f32[1,768]{1,0:T(1,128)S(1)}, f32[1,768]{1,0:T(1,128)S(1)}, u32[]{:S(2)}, u32[]{:S(2)}) collective-permute-start(f32[1,768]{1,0:T(1,128)S(1)} %get-tuple-element.56.mine_ref), channel_id=1, source_target_pairs={{255,0},{2,1},{1,2},{4,3},{3,4},{6,5},{5,6},{8,7},{7,8},{10,9},{9,... | collective-permute-start | bytes 9224 | tf_op jit(solution)/shard_map/ppermute | solution.py:418
  55.9 3.0 %collective-permute-start.11 = (f32[1,768]{1,0:T(1,128)S(1)}, f32[1,768]{1,0:T(1,128)S(1)}, u32[]{:S(2)}, u32[]{:S(2)}) collective-permute-start(f32[1,768]{1,0:T(1,128)S(1)} %get-tuple-element.56.mine_ref), channel_id=1, source_target_pairs={{1,0},{0,1},{3,2},{2,3},{5,4},{4,5},{7,6},{6,7},{9,8},{8,9},{11,10... | collective-permute-start | bytes 9224 | tf_op jit(solution)/shard_map/ppermute | solution.py:418
  55.9 8.7 %collective-permute-start.14 = (f32[1,768]{1,0:T(1,128)S(1)}, f32[1,768]{1,0:T(1,128)S(1)}, u32[]{:S(2)}, u32[]{:S(2)}) collective-permute-start(f32[1,768]{1,0:T(1,128)S(1)} %get-tuple-element.56.mine_ref), channel_id=1, source_target_pairs={{192,0},{193,1},{194,2},{195,3},{196,4},{197,5},{198,6},{199,7},{2... | collective-permute-start | bytes 9224 | tf_op jit(solution)/shard_map/ppermute | solution.py:418
  58.8 5.7 %collective-permute-start.13 = (f32[1,768]{1,0:T(1,128)S(1)}, f32[1,768]{1,0:T(1,128)S(1)}, u32[]{:S(2)}, u32[]{:S(2)}) collective-permute-start(f32[1,768]{1,0:T(1,128)S(1)} %get-tuple-element.56.mine_ref), channel_id=1, source_target_pairs={{64,0},{65,1},{66,2},{67,3},{68,4},{69,5},{70,6},{71,7},{72,8},{73... | collective-permute-start | bytes 9224 | tf_op jit(solution)/shard_map/ppermute | solution.py:418
  58.9 9.1 %collective-permute-start.16 = (f32[3,768]{1,0:T(4,128)S(1)}, f32[3,768]{1,0:T(4,128)S(1)}, u32[]{:S(2)}, u32[]{:S(2)}) collective-permute-start(f32[3,768]{1,0:T(4,128)S(1)} %trio.1.refs_10_), channel_id=1, source_target_pairs={{240,0},{241,1},{242,2},{243,3},{244,4},{245,5},{246,6},{247,7},{2... | collective-permute-start | bytes 27656 | tf_op jit(solution)/shard_map/ppermute | solution.py:418
  63.7 4.2 %collective-permute-start.15 = (f32[3,768]{1,0:T(4,128)S(1)}, f32[3,768]{1,0:T(4,128)S(1)}, u32[]{:S(2)}, u32[]{:S(2)}) collective-permute-start(f32[3,768]{1,0:T(4,128)S(1)} %trio.1.refs_10_), channel_id=1, source_target_pairs={{16,0},{17,1},{18,2},{19,3},{20,4},{21,5},{22,6},{23,7},{24,8},{25... | collective-permute-start | bytes 27656 | tf_op jit(solution)/shard_map/ppermute | solution.py:418

commit v6 on v5

--- a/solution.py
+++ b/solution.py
@@ -93,13 +93,14 @@
     return [pltpu.with_memory_space_constraint(array, pltpu.VMEM) for array in arrays]
 
 
-def call(kernel, name, in_specs, out_specs, out_shape, flops, moved, exps=0, scratch=()):
+def call(kernel, name, in_specs, out_specs, out_shape, flops, moved, exps=0, scratch=(), aliases={}):
     return pl.pallas_call(
         kernel,
         in_specs=in_specs,
         out_specs=out_specs,
         out_shape=out_shape,
         scratch_shapes=scratch,
+        input_output_aliases=aliases,
         compiler_params=pltpu.CompilerParams(vmem_limit_bytes=vmem_limit),
         cost_estimate=pl.CostEstimate(flops=flops, bytes_accessed=moved, transcendentals=exps),
         name=name,
@@ -255,15 +256,11 @@
 
 
 def corner_kernel(far17_ref, corner_ref, out_ref):
-    corner = at_corner()
-
-    @pl.when(corner)
+    del far17_ref
+
+    @pl.when(at_corner())
     def _():
         out_ref[...] = corner_ref[...]
-
-    @pl.when(~corner)
-    def _():
-        out_ref[...] = far17_ref[...]
 
 
 def turn_kernel(below_ref, above_ref, out_ref):
@@ -301,7 +298,7 @@
         out_ref[...] = above_ref[...]
 
 
-def choose(kernel, name, *choices):
+def choose(kernel, name, *choices, aliases={}):
     shape = choices[0].shape
     return call(
         kernel,
@@ -311,6 +308,7 @@
         pltpu.VMEM(shape, jnp.bfloat16),
         0,
         4 * shape[0] * shape[1],
+        aliases=aliases,
     )(*hold(*choices))
 
 
@@ -342,7 +340,7 @@
 
 def final_kernel(count, sums_ref, first_ref, *refs):
     exps_refs, block_refs = refs[:count], refs[count : 2 * count]
-    near_ref, far_ref, out_ref, held_ref, sems = refs[2 * count :]
+    far_ref, near_ref, out_ref, held_ref, sems = refs[2 * count :]
     core0 = lax.axis_index("row") % 2 == 0
     near17 = jnp.where(core0, near_ref[1:2, :], near_ref[2:3, :])
     far17 = jnp.where(core0, far_ref[2:3, :], far_ref[1:2, :])
@@ -373,7 +371,7 @@
     )(*hold(sums, matched, *exps, *blocks, *norms))
 
 
-def gather_final(sums, first, exps, blocks, near_trio, far_trio):
+def gather_final(sums, first, exps, blocks, far_trio, near_trio):
     count, (rows, width) = len(exps), first.shape
     return call(
         functools.partial(final_kernel, count),
@@ -387,17 +385,17 @@
             pltpu.VMEM((rows, width), jnp.float32),
             pltpu.SemaphoreType.DMA((rows // chunk + 1,)),
         ],
-    )(*hold(sums, first, *exps, *blocks, near_trio, far_trio))
-
-
-def trio_kernel(mine_ref, even_ref, odd_ref, out_ref):
+    )(*hold(sums, first, *exps, *blocks, far_trio, near_trio))
+
+
+def trio_kernel(mine_ref, odd_ref, even_ref, out_ref):
     even = lax.axis_index("col") % 2 == 0
     out_ref[0:1, :] = mine_ref[...]
     out_ref[1:2, :] = jnp.where(even, even_ref[...], odd_ref[...])
     out_ref[2:3, :] = jnp.where(even, odd_ref[...], even_ref[...])
 
 
-def trio_of(mine, even, odd):
+def trio_of(mine, odd, even):
     width = mine.shape[1]
     return call(
         trio_kernel,
@@ -407,7 +405,7 @@
         pltpu.VMEM((3, width), jnp.float32),
         0,
         24 * width,
-    )(*hold(mine, even, odd))
+    )(*hold(mine, odd, even))
 
 
 def on_device(embeddings, positives):
@@ -447,15 +445,15 @@
     below = choose(functools.partial(merge_kernel, 0, 0), "below", ring_below, turn, across)
     near17 = send(choose(near17_kernel, "near17", below, above), "near")
     sums = add(sums, above=above, below=below)
-    sums = add(sums, far17=choose(corner_kernel, "corner", far17, corner))
+    sums = add(sums, far17=choose(corner_kernel, "corner", far17, corner, aliases={0: 0}))
     blocks["near17"] = near17
     exps["near17"], sums, denoms = last_tile(normed, near17, sums)
 
-    trio = trio_of(denoms, send(denoms, "even"), send(denoms, "odd"))
+    trio = trio_of(denoms, send(denoms, "odd"), send(denoms, "even"))
     d_x_even = send(denoms, "x_even")
     d_x_odd = send(denoms, "x_odd")
+    far_trio = send(trio, "far")
     near_trio = send(trio, "near")
-    far_trio = send(trio, "far")
 
     names = ["above", "below", "x_first", "x_second"]
     first = gather_first(
@@ -471,8 +469,8 @@
         first,
         [exps[name] for name in names],
         [blocks[name] for name in names],
+        far_trio,
         near_trio,
-        far_trio,
     )
 
 

time: 71.6 us -> 71.2 us (level)
  transfers between devices with their start and end apart: 17 -> 17, of which waited for: 3 -> 4; matrix products, arithmetic and copies ran while one was open for 0% -> 0% of each run, Pallas kernels for 16% -> 16%
where the time goes in v6:
time: 71.2 us; the launch traced here: 71.1 us
  starting transfers between devices  31.8 us (45%)
  waiting for transfers between devices  22.1 us (31%)
  Pallas kernels  16.9 us (24%)
    ppermute x17, starting transfers between devices, send(): return lax.ppermute(block, both, route[name])  31.8 us
    ppermute x17, waiting for transfers between devices, send(): return lax.ppermute(block, both, route[name])  22.1 us
    pallas_call x7, Pallas kernels, pair_tile(): call(tile_kernel, 'pair_tile', [held] * 3, [held] * 2, [pltpu.VMEM((rows,...  5.89 us
    pallas_call x1, Pallas kernels, gather_final(): call(functools.partial(final_kernel, count), 'gather_final', [held] * (2...  3.42 us
    pallas_call x1, Pallas kernels, gather_first(): call(functools.partial(first_kernel, count), 'gather_first', [held] * (2...  3.38 us
    pallas_call x1, Pallas kernels, self_tile(): call(self_kernel, 'self_tile', [held, small], [held] * 3, [pltpu.VMEM((ro...  1.54 us
  transfers between devices with their start and end apart: 17, of which 4 were waited for; matrix products, arithmetic and copies ran while one was open for 0% of the time, Pallas kernels for 16%

profile of v6, /device:TPU:1, one launch (start us, length us, event | category | flops | bytes accessed | tf_op | source)
XLA Modules:
  0.0 71.1 jit_solution(7165009115955259751)
XLA Ops:
  0.0 0.0 copy-start
  0.0 1.4 %normalize.1.mine_ref.refs_5_ = bf16[768,512]{1,0:T(8,128)(2,1)S(1)} custom-call(bf16[768,512]{1,0:T(8,128)(2,1)} %rows_ref.1), custom_call_target="tpu_custom_call" | custom-call | flops 1572864 | bytes 1572864 | tf_op jit(solution)/shard_map/normalize/pallas_call | solution.py:130
  1.4 3.3 %collective-permute-start.1 = (bf16[768,512]{1,0:T(8,128)(2,1)S(1)}, bf16[768,512]{1,0:T(8,128)(2,1)S(1)}, u32[]{:S(2)}, u32[]{:S(2)}) collective-permute-start(bf16[768,512]{1,0:T(8,128)(2,1)S(1)} %normalize.1.mine_ref.refs_5_), channel_id=1, source_target_pairs={{16,0},{17,1},{18,2},{19,3},{20,4},{21,5},{22,6},{23,7},{24,8},{25... | collective-permute-start | bytes 2359304 | tf_op jit(solution)/shard_map/ppermute | solution.py:416
  4.7 0.0 collective-permute-start
  4.7 3.8 %collective-permute-start.2 = (bf16[768,512]{1,0:T(8,128)(2,1)S(1)}, bf16[768,512]{1,0:T(8,128)(2,1)S(1)}, u32[]{:S(2)}, u32[]{:S(2)}) collective-permute-start(bf16[768,512]{1,0:T(8,128)(2,1)S(1)} %normalize.1.mine_ref.refs_5_), channel_id=1, source_target_pairs={{1,0},{2,1},{3,2},{4,3},{5,4},{6,5},{7,6},{0,7},{9,8},{10,9},{11,1... | collective-permute-start | bytes 2359304 | tf_op jit(solution)/shard_map/ppermute | solution.py:416
  8.6 3.3 %collective-permute-start.6 = (bf16[768,512]{1,0:T(8,128)(2,1)S(1)}, bf16[768,512]{1,0:T(8,128)(2,1)S(1)}, u32[]{:S(2)}, u32[]{:S(2)}) collective-permute-start(bf16[768,512]{1,0:T(8,128)(2,1)S(1)} %normalize.1.mine_ref.refs_5_), channel_id=1, source_target_pairs={{240,0},{241,1},{242,2},{243,3},{244,4},{245,5},{246,6},{247,7},{2... | collective-permute-start | bytes 2359304 | tf_op jit(solution)/shard_map/ppermute | solution.py:416
  11.8 0.0 copy-done
  11.8 1.5 %self_tile.1 = (bf16[768,768]{1,0:T(8,128)(2,1)S(1)}, f32[768,128]{1,0:T(8,128)S(1)}, bf16[768,512]{1,0:T(8,128)(2,1)S(1)}) custom-call(bf16[768,512]{1,0:T(8,128)(2,1)S(1)} %normalize.1.mine_ref.refs_5_, s32[6,128]{1,0:T(8,128)S(1)} %bitcast.1), custom_call_target="tpu_custom_call" | custom-call | flops 1207959552 | bytes 2752512 | tf_op jit(solution)/shard_map/self_tile/pallas_call | solution.py:176
  13.4 0.0 collective-permute-done.1.near_ref.theirs_ref.refs_4_
  13.4 2.5 %collective-permute-start.5 = (bf16[768,512]{1,0:T(8,128)(2,1)S(1)}, bf16[768,512]{1,0:T(8,128)(2,1)S(1)}, u32[]{:S(2)}, u32[]{:S(2)}) collective-permute-start(bf16[768,512]{1,0:T(8,128)(2,1)S(1)} %normalize.1.mine_ref.refs_5_), channel_id=1, source_target_pairs={{192,0},{193,1},{194,2},{195,3},{196,4},{197,5},{198,6},{199,7},{2... | collective-permute-start | bytes 2359304 | tf_op jit(solution)/shard_map/ppermute | solution.py:416
  15.9 0.0 collective-permute-start.4
  15.9 10.5 %collective-permute-done.below_ref.ring_ref = bf16[768,512]{1,0:T(8,128)(2,1)S(1)} collective-permute-done((bf16[768,512]{1,0:T(8,128)(2,1)S(1)}, bf16[768,512]{1,0:T(8,128)(2,1)S(1)}, u32[]{:S(2)}, u32[]{:S(2)}) %collective-permute-start) | collective-permute-done | bytes 786464 | tf_op jit(solution)/shard_map/ppermute | solution.py:416
  26.4 0.0 collective-permute-done.2.above_ref.ring_ref
  26.4 0.1 turn.1
  26.5 1.4 %collective-permute-start.3 = (bf16[768,512]{1,0:T(8,128)(2,1)S(1)}, bf16[768,512]{1,0:T(8,128)(2,1)S(1)}, u32[]{:S(2)}, u32[]{:S(2)}) collective-permute-start(bf16[768,512]{1,0:T(8,128)(2,1)S(1)} %turn.1), channel_id=1, source_target_pairs={{248,255},{17,1},{18,2},{19,3},{20,4},{21,5},{22,6},{15,7},{0,8},{... | collective-permute-start | bytes 2359304 | tf_op jit(solution)/shard_map/ppermute | solution.py:416
  27.8 2.1 %collective-permute-done.6.far_ref.theirs_ref.refs_5_ = bf16[768,512]{1,0:T(8,128)(2,1)S(1)} collective-permute-done((bf16[768,512]{1,0:T(8,128)(2,1)S(1)}, bf16[768,512]{1,0:T(8,128)(2,1)S(1)}, u32[]{:S(2)}, u32[]{:S(2)}) %collective-permute-start.6) | collective-permute-done | bytes 786464 | tf_op jit(solution)/shard_map/ppermute | solution.py:416
  29.9 0.1 far17.1
  30.0 0.7 collective-permute-start.7
  30.7 1.0 %collective-permute-start.9 = (bf16[768,512]{1,0:T(8,128)(2,1)S(1)}, bf16[768,512]{1,0:T(8,128)(2,1)S(1)}, u32[]{:S(2)}, u32[]{:S(2)}) collective-permute-start(bf16[768,512]{1,0:T(8,128)(2,1)S(1)} %far17.1), channel_id=1, source_target_pairs={{47,63},{0,1},{1,2},{2,3},{3,4},{4,5},{5,6},{6,7},{231,8},{8,9},{9... | collective-permute-start | bytes 2359304 | tf_op jit(solution)/shard_map/ppermute | solution.py:416
  31.7 0.8 %pair_tile.7 = (bf16[768,768]{1,0:T(8,128)(2,1)S(1)}, f32[768,128]{1,0:T(8,128)S(1)}) custom-call(bf16[768,512]{1,0:T(8,128)(2,1)S(1)} %normalize.1.mine_ref.refs_5_, bf16[768,512]{1,0:T(8,128)(2,1)S(1)} %collective-permute-done.1.near_ref.theirs_ref.refs_4_, f32[768,128]{1,0:T(8,128)S(1)} %get-tuple-element.39.before_ref), custom_call_target="tpu_custom_call" | custom-call | flops 603979776 | bytes 2752512 | tf_op jit(solution)/shard_map/pair_tile/pallas_call | solution.py:201
  32.5 0.8 %pair_tile.8 = (bf16[768,768]{1,0:T(8,128)(2,1)S(1)}, f32[768,128]{1,0:T(8,128)S(1)}) custom-call(bf16[768,512]{1,0:T(8,128)(2,1)S(1)} %normalize.1.mine_ref.refs_5_, bf16[768,512]{1,0:T(8,128)(2,1)S(1)} %collective-permute-done.6.far_ref.theirs_ref.refs_5_, f32[768,128]{1,0:T(8,128)S(1)} %get-tuple-element.40.before_ref), custom_call_target="tpu_custom_call" | custom-call | flops 603979776 | bytes 2752512 | tf_op jit(solution)/shard_map/pair_tile/pallas_call | solution.py:201
  33.4 0.0 collective-permute-done.5.theirs_ref.refs_8_
  33.4 2.9 %collective-permute-start.10 = (bf16[768,512]{1,0:T(8,128)(2,1)S(1)}, bf16[768,512]{1,0:T(8,128)(2,1)S(1)}, u32[]{:S(2)}, u32[]{:S(2)}) collective-permute-start(bf16[768,512]{1,0:T(8,128)(2,1)S(1)} %collective-permute-done.5.theirs_ref.refs_8_), channel_id=1, source_target_pairs={{0,16},{1,17},{2,18},{3,19},{4,20},{5,21},{6,22},{7,23},{8,24},{9,... | collective-permute-start | bytes 2359304 | tf_op jit(solution)/shard_map/ppermute | solution.py:416
  36.3 0.8 %pair_tile.9 = (bf16[768,768]{1,0:T(8,128)(2,1)S(1)}, f32[768,128]{1,0:T(8,128)S(1)}) custom-call(bf16[768,512]{1,0:T(8,128)(2,1)S(1)} %normalize.1.mine_ref.refs_5_, bf16[768,512]{1,0:T(8,128)(2,1)S(1)} %collective-permute-done.5.theirs_ref.refs_8_, f32[768,128]{1,0:T(8,128)S(1)} %get-tuple-element.41.before_ref), custom_call_target="tpu_custom_call" | custom-call | flops 603979776 | bytes 2752512 | tf_op jit(solution)/shard_map/pair_tile/pallas_call | solution.py:201
  37.1 0.0 collective-permute-done.4.theirs_ref.refs_9_
  37.2 0.8 %pair_tile.10 = (bf16[768,768]{1,0:T(8,128)(2,1)S(1)}, f32[768,128]{1,0:T(8,128)S(1)}) custom-call(bf16[768,512]{1,0:T(8,128)(2,1)S(1)} %normalize.1.mine_ref.refs_5_, bf16[768,512]{1,0:T(8,128)(2,1)S(1)} %collective-permute-done.4.theirs_ref.refs_9_, f32[768,128]{1,0:T(8,128)S(1)} %get-tuple-element.42.before_ref), custom_call_target="tpu_custom_call" | custom-call | flops 603979776 | bytes 2752512 | tf_op jit(solution)/shard_map/pair_tile/pallas_call | solution.py:201
  38.0 9.2 %collective-permute-done.3.turn_ref = bf16[768,512]{1,0:T(8,128)(2,1)S(1)} collective-permute-done((bf16[768,512]{1,0:T(8,128)(2,1)S(1)}, bf16[768,512]{1,0:T(8,128)(2,1)S(1)}, u32[]{:S(2)}, u32[]{:S(2)}) %collective-permute-start.3) | collective-permute-done | bytes 786464 | tf_op jit(solution)/shard_map/ppermute | solution.py:416
  47.2 0.0 collective-permute-done.7.row_ref
  47.2 0.1 above.1.above_ref.theirs_ref.refs_6_
  47.2 0.1 below.1.below_ref.theirs_ref.refs_7_
  47.3 0.1 near17.1
  47.4 0.3 collective-permute-start.8
  47.7 0.9 %pair_tile.11 = (bf16[768,768]{1,0:T(8,128)(2,1)S(1)}, f32[768,128]{1,0:T(8,128)S(1)}) custom-call(bf16[768,512]{1,0:T(8,128)(2,1)S(1)} %normalize.1.mine_ref.refs_5_, bf16[768,512]{1,0:T(8,128)(2,1)S(1)} %above.1.above_ref.theirs_ref.refs_6_, f32[768,128]{1,0:T(8,128)S(1)} %get-tuple-element.45.before_ref), custom_call_target="tpu_custom_call" | custom-call | flops 603979776 | bytes 2752512 | tf_op jit(solution)/shard_map/pair_tile/pallas_call | solution.py:201
  48.6 0.8 %pair_tile.12 = (bf16[768,768]{1,0:T(8,128)(2,1)S(1)}, f32[768,128]{1,0:T(8,128)S(1)}) custom-call(bf16[768,512]{1,0:T(8,128)(2,1)S(1)} %normalize.1.mine_ref.refs_5_, bf16[768,512]{1,0:T(8,128)(2,1)S(1)} %below.1.below_ref.theirs_ref.refs_7_, f32[768,128]{1,0:T(8,128)S(1)} %get-tuple-element.46.before_ref), custom_call_target="tpu_custom_call" | custom-call | flops 603979776 | bytes 2752512 | tf_op jit(solution)/shard_map/pair_tile/pallas_call | solution.py:201
  49.4 0.0 collective-permute-done.9.far17_ref
  49.4 0.0 collective-permute-done.10.corner_ref
  49.5 0.8 %pair_tile.13 = (bf16[768,768]{1,0:T(8,128)(2,1)S(1)}, f32[768,128]{1,0:T(8,128)S(1)}) custom-call(bf16[768,512]{1,0:T(8,128)(2,1)S(1)} %normalize.1.mine_ref.refs_5_, bf16[768,512]{1,0:T(8,128)(2,1)S(1)} %corner.1.theirs_ref.refs_7_, f32[768,128]{1,0:T(8,128)S(1)} %get-tuple-element.47.before_ref), custom_call_target="tpu_custom_call" | custom-call | flops 603979776 | bytes 2752512 | tf_op jit(solution)/shard_map/pair_tile/pallas_call | solution.py:201
  50.3 0.0 collective-permute-done.8.theirs_ref.refs_6_
  50.3 0.9 %last_tile.1 = (bf16[768,768]{1,0:T(8,128)(2,1)S(1)}, f32[768,128]{1,0:T(8,128)S(1)}, f32[1,768]{1,0:T(1,128)S(1)}) custom-call(bf16[768,512]{1,0:T(8,128)(2,1)S(1)} %normalize.1.mine_ref.refs_5_, bf16[768,512]{1,0:T(8,128)(2,1)S(1)} %collective-permute-done.8.theirs_ref.refs_6_, f32[768,128]{1,0:T(8,128)S(1)} %get-tuple-element.48.before_ref), custom_call_target="tpu_custom_call" | custom-call | flops 603979776 | bytes 2752512 | tf_op jit(solution)/shard_map/last_tile/pallas_call | solution.py:224
  51.3 0.1 collective-permute-start.12
  51.4 4.5 %collective-permute-start.11 = (f32[1,768]{1,0:T(1,128)S(1)}, f32[1,768]{1,0:T(1,128)S(1)}, u32[]{:S(2)}, u32[]{:S(2)}) collective-permute-start(f32[1,768]{1,0:T(1,128)S(1)} %get-tuple-element.56.mine_ref), channel_id=1, source_target_pairs={{255,0},{2,1},{1,2},{4,3},{3,4},{6,5},{5,6},{8,7},{7,8},{10,9},{9,... | collective-permute-start | bytes 9224 | tf_op jit(solution)/shard_map/ppermute | solution.py:416
  55.9 3.0 %collective-permute-start.14 = (f32[1,768]{1,0:T(1,128)S(1)}, f32[1,768]{1,0:T(1,128)S(1)}, u32[]{:S(2)}, u32[]{:S(2)}) collective-permute-start(f32[1,768]{1,0:T(1,128)S(1)} %get-tuple-element.56.mine_ref), channel_id=1, source_target_pairs={{192,0},{193,1},{194,2},{195,3},{196,4},{197,5},{198,6},{199,7},{2... | collective-permute-start | bytes 9224 | tf_op jit(solution)/shard_map/ppermute | solution.py:416
  58.9 0.0 collective-permute-start.13
  58.9 0.0 collective-permute-done.12.even_ref
  58.9 0.0 collective-permute-done.11.odd_ref
  58.9 4.0 %collective-permute-start.16 = (f32[3,768]{1,0:T(4,128)S(1)}, f32[3,768]{1,0:T(4,128)S(1)}, u32[]{:S(2)}, u32[]{:S(2)}) collective-permute-start(f32[3,768]{1,0:T(4,128)S(1)} %trio.1.refs_10_), channel_id=1, source_target_pairs={{16,0},{17,1},{18,2},{19,3},{20,4},{21,5},{22,6},{23,7},{24,8},{25... | collective-permute-start | bytes 27656 | tf_op jit(solution)/shard_map/ppermute | solution.py:416
  62.9 0.9 %collective-permute-start.15 = (f32[3,768]{1,0:T(4,128)S(1)}, f32[3,768]{1,0:T(4,128)S(1)}, u32[]{:S(2)}, u32[]{:S(2)}) collective-permute-start(f32[3,768]{1,0:T(4,128)S(1)} %trio.1.refs_10_), channel_id=1, source_target_pairs={{240,0},{241,1},{242,2},{243,3},{244,4},{245,5},{246,6},{247,7},{2... | collective-permute-start | bytes 27656 | tf_op jit(solution)/shard_map/ppermute | solution.py:416
  63.8 0.0 collective-permute-done.14.refs_12_
  63.8 0.0 collective-permute-done.13.refs_11_
  63.8 3.4 %gather_first.1.first_ref = f32[768,512]{1,0:T(8,128)S(1)} custom-call(f32[768,128]{1,0:T(8,128)S(1)} %get-tuple-element.49.sums_ref, bf16[768,512]{1,0:T(8,128)(2,1)S(1)} %get-tuple-element.50.matched_ref, bf16[768,768]{1,0:T(8,128)(2,1)S(1)} %get-tuple-element.51.refs_0_, bf16[768,768]{1,0:T(8,128)(2,1)S(1)} %get-tuple-element.52.refs_1_, ...), custom_call_target="tpu_custom_call" | custom-call | flops 3019898880 | bytes 12976128 | tf_op jit(solution)/shard_map/gather_first/pallas_call | solution.py:363
  67.2 0.0 collective-permute-done.16.refs_9_
  67.2 0.3 collective-permute-done.15.refs_8_
  67.5 3.4 %gather_final.1 = f32[768,512]{1,0:T(8,128)} custom-call(f32[768,128]{1,0:T(8,128)S(1)} %get-tuple-element.49.sums_ref, f32[768,512]{1,0:T(8,128)S(1)} %gather_first.1.first_ref, bf16[768,768]{1,0:T(8,128)(2,1)S(1)} %get-tuple-element.57.refs_0_, bf16[768,768]{1,0:T(8,128)(2,1)S(1)} %get-tuple-element.58.refs_1_, ...), custom_call_target="tpu_custom_call" | custom-call | flops 2415919104 | bytes 11010048 | tf_op jit(solution)/shard_map/gather_final/pallas_call | solution.py:376
  (2 shorter events, 0.0 us)
Async XLA Ops:
  0.0 11.8 %copy-start = (s32[768]{0:T(1024)S(1)}, s32[768]{0:T(1024)}, u32[]{:S(2)}) copy-start(s32[768]{0:T(1024)} %param.3) | copy-start | bytes 9220
  1.4 12.0 %collective-permute-start.1 = (bf16[768,512]{1,0:T(8,128)(2,1)S(1)}, bf16[768,512]{1,0:T(8,128)(2,1)S(1)}, u32[]{:S(2)}, u32[]{:S(2)}) collective-permute-start(bf16[768,512]{1,0:T(8,128)(2,1)S(1)} %normalize.1.mine_ref.refs_5_), channel_id=1, source_target_pairs={{16,0},{17,1},{18,2},{19,3},{20,4},{21,5},{22,6},{23,7},{24,8},{25... | collective-permute-start | bytes 2359304 | tf_op jit(solution)/shard_map/ppermute | solution.py:416
  4.7 21.7 %collective-permute-start = (bf16[768,512]{1,0:T(8,128)(2,1)S(1)}, bf16[768,512]{1,0:T(8,128)(2,1)S(1)}, u32[]{:S(2)}, u32[]{:S(2)}) collective-permute-start(bf16[768,512]{1,0:T(8,128)(2,1)S(1)} %normalize.1.mine_ref.refs_5_), channel_id=1, source_target_pairs={{7,0},{0,1},{1,2},{2,3},{3,4},{4,5},{5,6},{6,7},{15,8},{8,9},{9,10... | collective-permute-start | bytes 2359304 | tf_op jit(solution)/shard_map/ppermute | solution.py:416
  4.7 21.7 %collective-permute-start.2 = (bf16[768,512]{1,0:T(8,128)(2,1)S(1)}, bf16[768,512]{1,0:T(8,128)(2,1)S(1)}, u32[]{:S(2)}, u32[]{:S(2)}) collective-permute-start(bf16[768,512]{1,0:T(8,128)(2,1)S(1)} %normalize.1.mine_ref.refs_5_), channel_id=1, source_target_pairs={{1,0},{2,1},{3,2},{4,3},{5,4},{6,5},{7,6},{0,7},{9,8},{10,9},{11,1... | collective-permute-start | bytes 2359304 | tf_op jit(solution)/shard_map/ppermute | solution.py:416
  8.6 21.4 %collective-permute-start.6 = (bf16[768,512]{1,0:T(8,128)(2,1)S(1)}, bf16[768,512]{1,0:T(8,128)(2,1)S(1)}, u32[]{:S(2)}, u32[]{:S(2)}) collective-permute-start(bf16[768,512]{1,0:T(8,128)(2,1)S(1)} %normalize.1.mine_ref.refs_5_), channel_id=1, source_target_pairs={{240,0},{241,1},{242,2},{243,3},{244,4},{245,5},{246,6},{247,7},{2... | collective-permute-start | bytes 2359304 | tf_op jit(solution)/shard_map/ppermute | solution.py:416
  13.4 20.0 %collective-permute-start.5 = (bf16[768,512]{1,0:T(8,128)(2,1)S(1)}, bf16[768,512]{1,0:T(8,128)(2,1)S(1)}, u32[]{:S(2)}, u32[]{:S(2)}) collective-permute-start(bf16[768,512]{1,0:T(8,128)(2,1)S(1)} %normalize.1.mine_ref.refs_5_), channel_id=1, source_target_pairs={{192,0},{193,1},{194,2},{195,3},{196,4},{197,5},{198,6},{199,7},{2... | collective-permute-start | bytes 2359304 | tf_op jit(solution)/shard_map/ppermute | solution.py:416
  15.9 21.2 %collective-permute-start.4 = (bf16[768,512]{1,0:T(8,128)(2,1)S(1)}, bf16[768,512]{1,0:T(8,128)(2,1)S(1)}, u32[]{:S(2)}, u32[]{:S(2)}) collective-permute-start(bf16[768,512]{1,0:T(8,128)(2,1)S(1)} %normalize.1.mine_ref.refs_5_), channel_id=1, source_target_pairs={{64,0},{65,1},{66,2},{67,3},{68,4},{69,5},{70,6},{71,7},{72,8},{73... | collective-permute-start | bytes 2359304 | tf_op jit(solution)/shard_map/ppermute | solution.py:416
  26.5 20.7 %collective-permute-start.3 = (bf16[768,512]{1,0:T(8,128)(2,1)S(1)}, bf16[768,512]{1,0:T(8,128)(2,1)S(1)}, u32[]{:S(2)}, u32[]{:S(2)}) collective-permute-start(bf16[768,512]{1,0:T(8,128)(2,1)S(1)} %turn.1), channel_id=1, source_target_pairs={{248,255},{17,1},{18,2},{19,3},{20,4},{21,5},{22,6},{15,7},{0,8},{... | collective-permute-start | bytes 2359304 | tf_op jit(solution)/shard_map/ppermute | solution.py:416
  30.0 17.2 %collective-permute-start.7 = (bf16[768,512]{1,0:T(8,128)(2,1)S(1)}, bf16[768,512]{1,0:T(8,128)(2,1)S(1)}, u32[]{:S(2)}, u32[]{:S(2)}) collective-permute-start(bf16[768,512]{1,0:T(8,128)(2,1)S(1)} %collective-permute-done.6.far_ref.theirs_ref.refs_5_), channel_id=1, source_target_pairs={{15,0},{48,63},{79,64},{112,127},{143,128},{176,191},{207,192},{24... | collective-permute-start | bytes 2359304 | tf_op jit(solution)/shard_map/ppermute | solution.py:416
  30.7 18.7 %collective-permute-start.9 = (bf16[768,512]{1,0:T(8,128)(2,1)S(1)}, bf16[768,512]{1,0:T(8,128)(2,1)S(1)}, u32[]{:S(2)}, u32[]{:S(2)}) collective-permute-start(bf16[768,512]{1,0:T(8,128)(2,1)S(1)} %far17.1), channel_id=1, source_target_pairs={{47,63},{0,1},{1,2},{2,3},{3,4},{4,5},{5,6},{6,7},{231,8},{8,9},{9... | collective-permute-start | bytes 2359304 | tf_op jit(solution)/shard_map/ppermute | solution.py:416
  33.4 16.0 %collective-permute-start.10 = (bf16[768,512]{1,0:T(8,128)(2,1)S(1)}, bf16[768,512]{1,0:T(8,128)(2,1)S(1)}, u32[]{:S(2)}, u32[]{:S(2)}) collective-permute-start(bf16[768,512]{1,0:T(8,128)(2,1)S(1)} %collective-permute-done.5.theirs_ref.refs_8_), channel_id=1, source_target_pairs={{0,16},{1,17},{2,18},{3,19},{4,20},{5,21},{6,22},{7,23},{8,24},{9,... | collective-permute-start | bytes 2359304 | tf_op jit(solution)/shard_map/ppermute | solution.py:416
  47.4 2.9 %collective-permute-start.8 = (bf16[768,512]{1,0:T(8,128)(2,1)S(1)}, bf16[768,512]{1,0:T(8,128)(2,1)S(1)}, u32[]{:S(2)}, u32[]{:S(2)}) collective-permute-start(bf16[768,512]{1,0:T(8,128)(2,1)S(1)} %near17.1), channel_id=1, source_target_pairs={{16,0},{17,1},{18,2},{19,3},{20,4},{21,5},{22,6},{23,7},{24,8},{25... | collective-permute-start | bytes 2359304 | tf_op jit(solution)/shard_map/ppermute | solution.py:416
  51.3 7.6 %collective-permute-start.12 = (f32[1,768]{1,0:T(1,128)S(1)}, f32[1,768]{1,0:T(1,128)S(1)}, u32[]{:S(2)}, u32[]{:S(2)}) collective-permute-start(f32[1,768]{1,0:T(1,128)S(1)} %get-tuple-element.56.mine_ref), channel_id=1, source_target_pairs={{1,0},{0,1},{3,2},{2,3},{5,4},{4,5},{7,6},{6,7},{9,8},{8,9},{11,10... | collective-permute-start | bytes 9224 | tf_op jit(solution)/shard_map/ppermute | solution.py:416
  51.4 7.5 %collective-permute-start.11 = (f32[1,768]{1,0:T(1,128)S(1)}, f32[1,768]{1,0:T(1,128)S(1)}, u32[]{:S(2)}, u32[]{:S(2)}) collective-permute-start(f32[1,768]{1,0:T(1,128)S(1)} %get-tuple-element.56.mine_ref), channel_id=1, source_target_pairs={{255,0},{2,1},{1,2},{4,3},{3,4},{6,5},{5,6},{8,7},{7,8},{10,9},{9,... | collective-permute-start | bytes 9224 | tf_op jit(solution)/shard_map/ppermute | solution.py:416
  55.9 7.9 %collective-permute-start.14 = (f32[1,768]{1,0:T(1,128)S(1)}, f32[1,768]{1,0:T(1,128)S(1)}, u32[]{:S(2)}, u32[]{:S(2)}) collective-permute-start(f32[1,768]{1,0:T(1,128)S(1)} %get-tuple-element.56.mine_ref), channel_id=1, source_target_pairs={{192,0},{193,1},{194,2},{195,3},{196,4},{197,5},{198,6},{199,7},{2... | collective-permute-start | bytes 9224 | tf_op jit(solution)/shard_map/ppermute | solution.py:416
  58.9 5.0 %collective-permute-start.13 = (f32[1,768]{1,0:T(1,128)S(1)}, f32[1,768]{1,0:T(1,128)S(1)}, u32[]{:S(2)}, u32[]{:S(2)}) collective-permute-start(f32[1,768]{1,0:T(1,128)S(1)} %get-tuple-element.56.mine_ref), channel_id=1, source_target_pairs={{64,0},{65,1},{66,2},{67,3},{68,4},{69,5},{70,6},{71,7},{72,8},{73... | collective-permute-start | bytes 9224 | tf_op jit(solution)/shard_map/ppermute | solution.py:416
  58.9 8.3 %collective-permute-start.16 = (f32[3,768]{1,0:T(4,128)S(1)}, f32[3,768]{1,0:T(4,128)S(1)}, u32[]{:S(2)}, u32[]{:S(2)}) collective-permute-start(f32[3,768]{1,0:T(4,128)S(1)} %trio.1.refs_10_), channel_id=1, source_target_pairs={{16,0},{17,1},{18,2},{19,3},{20,4},{21,5},{22,6},{23,7},{24,8},{25... | collective-permute-start | bytes 27656 | tf_op jit(solution)/shard_map/ppermute | solution.py:416
  62.9 4.6 %collective-permute-start.15 = (f32[3,768]{1,0:T(4,128)S(1)}, f32[3,768]{1,0:T(4,128)S(1)}, u32[]{:S(2)}, u32[]{:S(2)}) collective-permute-start(f32[3,768]{1,0:T(4,128)S(1)} %trio.1.refs_10_), channel_id=1, source_target_pairs={{240,0},{241,1},{242,2},{243,3},{244,4},{245,5},{246,6},{247,7},{2... | collective-permute-start | bytes 27656 | tf_op jit(solution)/shard_map/ppermute | solution.py:416

commit v7 on v6

--- a/solution.py
+++ b/solution.py
@@ -111,14 +111,18 @@
     return [slice(start, start + chunk) for start in range(0, rows, chunk)]
 
 
+def halves(rows):
+    return [slice(0, rows // 2), slice(rows // 2, rows)]
+
+
 def normalize_kernel(rows_ref, out_ref, held_ref, sems):
     rows = rows_ref.shape[0]
     copies = []
-    for number, part in enumerate(parts(rows)):
+    for number, part in enumerate(halves(rows)):
         copy = pltpu.make_async_copy(rows_ref.at[part], held_ref.at[part], sems.at[number])
         copy.start()
         copies.append(copy)
-    for copy, part in zip(copies, parts(rows)):
+    for copy, part in zip(copies, halves(rows)):
         copy.wait()
         wide = held_ref[part, :].astype(jnp.float32)
         scale = lax.rsqrt(jnp.sum(wide * wide, axis=-1, keepdims=True) + epsilon)
@@ -137,7 +141,7 @@
         4 * rows * width,
         scratch=[
             pltpu.VMEM((rows, width), jnp.bfloat16),
-            pltpu.SemaphoreType.DMA((rows // chunk,)),
+            pltpu.SemaphoreType.DMA((2,)),
         ],
     )(pltpu.with_memory_space_constraint(embeddings, pltpu.HBM))
 
@@ -388,14 +392,14 @@
     )(*hold(sums, first, *exps, *blocks, far_trio, near_trio))
 
 
-def trio_kernel(mine_ref, odd_ref, even_ref, out_ref):
+def trio_kernel(mine_ref, even_ref, odd_ref, out_ref):
     even = lax.axis_index("col") % 2 == 0
     out_ref[0:1, :] = mine_ref[...]
     out_ref[1:2, :] = jnp.where(even, even_ref[...], odd_ref[...])
     out_ref[2:3, :] = jnp.where(even, odd_ref[...], even_ref[...])
 
 
-def trio_of(mine, odd, even):
+def trio_of(mine, even, odd):
     width = mine.shape[1]
     return call(
         trio_kernel,
@@ -405,7 +409,7 @@
         pltpu.VMEM((3, width), jnp.float32),
         0,
         24 * width,
-    )(*hold(mine, odd, even))
+    )(*hold(mine, even, odd))
 
 
 def on_device(embeddings, positives):
@@ -449,7 +453,7 @@
     blocks["near17"] = near17
     exps["near17"], sums, denoms = last_tile(normed, near17, sums)
 
-    trio = trio_of(denoms, send(denoms, "odd"), send(denoms, "even"))
+    trio = trio_of(denoms, send(denoms, "even"), send(denoms, "odd"))
     d_x_even = send(denoms, "x_even")
     d_x_odd = send(denoms, "x_odd")
     far_trio = send(trio, "far")

time: 71.2 us -> 71.2 us (level)
  no operation moved by 1% of the time
where the time goes in v7:
time: 71.2 us; the launch traced here: 71.1 us
  starting transfers between devices  31.7 us (45%)
  waiting for transfers between devices  22.2 us (31%)
  Pallas kernels  16.8 us (24%)
    ppermute x17, starting transfers between devices, send(): return lax.ppermute(block, both, route[name])  31.7 us
    ppermute x17, waiting for transfers between devices, send(): return lax.ppermute(block, both, route[name])  22.2 us
    pallas_call x7, Pallas kernels, pair_tile(): call(tile_kernel, 'pair_tile', [held] * 3, [held] * 2, [pltpu.VMEM((rows,...  5.87 us
    pallas_call x1, Pallas kernels, gather_final(): call(functools.partial(final_kernel, count), 'gather_final', [held] * (2...  3.42 us
    pallas_call x1, Pallas kernels, gather_first(): call(functools.partial(first_kernel, count), 'gather_first', [held] * (2...  3.38 us
    pallas_call x1, Pallas kernels, self_tile(): call(self_kernel, 'self_tile', [held, small], [held] * 3, [pltpu.VMEM((ro...  1.53 us
  transfers between devices with their start and end apart: 17, of which 4 were waited for; matrix products, arithmetic and copies ran while one was open for 0% of the time, Pallas kernels for 16%

profile of v7, /device:TPU:1, one launch (start us, length us, event | category | flops | bytes accessed | tf_op | source)
XLA Modules:
  0.0 71.1 jit_solution(4481261039948836079)
XLA Ops:
  0.0 0.0 copy-start
  0.0 1.3 %normalize.1.mine_ref.refs_5_ = bf16[768,512]{1,0:T(8,128)(2,1)S(1)} custom-call(bf16[768,512]{1,0:T(8,128)(2,1)} %rows_ref.1), custom_call_target="tpu_custom_call" | custom-call | flops 1572864 | bytes 1572864 | tf_op jit(solution)/shard_map/normalize/pallas_call | solution.py:134
  1.4 3.3 %collective-permute-start.1 = (bf16[768,512]{1,0:T(8,128)(2,1)S(1)}, bf16[768,512]{1,0:T(8,128)(2,1)S(1)}, u32[]{:S(2)}, u32[]{:S(2)}) collective-permute-start(bf16[768,512]{1,0:T(8,128)(2,1)S(1)} %normalize.1.mine_ref.refs_5_), channel_id=1, source_target_pairs={{16,0},{17,1},{18,2},{19,3},{20,4},{21,5},{22,6},{23,7},{24,8},{25... | collective-permute-start | bytes 2359304 | tf_op jit(solution)/shard_map/ppermute | solution.py:420
  4.7 0.0 collective-permute-start
  4.7 3.8 %collective-permute-start.2 = (bf16[768,512]{1,0:T(8,128)(2,1)S(1)}, bf16[768,512]{1,0:T(8,128)(2,1)S(1)}, u32[]{:S(2)}, u32[]{:S(2)}) collective-permute-start(bf16[768,512]{1,0:T(8,128)(2,1)S(1)} %normalize.1.mine_ref.refs_5_), channel_id=1, source_target_pairs={{1,0},{2,1},{3,2},{4,3},{5,4},{6,5},{7,6},{0,7},{9,8},{10,9},{11,1... | collective-permute-start | bytes 2359304 | tf_op jit(solution)/shard_map/ppermute | solution.py:420
  8.5 3.3 %collective-permute-start.6 = (bf16[768,512]{1,0:T(8,128)(2,1)S(1)}, bf16[768,512]{1,0:T(8,128)(2,1)S(1)}, u32[]{:S(2)}, u32[]{:S(2)}) collective-permute-start(bf16[768,512]{1,0:T(8,128)(2,1)S(1)} %normalize.1.mine_ref.refs_5_), channel_id=1, source_target_pairs={{240,0},{241,1},{242,2},{243,3},{244,4},{245,5},{246,6},{247,7},{2... | collective-permute-start | bytes 2359304 | tf_op jit(solution)/shard_map/ppermute | solution.py:420
  11.8 0.0 copy-done
  11.8 1.5 %self_tile.1 = (bf16[768,768]{1,0:T(8,128)(2,1)S(1)}, f32[768,128]{1,0:T(8,128)S(1)}, bf16[768,512]{1,0:T(8,128)(2,1)S(1)}) custom-call(bf16[768,512]{1,0:T(8,128)(2,1)S(1)} %normalize.1.mine_ref.refs_5_, s32[6,128]{1,0:T(8,128)S(1)} %bitcast.1), custom_call_target="tpu_custom_call" | custom-call | flops 1207959552 | bytes 2752512 | tf_op jit(solution)/shard_map/self_tile/pallas_call | solution.py:180
  13.3 0.0 collective-permute-done.1.near_ref.theirs_ref.refs_4_
  13.3 2.6 %collective-permute-start.5 = (bf16[768,512]{1,0:T(8,128)(2,1)S(1)}, bf16[768,512]{1,0:T(8,128)(2,1)S(1)}, u32[]{:S(2)}, u32[]{:S(2)}) collective-permute-start(bf16[768,512]{1,0:T(8,128)(2,1)S(1)} %normalize.1.mine_ref.refs_5_), channel_id=1, source_target_pairs={{192,0},{193,1},{194,2},{195,3},{196,4},{197,5},{198,6},{199,7},{2... | collective-permute-start | bytes 2359304 | tf_op jit(solution)/shard_map/ppermute | solution.py:420
  15.9 0.0 collective-permute-start.4
  15.9 10.5 %collective-permute-done.below_ref.ring_ref = bf16[768,512]{1,0:T(8,128)(2,1)S(1)} collective-permute-done((bf16[768,512]{1,0:T(8,128)(2,1)S(1)}, bf16[768,512]{1,0:T(8,128)(2,1)S(1)}, u32[]{:S(2)}, u32[]{:S(2)}) %collective-permute-start) | collective-permute-done | bytes 786464 | tf_op jit(solution)/shard_map/ppermute | solution.py:420
  26.3 0.0 collective-permute-done.2.above_ref.ring_ref
  26.3 0.1 turn.1
  26.4 1.4 %collective-permute-start.3 = (bf16[768,512]{1,0:T(8,128)(2,1)S(1)}, bf16[768,512]{1,0:T(8,128)(2,1)S(1)}, u32[]{:S(2)}, u32[]{:S(2)}) collective-permute-start(bf16[768,512]{1,0:T(8,128)(2,1)S(1)} %turn.1), channel_id=1, source_target_pairs={{248,255},{17,1},{18,2},{19,3},{20,4},{21,5},{22,6},{15,7},{0,8},{... | collective-permute-start | bytes 2359304 | tf_op jit(solution)/shard_map/ppermute | solution.py:420
  27.8 2.1 %collective-permute-done.6.far_ref.theirs_ref.refs_5_ = bf16[768,512]{1,0:T(8,128)(2,1)S(1)} collective-permute-done((bf16[768,512]{1,0:T(8,128)(2,1)S(1)}, bf16[768,512]{1,0:T(8,128)(2,1)S(1)}, u32[]{:S(2)}, u32[]{:S(2)}) %collective-permute-start.6) | collective-permute-done | bytes 786464 | tf_op jit(solution)/shard_map/ppermute | solution.py:420
  29.9 0.1 far17.1
  29.9 0.7 %collective-permute-start.7 = (bf16[768,512]{1,0:T(8,128)(2,1)S(1)}, bf16[768,512]{1,0:T(8,128)(2,1)S(1)}, u32[]{:S(2)}, u32[]{:S(2)}) collective-permute-start(bf16[768,512]{1,0:T(8,128)(2,1)S(1)} %collective-permute-done.6.far_ref.theirs_ref.refs_5_), channel_id=1, source_target_pairs={{15,0},{48,63},{79,64},{112,127},{143,128},{176,191},{207,192},{24... | collective-permute-start | bytes 2359304 | tf_op jit(solution)/shard_map/ppermute | solution.py:420
  30.7 1.0 %collective-permute-start.9 = (bf16[768,512]{1,0:T(8,128)(2,1)S(1)}, bf16[768,512]{1,0:T(8,128)(2,1)S(1)}, u32[]{:S(2)}, u32[]{:S(2)}) collective-permute-start(bf16[768,512]{1,0:T(8,128)(2,1)S(1)} %far17.1), channel_id=1, source_target_pairs={{47,63},{0,1},{1,2},{2,3},{3,4},{4,5},{5,6},{6,7},{231,8},{8,9},{9... | collective-permute-start | bytes 2359304 | tf_op jit(solution)/shard_map/ppermute | solution.py:420
  31.7 0.8 %pair_tile.7 = (bf16[768,768]{1,0:T(8,128)(2,1)S(1)}, f32[768,128]{1,0:T(8,128)S(1)}) custom-call(bf16[768,512]{1,0:T(8,128)(2,1)S(1)} %normalize.1.mine_ref.refs_5_, bf16[768,512]{1,0:T(8,128)(2,1)S(1)} %collective-permute-done.1.near_ref.theirs_ref.refs_4_, f32[768,128]{1,0:T(8,128)S(1)} %get-tuple-element.39.before_ref), custom_call_target="tpu_custom_call" | custom-call | flops 603979776 | bytes 2752512 | tf_op jit(solution)/shard_map/pair_tile/pallas_call | solution.py:205
  32.5 0.8 %pair_tile.8 = (bf16[768,768]{1,0:T(8,128)(2,1)S(1)}, f32[768,128]{1,0:T(8,128)S(1)}) custom-call(bf16[768,512]{1,0:T(8,128)(2,1)S(1)} %normalize.1.mine_ref.refs_5_, bf16[768,512]{1,0:T(8,128)(2,1)S(1)} %collective-permute-done.6.far_ref.theirs_ref.refs_5_, f32[768,128]{1,0:T(8,128)S(1)} %get-tuple-element.40.before_ref), custom_call_target="tpu_custom_call" | custom-call | flops 603979776 | bytes 2752512 | tf_op jit(solution)/shard_map/pair_tile/pallas_call | solution.py:205
  33.3 0.0 collective-permute-done.5.theirs_ref.refs_8_
  33.4 2.9 %collective-permute-start.10 = (bf16[768,512]{1,0:T(8,128)(2,1)S(1)}, bf16[768,512]{1,0:T(8,128)(2,1)S(1)}, u32[]{:S(2)}, u32[]{:S(2)}) collective-permute-start(bf16[768,512]{1,0:T(8,128)(2,1)S(1)} %collective-permute-done.5.theirs_ref.refs_8_), channel_id=1, source_target_pairs={{0,16},{1,17},{2,18},{3,19},{4,20},{5,21},{6,22},{7,23},{8,24},{9,... | collective-permute-start | bytes 2359304 | tf_op jit(solution)/shard_map/ppermute | solution.py:420
  36.2 0.8 %pair_tile.9 = (bf16[768,768]{1,0:T(8,128)(2,1)S(1)}, f32[768,128]{1,0:T(8,128)S(1)}) custom-call(bf16[768,512]{1,0:T(8,128)(2,1)S(1)} %normalize.1.mine_ref.refs_5_, bf16[768,512]{1,0:T(8,128)(2,1)S(1)} %collective-permute-done.5.theirs_ref.refs_8_, f32[768,128]{1,0:T(8,128)S(1)} %get-tuple-element.41.before_ref), custom_call_target="tpu_custom_call" | custom-call | flops 603979776 | bytes 2752512 | tf_op jit(solution)/shard_map/pair_tile/pallas_call | solution.py:205
  37.1 0.0 collective-permute-done.4.theirs_ref.refs_9_
  37.1 0.8 %pair_tile.10 = (bf16[768,768]{1,0:T(8,128)(2,1)S(1)}, f32[768,128]{1,0:T(8,128)S(1)}) custom-call(bf16[768,512]{1,0:T(8,128)(2,1)S(1)} %normalize.1.mine_ref.refs_5_, bf16[768,512]{1,0:T(8,128)(2,1)S(1)} %collective-permute-done.4.theirs_ref.refs_9_, f32[768,128]{1,0:T(8,128)S(1)} %get-tuple-element.42.before_ref), custom_call_target="tpu_custom_call" | custom-call | flops 603979776 | bytes 2752512 | tf_op jit(solution)/shard_map/pair_tile/pallas_call | solution.py:205
  37.9 9.2 %collective-permute-done.3.turn_ref = bf16[768,512]{1,0:T(8,128)(2,1)S(1)} collective-permute-done((bf16[768,512]{1,0:T(8,128)(2,1)S(1)}, bf16[768,512]{1,0:T(8,128)(2,1)S(1)}, u32[]{:S(2)}, u32[]{:S(2)}) %collective-permute-start.3) | collective-permute-done | bytes 786464 | tf_op jit(solution)/shard_map/ppermute | solution.py:420
  47.1 0.0 collective-permute-done.7.row_ref
  47.1 0.1 above.1.above_ref.theirs_ref.refs_6_
  47.2 0.1 below.1.below_ref.theirs_ref.refs_7_
  47.3 0.1 near17.1
  47.4 0.3 collective-permute-start.8
  47.6 0.8 %pair_tile.11 = (bf16[768,768]{1,0:T(8,128)(2,1)S(1)}, f32[768,128]{1,0:T(8,128)S(1)}) custom-call(bf16[768,512]{1,0:T(8,128)(2,1)S(1)} %normalize.1.mine_ref.refs_5_, bf16[768,512]{1,0:T(8,128)(2,1)S(1)} %above.1.above_ref.theirs_ref.refs_6_, f32[768,128]{1,0:T(8,128)S(1)} %get-tuple-element.45.before_ref), custom_call_target="tpu_custom_call" | custom-call | flops 603979776 | bytes 2752512 | tf_op jit(solution)/shard_map/pair_tile/pallas_call | solution.py:205
  48.5 0.8 %pair_tile.12 = (bf16[768,768]{1,0:T(8,128)(2,1)S(1)}, f32[768,128]{1,0:T(8,128)S(1)}) custom-call(bf16[768,512]{1,0:T(8,128)(2,1)S(1)} %normalize.1.mine_ref.refs_5_, bf16[768,512]{1,0:T(8,128)(2,1)S(1)} %below.1.below_ref.theirs_ref.refs_7_, f32[768,128]{1,0:T(8,128)S(1)} %get-tuple-element.46.before_ref), custom_call_target="tpu_custom_call" | custom-call | flops 603979776 | bytes 2752512 | tf_op jit(solution)/shard_map/pair_tile/pallas_call | solution.py:205
  49.3 0.0 collective-permute-done.9.far17_ref
  49.4 0.0 collective-permute-done.10.corner_ref
  49.4 0.8 %pair_tile.13 = (bf16[768,768]{1,0:T(8,128)(2,1)S(1)}, f32[768,128]{1,0:T(8,128)S(1)}) custom-call(bf16[768,512]{1,0:T(8,128)(2,1)S(1)} %normalize.1.mine_ref.refs_5_, bf16[768,512]{1,0:T(8,128)(2,1)S(1)} %corner.1.theirs_ref.refs_7_, f32[768,128]{1,0:T(8,128)S(1)} %get-tuple-element.47.before_ref), custom_call_target="tpu_custom_call" | custom-call | flops 603979776 | bytes 2752512 | tf_op jit(solution)/shard_map/pair_tile/pallas_call | solution.py:205
  50.2 0.0 collective-permute-done.8.theirs_ref.refs_6_
  50.3 0.9 %last_tile.1 = (bf16[768,768]{1,0:T(8,128)(2,1)S(1)}, f32[768,128]{1,0:T(8,128)S(1)}, f32[1,768]{1,0:T(1,128)S(1)}) custom-call(bf16[768,512]{1,0:T(8,128)(2,1)S(1)} %normalize.1.mine_ref.refs_5_, bf16[768,512]{1,0:T(8,128)(2,1)S(1)} %collective-permute-done.8.theirs_ref.refs_6_, f32[768,128]{1,0:T(8,128)S(1)} %get-tuple-element.48.before_ref), custom_call_target="tpu_custom_call" | custom-call | flops 603979776 | bytes 2752512 | tf_op jit(solution)/shard_map/last_tile/pallas_call | solution.py:228
  51.2 4.6 %collective-permute-start.12 = (f32[1,768]{1,0:T(1,128)S(1)}, f32[1,768]{1,0:T(1,128)S(1)}, u32[]{:S(2)}, u32[]{:S(2)}) collective-permute-start(f32[1,768]{1,0:T(1,128)S(1)} %get-tuple-element.56.mine_ref), channel_id=1, source_target_pairs={{255,0},{2,1},{1,2},{4,3},{3,4},{6,5},{5,6},{8,7},{7,8},{10,9},{9,... | collective-permute-start | bytes 9224 | tf_op jit(solution)/shard_map/ppermute | solution.py:420
  55.8 0.0 collective-permute-start.11
  55.8 3.0 %collective-permute-start.14 = (f32[1,768]{1,0:T(1,128)S(1)}, f32[1,768]{1,0:T(1,128)S(1)}, u32[]{:S(2)}, u32[]{:S(2)}) collective-permute-start(f32[1,768]{1,0:T(1,128)S(1)} %get-tuple-element.56.mine_ref), channel_id=1, source_target_pairs={{192,0},{193,1},{194,2},{195,3},{196,4},{197,5},{198,6},{199,7},{2... | collective-permute-start | bytes 9224 | tf_op jit(solution)/shard_map/ppermute | solution.py:420
  58.8 0.0 collective-permute-start.13
  58.8 0.0 collective-permute-done.12.odd_ref
  58.8 0.0 collective-permute-done.11.even_ref
  58.8 4.1 %collective-permute-start.16 = (f32[3,768]{1,0:T(4,128)S(1)}, f32[3,768]{1,0:T(4,128)S(1)}, u32[]{:S(2)}, u32[]{:S(2)}) collective-permute-start(f32[3,768]{1,0:T(4,128)S(1)} %trio.1.refs_10_), channel_id=1, source_target_pairs={{16,0},{17,1},{18,2},{19,3},{20,4},{21,5},{22,6},{23,7},{24,8},{25... | collective-permute-start | bytes 27656 | tf_op jit(solution)/shard_map/ppermute | solution.py:420
  62.9 0.8 %collective-permute-start.15 = (f32[3,768]{1,0:T(4,128)S(1)}, f32[3,768]{1,0:T(4,128)S(1)}, u32[]{:S(2)}, u32[]{:S(2)}) collective-permute-start(f32[3,768]{1,0:T(4,128)S(1)} %trio.1.refs_10_), channel_id=1, source_target_pairs={{240,0},{241,1},{242,2},{243,3},{244,4},{245,5},{246,6},{247,7},{2... | collective-permute-start | bytes 27656 | tf_op jit(solution)/shard_map/ppermute | solution.py:420
  63.7 0.0 collective-permute-done.14.refs_12_
  63.7 0.0 collective-permute-done.13.refs_11_
  63.7 3.4 %gather_first.1.first_ref = f32[768,512]{1,0:T(8,128)S(1)} custom-call(f32[768,128]{1,0:T(8,128)S(1)} %get-tuple-element.49.sums_ref, bf16[768,512]{1,0:T(8,128)(2,1)S(1)} %get-tuple-element.50.matched_ref, bf16[768,768]{1,0:T(8,128)(2,1)S(1)} %get-tuple-element.51.refs_0_, bf16[768,768]{1,0:T(8,128)(2,1)S(1)} %get-tuple-element.52.refs_1_, ...), custom_call_target="tpu_custom_call" | custom-call | flops 3019898880 | bytes 12976128 | tf_op jit(solution)/shard_map/gather_first/pallas_call | solution.py:367
  67.1 0.0 collective-permute-done.16.refs_9_
  67.1 0.4 collective-permute-done.15.refs_8_
  67.5 3.4 %gather_final.1 = f32[768,512]{1,0:T(8,128)} custom-call(f32[768,128]{1,0:T(8,128)S(1)} %get-tuple-element.49.sums_ref, f32[768,512]{1,0:T(8,128)S(1)} %gather_first.1.first_ref, bf16[768,768]{1,0:T(8,128)(2,1)S(1)} %get-tuple-element.57.refs_0_, bf16[768,768]{1,0:T(8,128)(2,1)S(1)} %get-tuple-element.58.refs_1_, ...), custom_call_target="tpu_custom_call" | custom-call | flops 2415919104 | bytes 11010048 | tf_op jit(solution)/shard_map/gather_final/pallas_call | solution.py:380
  (2 shorter events, 0.0 us)
Async XLA Ops:
  0.0 11.8 %copy-start = (s32[768]{0:T(1024)S(1)}, s32[768]{0:T(1024)}, u32[]{:S(2)}) copy-start(s32[768]{0:T(1024)} %param.3) | copy-start | bytes 9220
  1.4 12.0 %collective-permute-start.1 = (bf16[768,512]{1,0:T(8,128)(2,1)S(1)}, bf16[768,512]{1,0:T(8,128)(2,1)S(1)}, u32[]{:S(2)}, u32[]{:S(2)}) collective-permute-start(bf16[768,512]{1,0:T(8,128)(2,1)S(1)} %normalize.1.mine_ref.refs_5_), channel_id=1, source_target_pairs={{16,0},{17,1},{18,2},{19,3},{20,4},{21,5},{22,6},{23,7},{24,8},{25... | collective-permute-start | bytes 2359304 | tf_op jit(solution)/shard_map/ppermute | solution.py:420
  4.7 21.7 %collective-permute-start = (bf16[768,512]{1,0:T(8,128)(2,1)S(1)}, bf16[768,512]{1,0:T(8,128)(2,1)S(1)}, u32[]{:S(2)}, u32[]{:S(2)}) collective-permute-start(bf16[768,512]{1,0:T(8,128)(2,1)S(1)} %normalize.1.mine_ref.refs_5_), channel_id=1, source_target_pairs={{7,0},{0,1},{1,2},{2,3},{3,4},{4,5},{5,6},{6,7},{15,8},{8,9},{9,10... | collective-permute-start | bytes 2359304 | tf_op jit(solution)/shard_map/ppermute | solution.py:420
  4.7 21.7 %collective-permute-start.2 = (bf16[768,512]{1,0:T(8,128)(2,1)S(1)}, bf16[768,512]{1,0:T(8,128)(2,1)S(1)}, u32[]{:S(2)}, u32[]{:S(2)}) collective-permute-start(bf16[768,512]{1,0:T(8,128)(2,1)S(1)} %normalize.1.mine_ref.refs_5_), channel_id=1, source_target_pairs={{1,0},{2,1},{3,2},{4,3},{5,4},{6,5},{7,6},{0,7},{9,8},{10,9},{11,1... | collective-permute-start | bytes 2359304 | tf_op jit(solution)/shard_map/ppermute | solution.py:420
  8.5 21.4 %collective-permute-start.6 = (bf16[768,512]{1,0:T(8,128)(2,1)S(1)}, bf16[768,512]{1,0:T(8,128)(2,1)S(1)}, u32[]{:S(2)}, u32[]{:S(2)}) collective-permute-start(bf16[768,512]{1,0:T(8,128)(2,1)S(1)} %normalize.1.mine_ref.refs_5_), channel_id=1, source_target_pairs={{240,0},{241,1},{242,2},{243,3},{244,4},{245,5},{246,6},{247,7},{2... | collective-permute-start | bytes 2359304 | tf_op jit(solution)/shard_map/ppermute | solution.py:420
  13.3 20.0 %collective-permute-start.5 = (bf16[768,512]{1,0:T(8,128)(2,1)S(1)}, bf16[768,512]{1,0:T(8,128)(2,1)S(1)}, u32[]{:S(2)}, u32[]{:S(2)}) collective-permute-start(bf16[768,512]{1,0:T(8,128)(2,1)S(1)} %normalize.1.mine_ref.refs_5_), channel_id=1, source_target_pairs={{192,0},{193,1},{194,2},{195,3},{196,4},{197,5},{198,6},{199,7},{2... | collective-permute-start | bytes 2359304 | tf_op jit(solution)/shard_map/ppermute | solution.py:420
  15.9 21.2 %collective-permute-start.4 = (bf16[768,512]{1,0:T(8,128)(2,1)S(1)}, bf16[768,512]{1,0:T(8,128)(2,1)S(1)}, u32[]{:S(2)}, u32[]{:S(2)}) collective-permute-start(bf16[768,512]{1,0:T(8,128)(2,1)S(1)} %normalize.1.mine_ref.refs_5_), channel_id=1, source_target_pairs={{64,0},{65,1},{66,2},{67,3},{68,4},{69,5},{70,6},{71,7},{72,8},{73... | collective-permute-start | bytes 2359304 | tf_op jit(solution)/shard_map/ppermute | solution.py:420
  26.4 20.7 %collective-permute-start.3 = (bf16[768,512]{1,0:T(8,128)(2,1)S(1)}, bf16[768,512]{1,0:T(8,128)(2,1)S(1)}, u32[]{:S(2)}, u32[]{:S(2)}) collective-permute-start(bf16[768,512]{1,0:T(8,128)(2,1)S(1)} %turn.1), channel_id=1, source_target_pairs={{248,255},{17,1},{18,2},{19,3},{20,4},{21,5},{22,6},{15,7},{0,8},{... | collective-permute-start | bytes 2359304 | tf_op jit(solution)/shard_map/ppermute | solution.py:420
  29.9 17.2 %collective-permute-start.7 = (bf16[768,512]{1,0:T(8,128)(2,1)S(1)}, bf16[768,512]{1,0:T(8,128)(2,1)S(1)}, u32[]{:S(2)}, u32[]{:S(2)}) collective-permute-start(bf16[768,512]{1,0:T(8,128)(2,1)S(1)} %collective-permute-done.6.far_ref.theirs_ref.refs_5_), channel_id=1, source_target_pairs={{15,0},{48,63},{79,64},{112,127},{143,128},{176,191},{207,192},{24... | collective-permute-start | bytes 2359304 | tf_op jit(solution)/shard_map/ppermute | solution.py:420
  30.7 18.7 %collective-permute-start.9 = (bf16[768,512]{1,0:T(8,128)(2,1)S(1)}, bf16[768,512]{1,0:T(8,128)(2,1)S(1)}, u32[]{:S(2)}, u32[]{:S(2)}) collective-permute-start(bf16[768,512]{1,0:T(8,128)(2,1)S(1)} %far17.1), channel_id=1, source_target_pairs={{47,63},{0,1},{1,2},{2,3},{3,4},{4,5},{5,6},{6,7},{231,8},{8,9},{9... | collective-permute-start | bytes 2359304 | tf_op jit(solution)/shard_map/ppermute | solution.py:420
  33.4 16.0 %collective-permute-start.10 = (bf16[768,512]{1,0:T(8,128)(2,1)S(1)}, bf16[768,512]{1,0:T(8,128)(2,1)S(1)}, u32[]{:S(2)}, u32[]{:S(2)}) collective-permute-start(bf16[768,512]{1,0:T(8,128)(2,1)S(1)} %collective-permute-done.5.theirs_ref.refs_8_), channel_id=1, source_target_pairs={{0,16},{1,17},{2,18},{3,19},{4,20},{5,21},{6,22},{7,23},{8,24},{9,... | collective-permute-start | bytes 2359304 | tf_op jit(solution)/shard_map/ppermute | solution.py:420
  47.4 2.9 %collective-permute-start.8 = (bf16[768,512]{1,0:T(8,128)(2,1)S(1)}, bf16[768,512]{1,0:T(8,128)(2,1)S(1)}, u32[]{:S(2)}, u32[]{:S(2)}) collective-permute-start(bf16[768,512]{1,0:T(8,128)(2,1)S(1)} %near17.1), channel_id=1, source_target_pairs={{16,0},{17,1},{18,2},{19,3},{20,4},{21,5},{22,6},{23,7},{24,8},{25... | collective-permute-start | bytes 2359304 | tf_op jit(solution)/shard_map/ppermute | solution.py:420
  51.2 7.6 %collective-permute-start.12 = (f32[1,768]{1,0:T(1,128)S(1)}, f32[1,768]{1,0:T(1,128)S(1)}, u32[]{:S(2)}, u32[]{:S(2)}) collective-permute-start(f32[1,768]{1,0:T(1,128)S(1)} %get-tuple-element.56.mine_ref), channel_id=1, source_target_pairs={{255,0},{2,1},{1,2},{4,3},{3,4},{6,5},{5,6},{8,7},{7,8},{10,9},{9,... | collective-permute-start | bytes 9224 | tf_op jit(solution)/shard_map/ppermute | solution.py:420
  55.8 3.0 %collective-permute-start.11 = (f32[1,768]{1,0:T(1,128)S(1)}, f32[1,768]{1,0:T(1,128)S(1)}, u32[]{:S(2)}, u32[]{:S(2)}) collective-permute-start(f32[1,768]{1,0:T(1,128)S(1)} %get-tuple-element.56.mine_ref), channel_id=1, source_target_pairs={{1,0},{0,1},{3,2},{2,3},{5,4},{4,5},{7,6},{6,7},{9,8},{8,9},{11,10... | collective-permute-start | bytes 9224 | tf_op jit(solution)/shard_map/ppermute | solution.py:420
  55.8 7.9 %collective-permute-start.14 = (f32[1,768]{1,0:T(1,128)S(1)}, f32[1,768]{1,0:T(1,128)S(1)}, u32[]{:S(2)}, u32[]{:S(2)}) collective-permute-start(f32[1,768]{1,0:T(1,128)S(1)} %get-tuple-element.56.mine_ref), channel_id=1, source_target_pairs={{192,0},{193,1},{194,2},{195,3},{196,4},{197,5},{198,6},{199,7},{2... | collective-permute-start | bytes 9224 | tf_op jit(solution)/shard_map/ppermute | solution.py:420
  58.8 4.9 %collective-permute-start.13 = (f32[1,768]{1,0:T(1,128)S(1)}, f32[1,768]{1,0:T(1,128)S(1)}, u32[]{:S(2)}, u32[]{:S(2)}) collective-permute-start(f32[1,768]{1,0:T(1,128)S(1)} %get-tuple-element.56.mine_ref), channel_id=1, source_target_pairs={{64,0},{65,1},{66,2},{67,3},{68,4},{69,5},{70,6},{71,7},{72,8},{73... | collective-permute-start | bytes 9224 | tf_op jit(solution)/shard_map/ppermute | solution.py:420
  58.8 8.3 %collective-permute-start.16 = (f32[3,768]{1,0:T(4,128)S(1)}, f32[3,768]{1,0:T(4,128)S(1)}, u32[]{:S(2)}, u32[]{:S(2)}) collective-permute-start(f32[3,768]{1,0:T(4,128)S(1)} %trio.1.refs_10_), channel_id=1, source_target_pairs={{16,0},{17,1},{18,2},{19,3},{20,4},{21,5},{22,6},{23,7},{24,8},{25... | collective-permute-start | bytes 27656 | tf_op jit(solution)/shard_map/ppermute | solution.py:420
  62.9 4.6 %collective-permute-start.15 = (f32[3,768]{1,0:T(4,128)S(1)}, f32[3,768]{1,0:T(4,128)S(1)}, u32[]{:S(2)}, u32[]{:S(2)}) collective-permute-start(f32[3,768]{1,0:T(4,128)S(1)} %trio.1.refs_10_), channel_id=1, source_target_pairs={{240,0},{241,1},{242,2},{243,3},{244,4},{245,5},{246,6},{247,7},{2... | collective-permute-start | bytes 27656 | tf_op jit(solution)/shard_map/ppermute | solution.py:420

commit v8 on v7

--- a/solution.py
+++ b/solution.py
@@ -290,16 +290,22 @@
             out_ref[...] = ref[...]
 
 
-def near17_kernel(below_ref, above_ref, out_ref):
+def near17_kernel(below_ref, above_ref, turn_ref, row_ref, out_ref):
+    line, col = lax.axis_size("col") // 2, lax.axis_index("col")
     core0 = lax.axis_index("row") % 2 == 0
-
-    @pl.when(core0)
-    def _():
-        out_ref[...] = below_ref[...]
-
-    @pl.when(~core0)
-    def _():
-        out_ref[...] = above_ref[...]
+    turns = jnp.where(core0, col, col + 1) % line == 0
+    corner = at_corner()
+    choices = [
+        (~turns & core0, below_ref),
+        (~turns & ~core0, above_ref),
+        (turns & ~corner, turn_ref),
+        (corner, row_ref),
+    ]
+    for chosen, ref in choices:
+
+        @pl.when(chosen)
+        def _():
+            out_ref[...] = ref[...]
 
 
 def choose(kernel, name, *choices, aliases={}):
@@ -445,9 +451,11 @@
 
     sums = add(sums, near=near, far=far, x_first=x_first, x_second=x_second)
     turn, sums = lax.optimization_barrier((turn, sums))
+    near17 = send(
+        choose(near17_kernel, "near17", ring_below, ring_above, turn, across), "near"
+    )
     above = choose(functools.partial(merge_kernel, 1, 1), "above", ring_above, turn, across)
     below = choose(functools.partial(merge_kernel, 0, 0), "below", ring_below, turn, across)
-    near17 = send(choose(near17_kernel, "near17", below, above), "near")
     sums = add(sums, above=above, below=below)
     sums = add(sums, far17=choose(corner_kernel, "corner", far17, corner, aliases={0: 0}))
     blocks["near17"] = near17

time: 71.2 us -> 71.3 us (level)
  no operation moved by 1% of the time
where the time goes in v8:
time: 71.3 us; the launch traced here: 71.1 us
  starting transfers between devices  31.5 us (44%)
  waiting for transfers between devices  22.1 us (31%)
  Pallas kernels  17.2 us (24%)
    ppermute x17, starting transfers between devices, send(): return lax.ppermute(block, both, route[name])  31.5 us
    ppermute x17, waiting for transfers between devices, send(): return lax.ppermute(block, both, route[name])  22.1 us
    pallas_call x7, Pallas kernels, pair_tile(): call(tile_kernel, 'pair_tile', [held] * 3, [held] * 2, [pltpu.VMEM((rows,...  6 us
    pallas_call x1, Pallas kernels, gather_final(): call(functools.partial(final_kernel, count), 'gather_final', [held] * (2...  3.46 us
    pallas_call x1, Pallas kernels, gather_first(): call(functools.partial(first_kernel, count), 'gather_first', [held] * (2...  3.37 us
    pallas_call x1, Pallas kernels, self_tile(): call(self_kernel, 'self_tile', [held, small], [held] * 3, [pltpu.VMEM((ro...  1.53 us
  transfers between devices with their start and end apart: 17, of which 4 were waited for; matrix products, arithmetic and copies ran while one was open for 0% of the time, Pallas kernels for 16%

profile of v8, /device:TPU:1, one launch (start us, length us, event | category | flops | bytes accessed | tf_op | source)
XLA Modules:
  0.0 71.1 jit_solution(8261269373198079849)
XLA Ops:
  0.0 0.0 copy-start
  0.0 1.3 %normalize.1.mine_ref.refs_5_ = bf16[768,512]{1,0:T(8,128)(2,1)S(1)} custom-call(bf16[768,512]{1,0:T(8,128)(2,1)} %rows_ref.1), custom_call_target="tpu_custom_call" | custom-call | flops 1572864 | bytes 1572864 | tf_op jit(solution)/shard_map/normalize/pallas_call | solution.py:134
  1.4 3.3 %collective-permute-start.1 = (bf16[768,512]{1,0:T(8,128)(2,1)S(1)}, bf16[768,512]{1,0:T(8,128)(2,1)S(1)}, u32[]{:S(2)}, u32[]{:S(2)}) collective-permute-start(bf16[768,512]{1,0:T(8,128)(2,1)S(1)} %normalize.1.mine_ref.refs_5_), channel_id=1, source_target_pairs={{16,0},{17,1},{18,2},{19,3},{20,4},{21,5},{22,6},{23,7},{24,8},{25... | collective-permute-start | bytes 2359304 | tf_op jit(solution)/shard_map/ppermute | solution.py:426
  4.7 0.0 collective-permute-start
  4.7 3.8 %collective-permute-start.2 = (bf16[768,512]{1,0:T(8,128)(2,1)S(1)}, bf16[768,512]{1,0:T(8,128)(2,1)S(1)}, u32[]{:S(2)}, u32[]{:S(2)}) collective-permute-start(bf16[768,512]{1,0:T(8,128)(2,1)S(1)} %normalize.1.mine_ref.refs_5_), channel_id=1, source_target_pairs={{1,0},{2,1},{3,2},{4,3},{5,4},{6,5},{7,6},{0,7},{9,8},{10,9},{11,1... | collective-permute-start | bytes 2359304 | tf_op jit(solution)/shard_map/ppermute | solution.py:426
  8.5 3.3 %collective-permute-start.6 = (bf16[768,512]{1,0:T(8,128)(2,1)S(1)}, bf16[768,512]{1,0:T(8,128)(2,1)S(1)}, u32[]{:S(2)}, u32[]{:S(2)}) collective-permute-start(bf16[768,512]{1,0:T(8,128)(2,1)S(1)} %normalize.1.mine_ref.refs_5_), channel_id=1, source_target_pairs={{240,0},{241,1},{242,2},{243,3},{244,4},{245,5},{246,6},{247,7},{2... | collective-permute-start | bytes 2359304 | tf_op jit(solution)/shard_map/ppermute | solution.py:426
  11.8 0.0 copy-done
  11.8 1.5 %self_tile.1 = (bf16[768,768]{1,0:T(8,128)(2,1)S(1)}, f32[768,128]{1,0:T(8,128)S(1)}, bf16[768,512]{1,0:T(8,128)(2,1)S(1)}) custom-call(bf16[768,512]{1,0:T(8,128)(2,1)S(1)} %normalize.1.mine_ref.refs_5_, s32[6,128]{1,0:T(8,128)S(1)} %bitcast.1), custom_call_target="tpu_custom_call" | custom-call | flops 1207959552 | bytes 2752512 | tf_op jit(solution)/shard_map/self_tile/pallas_call | solution.py:180
  13.3 0.0 collective-permute-done.1.near_ref.theirs_ref.refs_4_
  13.3 2.6 %collective-permute-start.5 = (bf16[768,512]{1,0:T(8,128)(2,1)S(1)}, bf16[768,512]{1,0:T(8,128)(2,1)S(1)}, u32[]{:S(2)}, u32[]{:S(2)}) collective-permute-start(bf16[768,512]{1,0:T(8,128)(2,1)S(1)} %normalize.1.mine_ref.refs_5_), channel_id=1, source_target_pairs={{192,0},{193,1},{194,2},{195,3},{196,4},{197,5},{198,6},{199,7},{2... | collective-permute-start | bytes 2359304 | tf_op jit(solution)/shard_map/ppermute | solution.py:426
  15.9 0.0 collective-permute-start.4
  15.9 10.5 %collective-permute-done.below_ref.ring_ref = bf16[768,512]{1,0:T(8,128)(2,1)S(1)} collective-permute-done((bf16[768,512]{1,0:T(8,128)(2,1)S(1)}, bf16[768,512]{1,0:T(8,128)(2,1)S(1)}, u32[]{:S(2)}, u32[]{:S(2)}) %collective-permute-start) | collective-permute-done | bytes 786464 | tf_op jit(solution)/shard_map/ppermute | solution.py:426
  26.3 0.0 collective-permute-done.2.above_ref.ring_ref
  26.3 0.1 turn.1
  26.4 1.4 %collective-permute-start.3 = (bf16[768,512]{1,0:T(8,128)(2,1)S(1)}, bf16[768,512]{1,0:T(8,128)(2,1)S(1)}, u32[]{:S(2)}, u32[]{:S(2)}) collective-permute-start(bf16[768,512]{1,0:T(8,128)(2,1)S(1)} %turn.1), channel_id=1, source_target_pairs={{248,255},{17,1},{18,2},{19,3},{20,4},{21,5},{22,6},{15,7},{0,8},{... | collective-permute-start | bytes 2359304 | tf_op jit(solution)/shard_map/ppermute | solution.py:426
  27.8 2.1 %collective-permute-done.6.far_ref.theirs_ref.refs_5_ = bf16[768,512]{1,0:T(8,128)(2,1)S(1)} collective-permute-done((bf16[768,512]{1,0:T(8,128)(2,1)S(1)}, bf16[768,512]{1,0:T(8,128)(2,1)S(1)}, u32[]{:S(2)}, u32[]{:S(2)}) %collective-permute-start.6) | collective-permute-done | bytes 786464 | tf_op jit(solution)/shard_map/ppermute | solution.py:426
  29.9 0.1 far17.1
  29.9 0.7 collective-permute-start.7
  30.7 1.0 %collective-permute-start.9 = (bf16[768,512]{1,0:T(8,128)(2,1)S(1)}, bf16[768,512]{1,0:T(8,128)(2,1)S(1)}, u32[]{:S(2)}, u32[]{:S(2)}) collective-permute-start(bf16[768,512]{1,0:T(8,128)(2,1)S(1)} %far17.1), channel_id=1, source_target_pairs={{47,63},{0,1},{1,2},{2,3},{3,4},{4,5},{5,6},{6,7},{231,8},{8,9},{9... | collective-permute-start | bytes 2359304 | tf_op jit(solution)/shard_map/ppermute | solution.py:426
  31.7 0.8 %pair_tile.7 = (bf16[768,768]{1,0:T(8,128)(2,1)S(1)}, f32[768,128]{1,0:T(8,128)S(1)}) custom-call(bf16[768,512]{1,0:T(8,128)(2,1)S(1)} %normalize.1.mine_ref.refs_5_, bf16[768,512]{1,0:T(8,128)(2,1)S(1)} %collective-permute-done.1.near_ref.theirs_ref.refs_4_, f32[768,128]{1,0:T(8,128)S(1)} %get-tuple-element.39.before_ref), custom_call_target="tpu_custom_call" | custom-call | flops 603979776 | bytes 2752512 | tf_op jit(solution)/shard_map/pair_tile/pallas_call | solution.py:205
  32.5 0.8 %pair_tile.8 = (bf16[768,768]{1,0:T(8,128)(2,1)S(1)}, f32[768,128]{1,0:T(8,128)S(1)}) custom-call(bf16[768,512]{1,0:T(8,128)(2,1)S(1)} %normalize.1.mine_ref.refs_5_, bf16[768,512]{1,0:T(8,128)(2,1)S(1)} %collective-permute-done.6.far_ref.theirs_ref.refs_5_, f32[768,128]{1,0:T(8,128)S(1)} %get-tuple-element.40.before_ref), custom_call_target="tpu_custom_call" | custom-call | flops 603979776 | bytes 2752512 | tf_op jit(solution)/shard_map/pair_tile/pallas_call | solution.py:205
  33.4 0.0 collective-permute-done.5.theirs_ref.refs_8_
  33.4 2.9 %collective-permute-start.10 = (bf16[768,512]{1,0:T(8,128)(2,1)S(1)}, bf16[768,512]{1,0:T(8,128)(2,1)S(1)}, u32[]{:S(2)}, u32[]{:S(2)}) collective-permute-start(bf16[768,512]{1,0:T(8,128)(2,1)S(1)} %collective-permute-done.5.theirs_ref.refs_8_), channel_id=1, source_target_pairs={{0,16},{1,17},{2,18},{3,19},{4,20},{5,21},{6,22},{7,23},{8,24},{9,... | collective-permute-start | bytes 2359304 | tf_op jit(solution)/shard_map/ppermute | solution.py:426
  36.3 0.9 %pair_tile.9 = (bf16[768,768]{1,0:T(8,128)(2,1)S(1)}, f32[768,128]{1,0:T(8,128)S(1)}) custom-call(bf16[768,512]{1,0:T(8,128)(2,1)S(1)} %normalize.1.mine_ref.refs_5_, bf16[768,512]{1,0:T(8,128)(2,1)S(1)} %collective-permute-done.5.theirs_ref.refs_8_, f32[768,128]{1,0:T(8,128)S(1)} %get-tuple-element.41.before_ref), custom_call_target="tpu_custom_call" | custom-call | flops 603979776 | bytes 2752512 | tf_op jit(solution)/shard_map/pair_tile/pallas_call | solution.py:205
  37.2 0.0 collective-permute-done.4.theirs_ref.refs_9_
  37.2 0.8 %pair_tile.10 = (bf16[768,768]{1,0:T(8,128)(2,1)S(1)}, f32[768,128]{1,0:T(8,128)S(1)}) custom-call(bf16[768,512]{1,0:T(8,128)(2,1)S(1)} %normalize.1.mine_ref.refs_5_, bf16[768,512]{1,0:T(8,128)(2,1)S(1)} %collective-permute-done.4.theirs_ref.refs_9_, f32[768,128]{1,0:T(8,128)S(1)} %get-tuple-element.42.before_ref), custom_call_target="tpu_custom_call" | custom-call | flops 603979776 | bytes 2752512 | tf_op jit(solution)/shard_map/pair_tile/pallas_call | solution.py:205
  38.0 9.1 %collective-permute-done.3.turn_ref = bf16[768,512]{1,0:T(8,128)(2,1)S(1)} collective-permute-done((bf16[768,512]{1,0:T(8,128)(2,1)S(1)}, bf16[768,512]{1,0:T(8,128)(2,1)S(1)}, u32[]{:S(2)}, u32[]{:S(2)}) %collective-permute-start.3) | collective-permute-done | bytes 786464 | tf_op jit(solution)/shard_map/ppermute | solution.py:426
  47.1 0.0 collective-permute-done.7.row_ref
  47.1 0.1 near17.1
  47.2 0.1 collective-permute-start.8
  47.3 0.1 above.1.theirs_ref.refs_6_
  47.4 0.3 below.1.theirs_ref.refs_7_
  47.7 0.8 %pair_tile.11 = (bf16[768,768]{1,0:T(8,128)(2,1)S(1)}, f32[768,128]{1,0:T(8,128)S(1)}) custom-call(bf16[768,512]{1,0:T(8,128)(2,1)S(1)} %normalize.1.mine_ref.refs_5_, bf16[768,512]{1,0:T(8,128)(2,1)S(1)} %above.1.theirs_ref.refs_6_, f32[768,128]{1,0:T(8,128)S(1)} %get-tuple-element.45.before_ref), custom_call_target="tpu_custom_call" | custom-call | flops 603979776 | bytes 2752512 | tf_op jit(solution)/shard_map/pair_tile/pallas_call | solution.py:205
  48.5 0.9 %pair_tile.12 = (bf16[768,768]{1,0:T(8,128)(2,1)S(1)}, f32[768,128]{1,0:T(8,128)S(1)}) custom-call(bf16[768,512]{1,0:T(8,128)(2,1)S(1)} %normalize.1.mine_ref.refs_5_, bf16[768,512]{1,0:T(8,128)(2,1)S(1)} %below.1.theirs_ref.refs_7_, f32[768,128]{1,0:T(8,128)S(1)} %get-tuple-element.46.before_ref), custom_call_target="tpu_custom_call" | custom-call | flops 603979776 | bytes 2752512 | tf_op jit(solution)/shard_map/pair_tile/pallas_call | solution.py:205
  49.4 0.0 collective-permute-done.9.far17_ref
  49.4 0.0 collective-permute-done.10.corner_ref
  49.4 0.9 %pair_tile.13 = (bf16[768,768]{1,0:T(8,128)(2,1)S(1)}, f32[768,128]{1,0:T(8,128)S(1)}) custom-call(bf16[768,512]{1,0:T(8,128)(2,1)S(1)} %normalize.1.mine_ref.refs_5_, bf16[768,512]{1,0:T(8,128)(2,1)S(1)} %corner.1.theirs_ref.refs_7_, f32[768,128]{1,0:T(8,128)S(1)} %get-tuple-element.47.before_ref), custom_call_target="tpu_custom_call" | custom-call | flops 603979776 | bytes 2752512 | tf_op jit(solution)/shard_map/pair_tile/pallas_call | solution.py:205
  50.3 0.0 collective-permute-done.8.theirs_ref.refs_6_
  50.3 1.0 %last_tile.1 = (bf16[768,768]{1,0:T(8,128)(2,1)S(1)}, f32[768,128]{1,0:T(8,128)S(1)}, f32[1,768]{1,0:T(1,128)S(1)}) custom-call(bf16[768,512]{1,0:T(8,128)(2,1)S(1)} %normalize.1.mine_ref.refs_5_, bf16[768,512]{1,0:T(8,128)(2,1)S(1)} %collective-permute-done.8.theirs_ref.refs_6_, f32[768,128]{1,0:T(8,128)S(1)} %get-tuple-element.48.before_ref), custom_call_target="tpu_custom_call" | custom-call | flops 603979776 | bytes 2752512 | tf_op jit(solution)/shard_map/last_tile/pallas_call | solution.py:228
  51.3 4.5 %collective-permute-start.12 = (f32[1,768]{1,0:T(1,128)S(1)}, f32[1,768]{1,0:T(1,128)S(1)}, u32[]{:S(2)}, u32[]{:S(2)}) collective-permute-start(f32[1,768]{1,0:T(1,128)S(1)} %get-tuple-element.56.mine_ref), channel_id=1, source_target_pairs={{255,0},{2,1},{1,2},{4,3},{3,4},{6,5},{5,6},{8,7},{7,8},{10,9},{9,... | collective-permute-start | bytes 9224 | tf_op jit(solution)/shard_map/ppermute | solution.py:426
  55.8 0.0 collective-permute-start.11
  55.8 3.0 %collective-permute-start.14 = (f32[1,768]{1,0:T(1,128)S(1)}, f32[1,768]{1,0:T(1,128)S(1)}, u32[]{:S(2)}, u32[]{:S(2)}) collective-permute-start(f32[1,768]{1,0:T(1,128)S(1)} %get-tuple-element.56.mine_ref), channel_id=1, source_target_pairs={{192,0},{193,1},{194,2},{195,3},{196,4},{197,5},{198,6},{199,7},{2... | collective-permute-start | bytes 9224 | tf_op jit(solution)/shard_map/ppermute | solution.py:426
  58.8 0.0 collective-permute-start.13
  58.8 0.0 collective-permute-done.12.odd_ref
  58.8 0.0 collective-permute-done.11.even_ref
  58.9 4.0 %collective-permute-start.16 = (f32[3,768]{1,0:T(4,128)S(1)}, f32[3,768]{1,0:T(4,128)S(1)}, u32[]{:S(2)}, u32[]{:S(2)}) collective-permute-start(f32[3,768]{1,0:T(4,128)S(1)} %trio.1.refs_10_), channel_id=1, source_target_pairs={{16,0},{17,1},{18,2},{19,3},{20,4},{21,5},{22,6},{23,7},{24,8},{25... | collective-permute-start | bytes 27656 | tf_op jit(solution)/shard_map/ppermute | solution.py:426
  62.9 0.8 %collective-permute-start.15 = (f32[3,768]{1,0:T(4,128)S(1)}, f32[3,768]{1,0:T(4,128)S(1)}, u32[]{:S(2)}, u32[]{:S(2)}) collective-permute-start(f32[3,768]{1,0:T(4,128)S(1)} %trio.1.refs_10_), channel_id=1, source_target_pairs={{240,0},{241,1},{242,2},{243,3},{244,4},{245,5},{246,6},{247,7},{2... | collective-permute-start | bytes 27656 | tf_op jit(solution)/shard_map/ppermute | solution.py:426
  63.7 0.0 collective-permute-done.14.refs_12_
  63.7 0.0 collective-permute-done.13.refs_11_
  63.7 3.4 %gather_first.1.first_ref = f32[768,512]{1,0:T(8,128)S(1)} custom-call(f32[768,128]{1,0:T(8,128)S(1)} %get-tuple-element.49.sums_ref, bf16[768,512]{1,0:T(8,128)(2,1)S(1)} %get-tuple-element.50.matched_ref, bf16[768,768]{1,0:T(8,128)(2,1)S(1)} %get-tuple-element.51.refs_0_, bf16[768,768]{1,0:T(8,128)(2,1)S(1)} %get-tuple-element.52.refs_1_, ...), custom_call_target="tpu_custom_call" | custom-call | flops 3019898880 | bytes 12976128 | tf_op jit(solution)/shard_map/gather_first/pallas_call | solution.py:373
  67.1 0.0 collective-permute-done.16.refs_9_
  67.1 0.4 collective-permute-done.15.refs_8_
  67.5 3.5 %gather_final.1 = f32[768,512]{1,0:T(8,128)} custom-call(f32[768,128]{1,0:T(8,128)S(1)} %get-tuple-element.49.sums_ref, f32[768,512]{1,0:T(8,128)S(1)} %gather_first.1.first_ref, bf16[768,768]{1,0:T(8,128)(2,1)S(1)} %get-tuple-element.57.refs_0_, bf16[768,768]{1,0:T(8,128)(2,1)S(1)} %get-tuple-element.58.refs_1_, ...), custom_call_target="tpu_custom_call" | custom-call | flops 2415919104 | bytes 11010048 | tf_op jit(solution)/shard_map/gather_final/pallas_call | solution.py:386
  (2 shorter events, 0.0 us)
Async XLA Ops:
  0.0 11.8 %copy-start = (s32[768]{0:T(1024)S(1)}, s32[768]{0:T(1024)}, u32[]{:S(2)}) copy-start(s32[768]{0:T(1024)} %param.3) | copy-start | bytes 9220
  1.4 12.0 %collective-permute-start.1 = (bf16[768,512]{1,0:T(8,128)(2,1)S(1)}, bf16[768,512]{1,0:T(8,128)(2,1)S(1)}, u32[]{:S(2)}, u32[]{:S(2)}) collective-permute-start(bf16[768,512]{1,0:T(8,128)(2,1)S(1)} %normalize.1.mine_ref.refs_5_), channel_id=1, source_target_pairs={{16,0},{17,1},{18,2},{19,3},{20,4},{21,5},{22,6},{23,7},{24,8},{25... | collective-permute-start | bytes 2359304 | tf_op jit(solution)/shard_map/ppermute | solution.py:426
  4.7 21.7 %collective-permute-start = (bf16[768,512]{1,0:T(8,128)(2,1)S(1)}, bf16[768,512]{1,0:T(8,128)(2,1)S(1)}, u32[]{:S(2)}, u32[]{:S(2)}) collective-permute-start(bf16[768,512]{1,0:T(8,128)(2,1)S(1)} %normalize.1.mine_ref.refs_5_), channel_id=1, source_target_pairs={{7,0},{0,1},{1,2},{2,3},{3,4},{4,5},{5,6},{6,7},{15,8},{8,9},{9,10... | collective-permute-start | bytes 2359304 | tf_op jit(solution)/shard_map/ppermute | solution.py:426
  4.7 21.7 %collective-permute-start.2 = (bf16[768,512]{1,0:T(8,128)(2,1)S(1)}, bf16[768,512]{1,0:T(8,128)(2,1)S(1)}, u32[]{:S(2)}, u32[]{:S(2)}) collective-permute-start(bf16[768,512]{1,0:T(8,128)(2,1)S(1)} %normalize.1.mine_ref.refs_5_), channel_id=1, source_target_pairs={{1,0},{2,1},{3,2},{4,3},{5,4},{6,5},{7,6},{0,7},{9,8},{10,9},{11,1... | collective-permute-start | bytes 2359304 | tf_op jit(solution)/shard_map/ppermute | solution.py:426
  8.5 21.4 %collective-permute-start.6 = (bf16[768,512]{1,0:T(8,128)(2,1)S(1)}, bf16[768,512]{1,0:T(8,128)(2,1)S(1)}, u32[]{:S(2)}, u32[]{:S(2)}) collective-permute-start(bf16[768,512]{1,0:T(8,128)(2,1)S(1)} %normalize.1.mine_ref.refs_5_), channel_id=1, source_target_pairs={{240,0},{241,1},{242,2},{243,3},{244,4},{245,5},{246,6},{247,7},{2... | collective-permute-start | bytes 2359304 | tf_op jit(solution)/shard_map/ppermute | solution.py:426
  13.3 20.0 %collective-permute-start.5 = (bf16[768,512]{1,0:T(8,128)(2,1)S(1)}, bf16[768,512]{1,0:T(8,128)(2,1)S(1)}, u32[]{:S(2)}, u32[]{:S(2)}) collective-permute-start(bf16[768,512]{1,0:T(8,128)(2,1)S(1)} %normalize.1.mine_ref.refs_5_), channel_id=1, source_target_pairs={{192,0},{193,1},{194,2},{195,3},{196,4},{197,5},{198,6},{199,7},{2... | collective-permute-start | bytes 2359304 | tf_op jit(solution)/shard_map/ppermute | solution.py:426
  15.9 21.3 %collective-permute-start.4 = (bf16[768,512]{1,0:T(8,128)(2,1)S(1)}, bf16[768,512]{1,0:T(8,128)(2,1)S(1)}, u32[]{:S(2)}, u32[]{:S(2)}) collective-permute-start(bf16[768,512]{1,0:T(8,128)(2,1)S(1)} %normalize.1.mine_ref.refs_5_), channel_id=1, source_target_pairs={{64,0},{65,1},{66,2},{67,3},{68,4},{69,5},{70,6},{71,7},{72,8},{73... | collective-permute-start | bytes 2359304 | tf_op jit(solution)/shard_map/ppermute | solution.py:426
  26.4 20.7 %collective-permute-start.3 = (bf16[768,512]{1,0:T(8,128)(2,1)S(1)}, bf16[768,512]{1,0:T(8,128)(2,1)S(1)}, u32[]{:S(2)}, u32[]{:S(2)}) collective-permute-start(bf16[768,512]{1,0:T(8,128)(2,1)S(1)} %turn.1), channel_id=1, source_target_pairs={{248,255},{17,1},{18,2},{19,3},{20,4},{21,5},{22,6},{15,7},{0,8},{... | collective-permute-start | bytes 2359304 | tf_op jit(solution)/shard_map/ppermute | solution.py:426
  29.9 17.2 %collective-permute-start.7 = (bf16[768,512]{1,0:T(8,128)(2,1)S(1)}, bf16[768,512]{1,0:T(8,128)(2,1)S(1)}, u32[]{:S(2)}, u32[]{:S(2)}) collective-permute-start(bf16[768,512]{1,0:T(8,128)(2,1)S(1)} %collective-permute-done.6.far_ref.theirs_ref.refs_5_), channel_id=1, source_target_pairs={{15,0},{48,63},{79,64},{112,127},{143,128},{176,191},{207,192},{24... | collective-permute-start | bytes 2359304 | tf_op jit(solution)/shard_map/ppermute | solution.py:426
  30.7 18.7 %collective-permute-start.9 = (bf16[768,512]{1,0:T(8,128)(2,1)S(1)}, bf16[768,512]{1,0:T(8,128)(2,1)S(1)}, u32[]{:S(2)}, u32[]{:S(2)}) collective-permute-start(bf16[768,512]{1,0:T(8,128)(2,1)S(1)} %far17.1), channel_id=1, source_target_pairs={{47,63},{0,1},{1,2},{2,3},{3,4},{4,5},{5,6},{6,7},{231,8},{8,9},{9... | collective-permute-start | bytes 2359304 | tf_op jit(solution)/shard_map/ppermute | solution.py:426
  33.4 16.0 %collective-permute-start.10 = (bf16[768,512]{1,0:T(8,128)(2,1)S(1)}, bf16[768,512]{1,0:T(8,128)(2,1)S(1)}, u32[]{:S(2)}, u32[]{:S(2)}) collective-permute-start(bf16[768,512]{1,0:T(8,128)(2,1)S(1)} %collective-permute-done.5.theirs_ref.refs_8_), channel_id=1, source_target_pairs={{0,16},{1,17},{2,18},{3,19},{4,20},{5,21},{6,22},{7,23},{8,24},{9,... | collective-permute-start | bytes 2359304 | tf_op jit(solution)/shard_map/ppermute | solution.py:426
  47.2 3.1 %collective-permute-start.8 = (bf16[768,512]{1,0:T(8,128)(2,1)S(1)}, bf16[768,512]{1,0:T(8,128)(2,1)S(1)}, u32[]{:S(2)}, u32[]{:S(2)}) collective-permute-start(bf16[768,512]{1,0:T(8,128)(2,1)S(1)} %near17.1), channel_id=1, source_target_pairs={{16,0},{17,1},{18,2},{19,3},{20,4},{21,5},{22,6},{23,7},{24,8},{25... | collective-permute-start | bytes 2359304 | tf_op jit(solution)/shard_map/ppermute | solution.py:426
  51.3 7.5 %collective-permute-start.12 = (f32[1,768]{1,0:T(1,128)S(1)}, f32[1,768]{1,0:T(1,128)S(1)}, u32[]{:S(2)}, u32[]{:S(2)}) collective-permute-start(f32[1,768]{1,0:T(1,128)S(1)} %get-tuple-element.56.mine_ref), channel_id=1, source_target_pairs={{255,0},{2,1},{1,2},{4,3},{3,4},{6,5},{5,6},{8,7},{7,8},{10,9},{9,... | collective-permute-start | bytes 9224 | tf_op jit(solution)/shard_map/ppermute | solution.py:426
  55.8 3.0 %collective-permute-start.11 = (f32[1,768]{1,0:T(1,128)S(1)}, f32[1,768]{1,0:T(1,128)S(1)}, u32[]{:S(2)}, u32[]{:S(2)}) collective-permute-start(f32[1,768]{1,0:T(1,128)S(1)} %get-tuple-element.56.mine_ref), channel_id=1, source_target_pairs={{1,0},{0,1},{3,2},{2,3},{5,4},{4,5},{7,6},{6,7},{9,8},{8,9},{11,10... | collective-permute-start | bytes 9224 | tf_op jit(solution)/shard_map/ppermute | solution.py:426
  55.8 7.9 %collective-permute-start.14 = (f32[1,768]{1,0:T(1,128)S(1)}, f32[1,768]{1,0:T(1,128)S(1)}, u32[]{:S(2)}, u32[]{:S(2)}) collective-permute-start(f32[1,768]{1,0:T(1,128)S(1)} %get-tuple-element.56.mine_ref), channel_id=1, source_target_pairs={{192,0},{193,1},{194,2},{195,3},{196,4},{197,5},{198,6},{199,7},{2... | collective-permute-start | bytes 9224 | tf_op jit(solution)/shard_map/ppermute | solution.py:426
  58.8 4.9 %collective-permute-start.13 = (f32[1,768]{1,0:T(1,128)S(1)}, f32[1,768]{1,0:T(1,128)S(1)}, u32[]{:S(2)}, u32[]{:S(2)}) collective-permute-start(f32[1,768]{1,0:T(1,128)S(1)} %get-tuple-element.56.mine_ref), channel_id=1, source_target_pairs={{64,0},{65,1},{66,2},{67,3},{68,4},{69,5},{70,6},{71,7},{72,8},{73... | collective-permute-start | bytes 9224 | tf_op jit(solution)/shard_map/ppermute | solution.py:426
  58.9 8.3 %collective-permute-start.16 = (f32[3,768]{1,0:T(4,128)S(1)}, f32[3,768]{1,0:T(4,128)S(1)}, u32[]{:S(2)}, u32[]{:S(2)}) collective-permute-start(f32[3,768]{1,0:T(4,128)S(1)} %trio.1.refs_10_), channel_id=1, source_target_pairs={{16,0},{17,1},{18,2},{19,3},{20,4},{21,5},{22,6},{23,7},{24,8},{25... | collective-permute-start | bytes 27656 | tf_op jit(solution)/shard_map/ppermute | solution.py:426
  62.9 4.6 %collective-permute-start.15 = (f32[3,768]{1,0:T(4,128)S(1)}, f32[3,768]{1,0:T(4,128)S(1)}, u32[]{:S(2)}, u32[]{:S(2)}) collective-permute-start(f32[3,768]{1,0:T(4,128)S(1)} %trio.1.refs_10_), channel_id=1, source_target_pairs={{240,0},{241,1},{242,2},{243,3},{244,4},{245,5},{246,6},{247,7},{2... | collective-permute-start | bytes 27656 | tf_op jit(solution)/shard_map/ppermute | solution.py:426
